TPU v7x, 512 devices: a whole 4x8x8 slice. The times are simulated.
512 devices in a mesh: tm: 32 (over z_hi, y), space: 4 (over z_lo, core), heads: 4 (over x).
Axes of the slice: x: 4, y: 8, z: 8 (z_hi: 4, z_lo: 2; z = z_hi * 2 + z_lo), core: 2. Of those that a mesh axis runs over, the one named last changes fastest.
Arguments:
- query_tiles: bfloat16 [32, 4, 384, 1536], P('tm', 'space', None, 'heads'), may hold values from -6 to 6
- key_tiles: bfloat16 [32, 4, 384, 1536], P('tm', 'space', None, 'heads'), may hold values from -6 to 6
- value_tiles: bfloat16 [32, 4, 384, 1536], P('tm', 'space', None, 'heads'), may hold values from -6 to 6
- grad_output: bfloat16 [32, 4, 384, 1536], P('tm', 'space', None, 'heads'), may hold values from -6 to 6
- log_norm: float32 [32, 4, 12, 384], P('tm', 'space', 'heads'), may hold values from 5 to 6.5
- row_delta: float32 [32, 4, 12, 384], P('tm', 'space', 'heads'), may hold values from -24 to 24
- extents: int32 [32, 4, 3], replicated, may hold values from 0 to 1, as said below
Outputs:
- grad_query: bfloat16 [32, 4, 384, 1536], P('tm', 'space', None, 'heads')
- grad_key: bfloat16 [32, 4, 384, 1536], P('tm', 'space', None, 'heads')
- grad_value: bfloat16 [32, 4, 384, 1536], P('tm', 'space', None, 'heads')
Inputs may be any that keep to these rules, and one draw needn't show every extreme that they name: `extents`: in every time tile at least one frame tile has time half-extent 1.
All inputs are finite; a program needn't handle non-finite values.
Results may differ from a plain program's by a relative error of at most 0.0057.
Values may be sent and summed in bfloat16 or wider, within the bound.
No kernel may reach another device: no remote copies, remote signals or barrier semaphores. Data moves between devices by JAX's collectives and lax.ppermute only.
A program may use at most 128 MiB of HBM per device.

v0:
```python
import jax
import jax.numpy as jnp
import numpy as np
from jax import lax
from jax.sharding import PartitionSpec as P

WIDTH_TILES = 2


def with_halo(shard, sides, width):
    for axis, dim in sides:
        size, length = (lax.axis_size(axis), shard.shape[dim])
        up = [(i, (i + 1) % size) for i in range(size - 1)]
        down = [(j, i) for i, j in up]
        last = lax.slice_in_dim(shard, length - width, length, axis=dim)
        leading = lax.slice_in_dim(shard, 0, width, axis=dim)
        before = lax.ppermute(last, axis, up)
        after = lax.ppermute(leading, axis, down)
        shard = jnp.concatenate([before, shard, after], axis=dim)
    return shard


def shifted(block, axis, distance):
    devices = range(lax.axis_size(axis))
    route = [(i - distance, i) for i in devices if i - distance in devices]
    return lax.ppermute(block, axis, route)


def pair_core(query_part, key_part, value_part, grad_part, norm_part, delta_part, allowed, factor):
    scores = (
        jnp.einsum("qhd,khd->hqk", query_part, key_part, preferred_element_type=jnp.float32)
        * factor
    )
    attend = allowed * jnp.exp(scores - norm_part[:, :, None])
    grad_attend = jnp.einsum(
        "qhd,khd->hqk", grad_part, value_part, preferred_element_type=jnp.float32
    )
    grad_scores = (attend * (grad_attend - delta_part[:, :, None])).astype(jnp.bfloat16)
    return (attend.astype(jnp.bfloat16), grad_scores)


def body(query_tiles, key_tiles, value_tiles, grad_output, log_norm, row_delta, extents):
    tile_rows = query_tiles.shape[2]
    channels = query_tiles.shape[3]
    local_heads = log_norm.shape[2]
    head_size = channels // local_heads
    factor = head_size ** (-0.5)
    time_all = lax.axis_size("tm")
    frame_tiles = lax.axis_size("space")
    time_pos = lax.axis_index("tm")
    frame_pos = lax.axis_index("space")
    pair_count = 3 * frame_tiles
    time_offsets = np.repeat(np.arange(-1, 2), frame_tiles).astype(np.int32)
    targets = np.tile(np.arange(frame_tiles), 3).astype(np.int32)
    target_height = targets // WIDTH_TILES
    target_width = targets % WIDTH_TILES
    time_gap = np.abs(time_offsets)
    local_time = time_pos % time_all + time_offsets
    inside = (local_time >= 0) & (local_time < time_all)
    height_gap = jnp.abs(target_height - frame_pos // WIDTH_TILES)
    width_gap = jnp.abs(target_width - frame_pos % WIDTH_TILES)
    split_shape = (tile_rows, local_heads, head_size)
    own_query = query_tiles[0, 0].reshape(split_shape)
    own_grad = grad_output[0, 0].reshape(split_shape)
    own_norm = log_norm[0, 0]
    own_delta = row_delta[0, 0]
    own_extent = extents[time_pos, frame_pos]
    key_flags = (
        inside
        & (time_gap <= own_extent[0])
        & (height_gap <= own_extent[1])
        & (width_gap <= own_extent[2])
    ).astype(jnp.float32)
    frame_keys, frame_values = (
        lax.all_gather(key_tiles, "space", axis=1, tiled=True),
        lax.all_gather(value_tiles, "space", axis=1, tiled=True),
    )
    near_keys, near_values = (
        with_halo(frame_keys, (("tm", 0),), 1),
        with_halo(frame_values, (("tm", 0),), 1),
    )
    near_keys = near_keys.reshape((pair_count,) + split_shape)
    near_values = near_values.reshape((pair_count,) + split_shape)
    zero_query = jnp.zeros(split_shape, jnp.float32)

    def pair_step(running, member):
        allowed, near_key, near_value = member
        attend, grad_scores = pair_core(
            own_query, near_key, near_value, own_grad, own_norm, own_delta, allowed, factor
        )
        query_term = (
            jnp.einsum("hqk,khd->qhd", grad_scores, near_key, preferred_element_type=jnp.float32)
            * factor
        )
        key_term = (
            jnp.einsum("hqk,qhd->khd", grad_scores, own_query, preferred_element_type=jnp.float32)
            * factor
        ).astype(jnp.bfloat16)
        value_term = jnp.einsum(
            "hqk,qhd->khd", attend, own_grad, preferred_element_type=jnp.float32
        ).astype(jnp.bfloat16)
        query_term, pair_part = (
            query_term,
            jnp.stack(
                [key_term.reshape(tile_rows, channels), value_term.reshape(tile_rows, channels)]
            ),
        )
        return (running + query_term, pair_part)

    grad_query, pair_parts = lax.scan(pair_step, zero_query, (key_flags, near_keys, near_values))
    pair_parts = pair_parts.reshape(3, frame_tiles, 2, tile_rows, channels)
    arrived = []
    for shift_by, row_part in ((-1, pair_parts[0]), (1, pair_parts[2])):
        arrived.append(shifted(row_part, "tm", shift_by))
    by_source = jnp.stack([pair_parts[1], arrived[0], arrived[1]])
    landed = lax.all_to_all(by_source, "space", split_axis=1, concat_axis=1, tiled=True)
    pair_total = jnp.sum(landed.astype(jnp.float32), axis=(0, 1))
    out_shape = (1, 1, tile_rows, channels)
    grad_key = pair_total[0].astype(jnp.bfloat16).reshape(out_shape)
    grad_value = pair_total[1].astype(jnp.bfloat16).reshape(out_shape)
    return (grad_query.astype(jnp.bfloat16).reshape(out_shape), grad_key, grad_value)


def solution(mesh):
    placed = (
        P("tm", "space", None, "heads"),
        P("tm", "space", None, "heads"),
        P("tm", "space", None, "heads"),
        P("tm", "space", None, "heads"),
        P("tm", "space", "heads", None),
        P("tm", "space", "heads", None),
        P(),
    )
    return jax.shard_map(
        body,
        mesh=mesh,
        in_specs=placed,
        out_specs=(
            P("tm", "space", None, "heads"),
            P("tm", "space", None, "heads"),
            P("tm", "space", None, "heads"),
        ),
        check_vma=False,
    )
```

profile of v0, /device:TPU:184, one launch (start us, length us, event | category | flops | bytes accessed | tf_op | source)
XLA Modules:
  0.0 486.2 jit_solution(12768828253215446786)
XLA Ops:
  8.7 31.1 %all-gather.5.cloned.1.call-done = bf16[1,4,384,384]{3,2,0,1:T(8,128)(2,1)} async-done(((bf16[1,1,384,384]{3,2,0,1:T(8,128)(2,1)}), bf16[1,4,384,384]{3,2,0,1:T(8,128)(2,1)}) %all-gather.5.cloned.1.call-update) | async-done | bytes 1179664 | tf_op jit(solution)/shard_map/all_gather | solution.py:76
  41.5 3.3 collective-permute-start.3
  44.8 6.7 %collective-permute-start.2 = (bf16[1,4,384,384]{2,3,1,0:T(8,128)(2,1)S(1)}, bf16[1,4,384,384]{2,3,1,0:T(8,128)(2,1)}, u32[]{:S(2)}, u32[]{:S(2)}) collective-permute-start(bf16[1,4,384,384]{2,3,1,0:T(8,128)(2,1)S(1)} %copy.43), channel_id=1, source_target_pairs={{0,16},{16,32},{32,48},{48,64},{64,80},{80,96},{96,112},{112,128},... | collective-permute-start | bytes 3538952 | tf_op jit(solution)/shard_map/ppermute | solution.py:17
  51.6 57.2 %all-gather.3.cloned.1.call-done = bf16[1,4,384,384]{3,2,0,1:T(8,128)(2,1)} async-done(((bf16[1,1,384,384]{3,2,0,1:T(8,128)(2,1)}), bf16[1,4,384,384]{3,2,0,1:T(8,128)(2,1)}) %all-gather.3.cloned.1.call-update) | async-done | bytes 1179664 | tf_op jit(solution)/shard_map/all_gather | solution.py:75
  110.5 1.9 collective-permute-start.1
  112.4 9.5 %collective-permute-start = (bf16[1,4,384,384]{2,3,1,0:T(8,128)(2,1)S(1)}, bf16[1,4,384,384]{2,3,1,0:T(8,128)(2,1)}, u32[]{:S(2)}, u32[]{:S(2)}) collective-permute-start(bf16[1,4,384,384]{2,3,1,0:T(8,128)(2,1)S(1)} %copy.38), channel_id=1, source_target_pairs={{0,16},{16,32},{32,48},{48,64},{64,80},{80,96},{96,112},{112,128},... | collective-permute-start | bytes 3538952 | tf_op jit(solution)/shard_map/ppermute | solution.py:17
  124.8 3.2 and_convert_fusion
  127.9 3.3 pad_maximum_fusion.2
  131.2 39.2 %collective-permute-done.1 = bf16[1,4,384,384]{2,3,1,0:T(8,128)(2,1)} collective-permute-done((bf16[1,4,384,384]{2,3,1,0:T(8,128)(2,1)S(1)}, bf16[1,4,384,384]{2,3,1,0:T(8,128)(2,1)}, u32[]{:S(2)}, u32[]{:S(2)}) %collective-permute-start.1) | collective-permute-done | bytes 1179680 | tf_op jit(solution)/shard_map/ppermute | solution.py:18
  171.3 3.4 pad_maximum_fusion.1
  174.7 87.9 %while.13 = (s32[]{:T(128)}, f32[384,3,128]{0,2,1:T(8,128)S(1)}, bf16[12,2,384,384]{2,3,1,0:T(8,128)(2,1)}, bf16[12,384,3,128]{1,3,2,0:T(8,128)(2,1)}, f32[12]{0...) while((s32[]{:T(128)}, f32[384,3,128]{0,2,1:T(8,128)S(1)}, ...), condition=%wide.region_1.2_spmd.clone, body=%wide.region_0.1_spmd.clone.sunk | while | flops 571392000 | bytes 12986019 | solution.py:110
  175.2 2.1 exponential_multiply_fusion.2
  182.6 2.1 exponential_multiply_fusion.2
  189.9 2.1 exponential_multiply_fusion.2
  197.2 2.1 exponential_multiply_fusion.2
  204.5 2.1 exponential_multiply_fusion.2
  211.9 2.1 exponential_multiply_fusion.2
  219.2 2.1 exponential_multiply_fusion.2
  226.5 2.1 exponential_multiply_fusion.2
  233.8 2.1 exponential_multiply_fusion.2
  241.1 2.1 exponential_multiply_fusion.2
  248.5 2.1 exponential_multiply_fusion.2
  255.8 2.1 exponential_multiply_fusion.2
  262.5 4.0 slice_bitcast_fusion
  266.5 10.7 %collective-permute-start.5 = (bf16[4,2,384,384]{2,3,1,0:T(8,128)(2,1)S(1)}, bf16[4,2,384,384]{2,3,1,0:T(8,128)(2,1)S(1)}, u32[]{:S(2)}, u32[]{:S(2)}) collective-permute-start(bf16[4,2,384,384]{2,3,1,0:T(8,128)(2,1)S(1)} %get-tuple-element.148), channel_id=1, source_target_pairs={{0,16},{16,32},{32,48},{48,64},{64,80},{80,96},{96,112},{112,128},... | collective-permute-start | bytes 7077896 | tf_op jit(solution)/shard_map/ppermute | solution.py:26
  277.2 1.9 collective-permute-start.4
  279.1 96.6 %collective-permute-done.5 = bf16[4,2,384,384]{2,3,1,0:T(8,128)(2,1)S(1)} collective-permute-done((bf16[4,2,384,384]{2,3,1,0:T(8,128)(2,1)S(1)}, bf16[4,2,384,384]{2,3,1,0:T(8,128)(2,1)S(1)}, u32[]{:S(2)}, u32[]{:S(2)}) %collective-permute-start.5) | collective-permute-done | bytes 2359328 | tf_op jit(solution)/shard_map/ppermute | solution.py:26
  375.7 9.5 %collective-permute-done.4 = bf16[4,2,384,384]{2,3,1,0:T(8,128)(2,1)S(1)} collective-permute-done((bf16[4,2,384,384]{2,3,1,0:T(8,128)(2,1)S(1)}, bf16[4,2,384,384]{2,3,1,0:T(8,128)(2,1)S(1)}, u32[]{:S(2)}, u32[]{:S(2)}) %collective-permute-start.4) | collective-permute-done | bytes 2359328 | tf_op jit(solution)/shard_map/ppermute | solution.py:26
  385.2 3.7 pad_maximum_fusion
  388.8 5.4 %all-to-all-start = ((bf16[3,4,2,384,384]{3,4,2,0,1:T(8,128)(2,1)}), bf16[3,4,2,384,384]{3,4,2,0,1:T(8,128)(2,1)}, u32[]{:S(2)}, u32[]{:S(2)}) async-start(bf16[3,4,2,384,384]{3,4,2,0,1:T(8,128)(2,1)} %pad_maximum_fusion), calls=%async_computation | async-start | bytes 14155776 | tf_op jit(solution)/shard_map/all_to_all | solution.py:116
  395.2 78.2 %all-to-all-done = bf16[3,4,2,384,384]{3,4,2,0,1:T(8,128)(2,1)} async-done(((bf16[3,4,2,384,384]{3,4,2,0,1:T(8,128)(2,1)}), bf16[3,4,2,384,384]{3,4,2,0,1:T(8,128)(2,1)}, u32[]{:S(2)}, u32[]{:S(2)}) %all-to-all-start) | async-done | bytes 7077920 | tf_op jit(solution)/shard_map/all_to_all | solution.py:116
  473.4 4.2 reduce
  (101 shorter events, 73.1 us)
Async XLA Ops:
  7.2 32.6 %all-gather.5.cloned.1.call-start = ((), (), s32[]{:S(2)}) async-start(), calls=%async_computation.2 | async-start | bytes 1474560 | tf_op jit(solution)/shard_map/all_gather | solution.py:76
  7.9 100.9 %all-gather.3.cloned.1.call-start = ((), (), s32[]{:S(2)}) async-start(), calls=%async_computation.1 | async-start | bytes 1474560 | tf_op jit(solution)/shard_map/all_gather | solution.py:75
  8.6 113.3 %copy-start.1 = (f32[1,1,3,384]{3,1,2,0:T(1,128)S(1)}, f32[1,1,3,384]{3,1,2,0:T(1,128)}, u32[]{:S(2)}) copy-start(f32[1,1,3,384]{3,1,2,0:T(1,128)} %param.17) | copy-start | bytes 13828
  8.7 113.3 %copy-start.2 = (f32[1,1,3,384]{3,1,2,0:T(1,128)S(1)}, f32[1,1,3,384]{3,1,2,0:T(1,128)}, u32[]{:S(2)}) copy-start(f32[1,1,3,384]{3,1,2,0:T(1,128)} %param.18) | copy-start | bytes 13828
  8.7 113.3 %copy-start = (bf16[1,1,384,384]{3,2,1,0:T(8,128)(2,1)S(1)}, bf16[1,1,384,384]{3,2,1,0:T(8,128)(2,1)}, u32[]{:S(2)}) copy-start(bf16[1,1,384,384]{3,2,1,0:T(8,128)(2,1)} %param.13) | copy-start | bytes 884740
  41.5 86.4 %collective-permute-start.3 = (bf16[1,4,384,384]{2,3,1,0:T(8,128)(2,1)S(1)}, bf16[1,4,384,384]{2,3,1,0:T(8,128)(2,1)}, u32[]{:S(2)}, u32[]{:S(2)}) collective-permute-start(bf16[1,4,384,384]{2,3,1,0:T(8,128)(2,1)S(1)} %copy.43), channel_id=1, source_target_pairs={{16,0},{32,16},{48,32},{64,48},{80,64},{96,80},{112,96},{128,112},... | collective-permute-start | bytes 3538952 | tf_op jit(solution)/shard_map/ppermute | solution.py:18
  44.8 83.1 %collective-permute-start.2 = (bf16[1,4,384,384]{2,3,1,0:T(8,128)(2,1)S(1)}, bf16[1,4,384,384]{2,3,1,0:T(8,128)(2,1)}, u32[]{:S(2)}, u32[]{:S(2)}) collective-permute-start(bf16[1,4,384,384]{2,3,1,0:T(8,128)(2,1)S(1)} %copy.43), channel_id=1, source_target_pairs={{0,16},{16,32},{32,48},{48,64},{64,80},{80,96},{96,112},{112,128},... | collective-permute-start | bytes 3538952 | tf_op jit(solution)/shard_map/ppermute | solution.py:17
  110.5 59.9 %collective-permute-start.1 = (bf16[1,4,384,384]{2,3,1,0:T(8,128)(2,1)S(1)}, bf16[1,4,384,384]{2,3,1,0:T(8,128)(2,1)}, u32[]{:S(2)}, u32[]{:S(2)}) collective-permute-start(bf16[1,4,384,384]{2,3,1,0:T(8,128)(2,1)S(1)} %copy.38), channel_id=1, source_target_pairs={{16,0},{32,16},{48,32},{64,48},{80,64},{96,80},{112,96},{128,112},... | collective-permute-start | bytes 3538952 | tf_op jit(solution)/shard_map/ppermute | solution.py:18
  112.4 58.9 %collective-permute-start = (bf16[1,4,384,384]{2,3,1,0:T(8,128)(2,1)S(1)}, bf16[1,4,384,384]{2,3,1,0:T(8,128)(2,1)}, u32[]{:S(2)}, u32[]{:S(2)}) collective-permute-start(bf16[1,4,384,384]{2,3,1,0:T(8,128)(2,1)S(1)} %copy.38), channel_id=1, source_target_pairs={{0,16},{16,32},{32,48},{48,64},{64,80},{80,96},{96,112},{112,128},... | collective-permute-start | bytes 3538952 | tf_op jit(solution)/shard_map/ppermute | solution.py:17
  131.2 43.4 %copy-start.3 = (f32[12]{0:T(128)S(1)}, f32[12]{0:T(128)}, u32[]{:S(2)}) copy-start(f32[12]{0:T(128)} %and_convert_fusion) | copy-start | bytes 148
  266.5 109.2 %collective-permute-start.5 = (bf16[4,2,384,384]{2,3,1,0:T(8,128)(2,1)S(1)}, bf16[4,2,384,384]{2,3,1,0:T(8,128)(2,1)S(1)}, u32[]{:S(2)}, u32[]{:S(2)}) collective-permute-start(bf16[4,2,384,384]{2,3,1,0:T(8,128)(2,1)S(1)} %get-tuple-element.148), channel_id=1, source_target_pairs={{0,16},{16,32},{32,48},{48,64},{64,80},{80,96},{96,112},{112,128},... | collective-permute-start | bytes 7077896 | tf_op jit(solution)/shard_map/ppermute | solution.py:26
  277.2 108.0 %collective-permute-start.4 = (bf16[4,2,384,384]{2,3,1,0:T(8,128)(2,1)S(1)}, bf16[4,2,384,384]{2,3,1,0:T(8,128)(2,1)S(1)}, u32[]{:S(2)}, u32[]{:S(2)}) collective-permute-start(bf16[4,2,384,384]{2,3,1,0:T(8,128)(2,1)S(1)} %get-tuple-element.149), channel_id=1, source_target_pairs={{16,0},{32,16},{48,32},{64,48},{80,64},{96,80},{112,96},{128,112},... | collective-permute-start | bytes 7077896 | tf_op jit(solution)/shard_map/ppermute | solution.py:26
  388.8 84.6 %all-to-all-start = ((bf16[3,4,2,384,384]{3,4,2,0,1:T(8,128)(2,1)}), bf16[3,4,2,384,384]{3,4,2,0,1:T(8,128)(2,1)}, u32[]{:S(2)}, u32[]{:S(2)}) async-start(bf16[3,4,2,384,384]{3,4,2,0,1:T(8,128)(2,1)} %pad_maximum_fusion), calls=%async_computation | async-start | bytes 14155776 | tf_op jit(solution)/shard_map/all_to_all | solution.py:116
Sparse Core Ops, SparseCore 0:
  10.1 29.6 all-gather.4
  41.9 66.8 all-gather.2
where the time goes:
time: 488 us; the launch traced here: 486 us
  waiting for transfers between devices  314 us (64%)
  matrix products  69.7 us (14%)
  starting transfers between devices  39.5 us (8%)
  other arithmetic  28.4 us (6%)
  local copies, waits for them, and re-layouts  19.8 us (4%)
  between operations  14.3 us (3%)
    ppermute x2, waiting for transfers between devices, shifted(): return lax.ppermute(block, axis, route)  106 us
    all_to_all x1, waiting for transfers between devices, body(): lax.all_to_all(by_source, 'space', split_axis=1, concat_axis=1, tiled=True)  78.2 us
    all_gather x1, waiting for transfers between devices, body(): lax.all_gather(key_tiles, 'space', axis=1, tiled=True)  57.2 us
    ppermute x2, waiting for transfers between devices, with_halo(): after = lax.ppermute(leading, axis, down)  39.2 us
    all_gather x1, waiting for transfers between devices, body(): lax.all_gather(value_tiles, 'space', axis=1, tiled=True)  31.1 us
    dot_general x12, matrix products, pair_core(): jnp.einsum('qhd,khd->hqk', query_part, key_part, preferred_element_type=j...  25.6 us
    dot_general x12, matrix products, pair_core(): jnp.einsum('qhd,khd->hqk', grad_part, value_part, preferred_element_type=...  17.1 us
    dot_general x12, matrix products, pair_step(): jnp.einsum('hqk,khd->qhd', grad_scores, near_key, preferred_element_type=...  17 us
  transfers between devices with their start and end apart: 9, of which 7 were waited for; matrix products, arithmetic and copies ran while one was open for 3% of the time, Pallas kernels for 0%

commit v1 on v0

v1 whole, which is shorter than its diff:
```python
import functools

import jax
import jax.numpy as jnp
from jax import lax
from jax.experimental import pallas as pl
from jax.experimental.pallas import tpu as pltpu
from jax.sharding import PartitionSpec as P

RING = 8
LOG2E = 1.4426950408889634
HEAD = 128
BF = jnp.bfloat16
F32 = jnp.float32


def send(block, pairs):
    return lax.ppermute(block, ("tm", "space"), pairs)


def routes(time_all):
    at = lambda t, c, w: t * 4 + c * 2 + w
    ts, cs = range(time_all), range(2)
    core = [(at(t, c, w), at(t, c, 1 - w)) for t in ts for c in cs for w in cs]
    pair = [(at(t, c, w), at(t, 1 - c, w)) for t in ts for c in cs for w in cs]
    up, lend, lent_core = [], [], []
    for t in range(time_all - 1):
        for w in cs:
            if t % RING == RING - 1:
                up.append((at(t, 1, w), at(t + 1, 0, w)))
                lend.append((at(t, 0, w), at(t, 1, w)))
                lend.append((at(t + 1, 1, w), at(t + 1, 0, w)))
                lent_core.append((at(t, 1, w), at(t, 1, 1 - w)))
                lent_core.append((at(t + 1, 0, w), at(t + 1, 0, 1 - w)))
            else:
                up += [(at(t, c, w), at(t + 1, c, w)) for c in cs]
    back = lambda pairs: [(j, i) for i, j in pairs]
    return dict(core=core, pair=pair, up=up, down=back(up), lend=lend, lent_core=lent_core, give=back(lend))


def aux_rows(pack, rows):
    return pack[2 * rows :, :].astype(F32)


def accumulate(pack, flags, base, count, kv, acc, dq, rows, factor):
    heads = pack.shape[1] // HEAD
    dq[...] = jnp.zeros_like(dq)
    aux = pack[2 * rows :, :].astype(F32)

    def step(j, carry):
        @pl.when(flags[base + j] != 0)
        def _():
            for h in range(heads):
                cols = slice(h * HEAD, (h + 1) * HEAD)
                part = lambda i: aux[(3 * i) * heads + h : (3 * i) * heads + h + 1] + (
                    aux[(3 * i + 1) * heads + h : (3 * i + 1) * heads + h + 1]
                    + aux[(3 * i + 2) * heads + h : (3 * i + 2) * heads + h + 1]
                )
                norm, delta = part(0) * LOG2E, part(1)
                q, g = pack[0:rows, cols], pack[rows : 2 * rows, cols]
                k, v = kv[j, 0:rows, cols], kv[j, rows : 2 * rows, cols]
                last = (((1,), (1,)), ((), ()))
                st = lax.dot_general(k, q, last, preferred_element_type=F32)
                p = jnp.exp2(st * (factor * LOG2E) - norm)
                dp = lax.dot_general(v, g, last, preferred_element_type=F32)
                ds = (p * (dp - delta)).astype(BF)
                acc[j, rows : 2 * rows, cols] += jnp.dot(p.astype(BF), g, preferred_element_type=F32)
                acc[j, 0:rows, cols] += jnp.dot(ds, q, preferred_element_type=F32)
                dq[:, cols] += lax.dot_general(ds, k, (((0,), (0,)), ((), ())), preferred_element_type=F32)

        return carry

    lax.fori_loop(0, count, step, 0)


def frame_kernel(rows, factor, flags, mine, other, kv_a, kv_b, acc, dq_mine, dq_other, kv):
    kv[0] = kv_a[...]
    kv[1] = kv_b[...]
    acc[...] = jnp.zeros_like(acc)
    accumulate(mine, flags, 0, 2, kv, acc, dq_mine, rows, factor)
    accumulate(other, flags, 4, 2, kv, acc, dq_other, rows, factor)
    dq_mine[...] = dq_mine[...] * factor
    dq_other[...] = dq_other[...] * factor


def near_kernel(rows, factor, flags, low, high, kv_a, kv_b, kv_c, kv_d, acc_in, acc, dq_low, dq_high, kv, dq):
    for i, ref in enumerate((kv_a, kv_b, kv_c, kv_d)):
        kv[i] = ref[...]
    acc[0:2] = acc_in[...]
    acc[2:4] = jnp.zeros_like(acc[2:4])
    accumulate(low, flags, 8, 4, kv, acc, dq, rows, factor)
    dq_low[...] = (dq[...] * factor).astype(BF)
    accumulate(high, flags, 12, 4, kv, acc, dq, rows, factor)
    dq_high[...] = (dq[...] * factor).astype(BF)


def far_kernel(rows, factor, flags, low, high, kv_a, kv_b, kv_c, kv_d, acc_in, near_low, near_high,
               msg_low, msg_high, own, lent, sib, kv, acc, dq):
    for i, ref in enumerate((kv_a, kv_b, kv_c, kv_d)):
        kv[i] = ref[...]
    acc[...] = acc_in[...]
    msg_low[0:rows] = near_low[...]
    msg_high[0:rows] = near_high[...]
    accumulate(low, flags, 16, 4, kv, acc, dq, rows, factor)
    msg_low[rows:] = (dq[...] * factor).astype(BF)
    accumulate(high, flags, 20, 4, kv, acc, dq, rows, factor)
    msg_high[rows:] = (dq[...] * factor).astype(BF)
    own[0:rows] = acc[0, 0:rows] * factor
    own[rows:] = acc[0, rows:]
    lent[0:rows] = acc[2, 0:rows] * factor
    lent[rows:] = acc[2, rows:]
    for i, j in enumerate((1, 3)):
        sib[i, 0:rows] = (acc[j, 0:rows] * factor).astype(BF)
        sib[i, rows:] = acc[j, rows:].astype(BF)


def call(kernel, shapes, scratch, operands, pairs, name):
    whole = pl.BlockSpec(memory_space=pltpu.VMEM)
    return pl.pallas_call(
        kernel,
        out_shape=shapes,
        in_specs=[pl.BlockSpec(memory_space=pltpu.SMEM)] + [whole] * (len(operands) - 1),
        out_specs=[whole] * len(shapes),
        scratch_shapes=scratch,
        compiler_params=pltpu.CompilerParams(vmem_limit_bytes=40 * 2**20),
        cost_estimate=pl.CostEstimate(flops=pairs * 566_000_000, bytes_accessed=8_000_000, transcendentals=pairs * 442_368),
        name=name,
    )(*operands)


def thirds(x):
    hi = lax.reduce_precision(x, 8, 7)
    mid = lax.reduce_precision(x - hi, 8, 7)
    return [hi.astype(BF), mid.astype(BF), (x - hi - mid).astype(BF)]


def pair_flags(extents, time_pos, chip, core, time_all):
    low_cross = (time_pos % RING == 0) & (time_pos > 0)
    high_cross = (time_pos % RING == RING - 1) & (time_pos < time_all - 1)
    false = jnp.bool_(False)
    flags = []
    for step, cross, inner, flip in (
        (0, false, false, 0), (0, false, false, 1),
        (-1, low_cross, chip == 0, 0), (1, high_cross, chip == 1, 0),
        (-1, low_cross, chip == 0, 1), (1, high_cross, chip == 1, 1),
    ):
        when = time_pos + step
        inside = (when >= 0) & (when < time_all)
        height = jnp.where(cross, 1 - chip, chip)
        height = 1 - height if flip else height
        extent = extents[jnp.clip(when, 0, time_all - 1), height * 2 + core]
        for key_flip, width_gap in ((0, 0), (0, 1), (1, 0), (1, 1)):
            key_height = 1 - chip if key_flip else chip
            taken = cross & inner if key_flip else ~cross | inner
            flags.append(
                inside & taken & (abs(step) <= extent[0])
                & (jnp.abs(key_height - height) <= extent[1]) & (width_gap <= extent[2])
            )
    return jnp.stack(flags).astype(jnp.int32)


def body(query_tiles, key_tiles, value_tiles, grad_output, log_norm, row_delta, extents):
    rows, channels = query_tiles.shape[2:]
    heads = log_norm.shape[2]
    factor = (channels // heads) ** (-0.5)
    time_all = lax.axis_size("tm")
    time_pos, frame_pos = lax.axis_index("tm"), lax.axis_index("space")
    chip, core = frame_pos // 2, frame_pos % 2
    route = routes(time_all)
    flags = pair_flags(extents, time_pos, chip, core, time_all)

    pad = jnp.zeros((32 - 6 * heads, channels), BF)
    mine = jnp.concatenate(
        [query_tiles[0, 0], grad_output[0, 0]] + thirds(log_norm[0, 0]) + thirds(row_delta[0, 0]) + [pad]
    )
    kv_a = jnp.concatenate([key_tiles[0, 0], value_tiles[0, 0]])

    other = send(mine, route["pair"])
    near_low = send(mine, route["up"])
    near_high = send(mine, route["down"])
    kv_b = send(kv_a, route["core"])
    far_low = send(other, route["up"])
    far_high = send(other, route["down"])
    kv_c = send(kv_a, route["lend"])
    kv_d = send(kv_c, route["lent_core"])

    tile, two = (rows, channels), (2 * rows, channels)
    out = jax.ShapeDtypeStruct
    with jax.named_scope("frame"):
        acc, dq_mine, dq_other = call(
            functools.partial(frame_kernel, rows, factor),
            [out((2,) + two, F32), out(tile, F32), out(tile, F32)],
            [pltpu.VMEM((2,) + two, BF)],
            (flags, mine, other, kv_a, kv_b), 4, "frame",
        )
    with jax.named_scope("near"):
        acc, dq_low, dq_high = call(
            functools.partial(near_kernel, rows, factor),
            [out((4,) + two, F32), out(tile, BF), out(tile, BF)],
            [pltpu.VMEM((4,) + two, BF), pltpu.VMEM(tile, F32)],
            (flags, near_low, near_high, kv_a, kv_b, kv_c, kv_d, acc), 6, "near",
        )
    with jax.named_scope("far"):
        msg_low, msg_high, own, lent, sib = call(
            functools.partial(far_kernel, rows, factor),
            [out(two, BF), out(two, BF), out(two, F32), out(two, F32), out((2,) + two, BF)],
            [pltpu.VMEM((4,) + two, BF), pltpu.VMEM((4,) + two, F32), pltpu.VMEM(tile, F32)],
            (flags, far_low, far_high, kv_a, kv_b, kv_c, kv_d, acc, dq_low, dq_high), 6, "far",
        )
    from_high = send(msg_low, route["down"])
    from_low = send(msg_high, route["up"])
    sib = send(sib, route["core"])
    lent = (lent + sib[1].astype(F32)).astype(BF)
    given = send(lent, route["give"])
    other_total = dq_other + from_high[rows:].astype(F32) + from_low[rows:].astype(F32)
    swapped = send(other_total.astype(BF), route["pair"])
    total = dq_mine + from_high[:rows].astype(F32) + from_low[:rows].astype(F32) + swapped.astype(F32)
    grad_kv = (own + sib[0].astype(F32) + given.astype(F32)).astype(BF)
    shape = (1, 1, rows, channels)
    return total.astype(BF).reshape(shape), grad_kv[:rows].reshape(shape), grad_kv[rows:].reshape(shape)


def solution(mesh):
    tiles, per_row = P("tm", "space", None, "heads"), P("tm", "space", "heads", None)
    return jax.shard_map(
        body,
        mesh=mesh,
        in_specs=(tiles, tiles, tiles, tiles, per_row, per_row, P()),
        out_specs=(tiles, tiles, tiles),
        check_vma=False,
    )
```

time: 488 us -> 117 us (0.24)
  the two profiles are of different devices: /device:TPU:184 before, /device:TPU:384 now
where the time goes in v1:
time: 117 us
  starting transfers between devices  39.4 us (34%)
  waiting for transfers between devices  35.9 us (31%)
  between operations  18.7 us (16%)
  Pallas kernels  15.7 us (13%)
  local copies, waits for them, and re-layouts  4.38 us (4%)
  other arithmetic  2.45 us (2%)
    ppermute x13, starting transfers between devices, send(): return lax.ppermute(block, ('tm', 'space'), pairs)  39.4 us
    ppermute x13, waiting for transfers between devices, send(): return lax.ppermute(block, ('tm', 'space'), pairs)  35.9 us
    pallas_call x3, Pallas kernels, call(): pl.pallas_call(kernel, out_shape=shapes, in_specs=[pl.BlockSpec(memory_sp...  15.7 us
  transfers between devices with their start and end apart: 13, of which 5 were waited for; matrix products, arithmetic and copies ran while one was open for 2% of the time, Pallas kernels for 10%

profile of v1, /device:TPU:384, one launch (start us, length us, event | category | flops | bytes accessed | tf_op | source)
XLA Modules:
  0.0 116.5 jit_solution(5358537289161889630)
XLA Ops:
  0.7 1.2 %pad_maximum_fusion.kv_a = bf16[768,384]{1,0:T(8,128)(2,1)S(1)} fusion(bf16[384,384]{1,0:T(8,128)(2,1)} %bitcast.78, bf16[384,384]{1,0:T(8,128)(2,1)} %bitcast.79), kind=kLoop, calls=%fused_computation.7 | loop fusion | flops 1179648 | bytes 1179648 | tf_op jit(solution)/shard_map/concatenate | solution.py:176
  1.9 1.3 %collective-permute-start.4 = (bf16[768,384]{1,0:T(8,128)(2,1)S(1)}, bf16[768,384]{1,0:T(8,128)(2,1)}, u32[]{:S(2)}, u32[]{:S(2)}) collective-permute-start(bf16[768,384]{1,0:T(8,128)(2,1)S(1)} %pad_maximum_fusion.kv_a), channel_id=1, source_target_pairs={{112,120},{136,128},{116,124},{140,132},{240,248},{264,256},{244,2... | collective-permute-start | bytes 1769480 | tf_op jit(solution)/shard_map/ppermute | solution.py:18
  3.2 0.7 concatenate.6.mine
  3.9 5.3 %collective-permute-start = (bf16[800,384]{1,0:T(8,128)(2,1)S(1)}, bf16[800,384]{1,0:T(8,128)(2,1)S(1)}, u32[]{:S(2)}, u32[]{:S(2)}) collective-permute-start(bf16[800,384]{1,0:T(8,128)(2,1)S(1)} %concatenate.6.mine), channel_id=1, source_target_pairs={{0,8},{4,12},{8,0},{12,4},{16,24},{20,28},{24,16},{28,20},{32,40},... | collective-permute-start | bytes 1843208 | tf_op jit(solution)/shard_map/ppermute | solution.py:18
  9.3 1.9 %collective-permute-start.1 = (bf16[768,384]{1,0:T(8,128)(2,1)S(1)}, bf16[768,384]{1,0:T(8,128)(2,1)S(1)}, u32[]{:S(2)}, u32[]{:S(2)}) collective-permute-start(bf16[768,384]{1,0:T(8,128)(2,1)S(1)} %pad_maximum_fusion.kv_a), channel_id=1, source_target_pairs={{0,4},{4,0},{8,12},{12,8},{16,20},{20,16},{24,28},{28,24},{32,36},... | collective-permute-start | bytes 1769480 | tf_op jit(solution)/shard_map/ppermute | solution.py:18
  11.2 5.4 %collective-permute-start.7 = (bf16[800,384]{1,0:T(8,128)(2,1)S(1)}, bf16[800,384]{1,0:T(8,128)(2,1)S(1)}, u32[]{:S(2)}, u32[]{:S(2)}) collective-permute-start(bf16[800,384]{1,0:T(8,128)(2,1)S(1)} %concatenate.6.mine), channel_id=1, source_target_pairs={{16,0},{24,8},{20,4},{28,12},{32,16},{40,24},{36,20},{44,28},{48,3... | collective-permute-start | bytes 1843208 | tf_op jit(solution)/shard_map/ppermute | solution.py:18
  16.6 1.9 %collective-permute-start.6 = (bf16[800,384]{1,0:T(8,128)(2,1)S(1)}, bf16[800,384]{1,0:T(8,128)(2,1)}, u32[]{:S(2)}, u32[]{:S(2)}) collective-permute-start(bf16[800,384]{1,0:T(8,128)(2,1)S(1)} %concatenate.6.mine), channel_id=1, source_target_pairs={{0,16},{8,24},{4,20},{12,28},{16,32},{24,40},{20,36},{28,44},{32,4... | collective-permute-start | bytes 1843208 | tf_op jit(solution)/shard_map/ppermute | solution.py:18
  18.5 1.6 %collective-permute-done.4.kv_c = bf16[768,384]{1,0:T(8,128)(2,1)} collective-permute-done((bf16[768,384]{1,0:T(8,128)(2,1)S(1)}, bf16[768,384]{1,0:T(8,128)(2,1)}, u32[]{:S(2)}, u32[]{:S(2)}) %collective-permute-start.4) | collective-permute-done | bytes 589856 | tf_op jit(solution)/shard_map/ppermute | solution.py:18
  20.1 1.9 %collective-permute-start.5 = (bf16[768,384]{1,0:T(8,128)(2,1)}, bf16[768,384]{1,0:T(8,128)(2,1)}, u32[]{:S(2)}, u32[]{:S(2)}) collective-permute-start(bf16[768,384]{1,0:T(8,128)(2,1)} %collective-permute-done.4.kv_c), channel_id=1, source_target_pairs={{120,124},{128,132},{124,120},{132,128},{248,252},{256,260},{252,2... | collective-permute-start | bytes 1769480 | tf_op jit(solution)/shard_map/ppermute | solution.py:18
  22.0 10.0 %collective-permute-done.other = bf16[800,384]{1,0:T(8,128)(2,1)S(1)} collective-permute-done((bf16[800,384]{1,0:T(8,128)(2,1)S(1)}, bf16[800,384]{1,0:T(8,128)(2,1)S(1)}, u32[]{:S(2)}, u32[]{:S(2)}) %collective-permute-start) | collective-permute-done | bytes 614432 | tf_op jit(solution)/shard_map/ppermute | solution.py:18
  32.0 5.4 %collective-permute-start.3 = (bf16[800,384]{1,0:T(8,128)(2,1)S(1)}, bf16[800,384]{1,0:T(8,128)(2,1)S(1)}, u32[]{:S(2)}, u32[]{:S(2)}) collective-permute-start(bf16[800,384]{1,0:T(8,128)(2,1)S(1)} %collective-permute-done.other), channel_id=1, source_target_pairs={{16,0},{24,8},{20,4},{28,12},{32,16},{40,24},{36,20},{44,28},{48,3... | collective-permute-start | bytes 1843208 | tf_op jit(solution)/shard_map/ppermute | solution.py:18
  37.4 0.8 copy-done
  38.2 1.9 %collective-permute-start.2 = (bf16[800,384]{1,0:T(8,128)(2,1)S(1)}, bf16[800,384]{1,0:T(8,128)(2,1)}, u32[]{:S(2)}, u32[]{:S(2)}) collective-permute-start(bf16[800,384]{1,0:T(8,128)(2,1)S(1)} %collective-permute-done.other), channel_id=1, source_target_pairs={{0,16},{8,24},{4,20},{12,28},{16,32},{24,40},{20,36},{28,44},{32,4... | collective-permute-start | bytes 1843208 | tf_op jit(solution)/shard_map/ppermute | solution.py:18
  40.2 0.8 fusion.6
  58.7 0.1 stack.83
  58.8 1.1 copy-done.1
  59.9 6.7 %frame.1 = (f32[2,768,384]{2,1,0:T(8,128)S(1)}, f32[384,384]{1,0:T(8,128)S(1)}, f32[384,384]{1,0:T(8,128)S(1)}) custom-call(s32[24]{0:T(128)S(1)} %convert_element_type.63.flags, bf16[800,384]{1,0:T(8,128)(2,1)S(1)} %concatenate.6.mine, bf16[800,384]{1,0:T(8,128)(2,1)S(1)} %collective-permute-done.other, bf16[768,384]{1,0:T(8,128)(2,1)S(1)} %pad_maximum_fusion.kv_a, ...), custom_call_target="tpu_custom_call" | custom-call | flops 2264000000 | bytes 8000000 | tf_op jit(solution)/shard_map/frame/frame/pallas_call | solution.py:119
  66.6 5.0 %near.1 = (f32[4,768,384]{2,1,0:T(8,128)S(1)}, bf16[384,384]{1,0:T(8,128)(2,1)S(1)}, bf16[384,384]{1,0:T(8,128)(2,1)S(1)}) custom-call(s32[24]{0:T(128)S(1)} %convert_element_type.63.flags, bf16[800,384]{1,0:T(8,128)(2,1)} %collective-permute-done.6.low, bf16[800,384]{1,0:T(8,128)(2,1)S(1)} %collective-permute-done.7.high, ...), custom_call_target="tpu_custom_call" | custom-call | flops 3396000000 | bytes 8000000 | tf_op jit(solution)/shard_map/near/near/pallas_call | solution.py:119
  71.6 4.0 %far.1 = (bf16[768,384]{1,0:T(8,128)(2,1)S(1)}, bf16[768,384]{1,0:T(8,128)(2,1)S(1)}, f32[768,384]{1,0:T(8,128)S(1)}, f32[768,384]{1,0:T(8,128)S(1)}, bf16[2,768,384]{2,1,0:T(8,128)(2,1)S(1)}) custom-call(s32[24]{0:T(128)S(1)} %convert_element_type.63.flags, bf16[800,384]{1,0:T(8,128)(2,1)} %collective-permute-done.2.low, ...), custom_call_target="tpu_custom_call" | custom-call | flops 3396000000 | bytes 8000000 | tf_op jit(solution)/shard_map/far/far/pallas_call | solution.py:119
  75.6 1.9 %collective-permute-start.11 = (bf16[2,768,384]{2,1,0:T(8,128)(2,1)S(1)}, bf16[2,768,384]{2,1,0:T(8,128)(2,1)S(1)}, u32[]{:S(2)}, u32[]{:S(2)}) collective-permute-start(bf16[2,768,384]{2,1,0:T(8,128)(2,1)S(1)} %get-tuple-element.23), channel_id=1, source_target_pairs={{0,4},{4,0},{8,12},{12,8},{16,20},{20,16},{24,28},{28,24},{32,36},... | collective-permute-start | bytes 3538952 | tf_op jit(solution)/shard_map/ppermute | solution.py:18
  77.5 7.3 %collective-permute-start.8 = (bf16[768,384]{1,0:T(8,128)(2,1)S(1)}, bf16[768,384]{1,0:T(8,128)(2,1)S(1)}, u32[]{:S(2)}, u32[]{:S(2)}) collective-permute-start(bf16[768,384]{1,0:T(8,128)(2,1)S(1)} %get-tuple-element.19), channel_id=1, source_target_pairs={{16,0},{24,8},{20,4},{28,12},{32,16},{40,24},{36,20},{44,28},{48,3... | collective-permute-start | bytes 1769480 | tf_op jit(solution)/shard_map/ppermute | solution.py:18
  84.9 1.9 %collective-permute-start.9 = (bf16[768,384]{1,0:T(8,128)(2,1)S(1)}, bf16[768,384]{1,0:T(8,128)(2,1)S(1)}, u32[]{:S(2)}, u32[]{:S(2)}) collective-permute-start(bf16[768,384]{1,0:T(8,128)(2,1)S(1)} %get-tuple-element.20), channel_id=1, source_target_pairs={{0,16},{8,24},{4,20},{12,28},{16,32},{24,40},{20,36},{28,44},{32,4... | collective-permute-start | bytes 1769480 | tf_op jit(solution)/shard_map/ppermute | solution.py:18
  86.8 0.1 fusion
  86.9 1.3 %collective-permute-start.12 = (bf16[768,384]{1,0:T(8,128)(2,1)S(1)}, bf16[768,384]{1,0:T(8,128)(2,1)S(1)}, u32[]{:S(2)}, u32[]{:S(2)}) collective-permute-start(bf16[768,384]{1,0:T(8,128)(2,1)S(1)} %fusion), channel_id=1, source_target_pairs={{120,112},{128,136},{124,116},{132,140},{248,240},{256,264},{252,2... | collective-permute-start | bytes 1769480 | tf_op jit(solution)/shard_map/ppermute | solution.py:18
  88.3 9.8 %collective-permute-done.8 = bf16[768,384]{1,0:T(8,128)(2,1)S(1)} collective-permute-done((bf16[768,384]{1,0:T(8,128)(2,1)S(1)}, bf16[768,384]{1,0:T(8,128)(2,1)S(1)}, u32[]{:S(2)}, u32[]{:S(2)}) %collective-permute-start.8) | collective-permute-done | bytes 589856 | tf_op jit(solution)/shard_map/ppermute | solution.py:18
  98.1 6.2 %collective-permute-done.9 = bf16[768,384]{1,0:T(8,128)(2,1)S(1)} collective-permute-done((bf16[768,384]{1,0:T(8,128)(2,1)S(1)}, bf16[768,384]{1,0:T(8,128)(2,1)S(1)}, u32[]{:S(2)}, u32[]{:S(2)}) %collective-permute-start.9) | collective-permute-done | bytes 589856 | tf_op jit(solution)/shard_map/ppermute | solution.py:18
  104.3 0.1 add_convert_fusion.1
  104.4 1.9 %collective-permute-start.10 = (bf16[384,384]{1,0:T(8,128)(2,1)S(1)}, bf16[384,384]{1,0:T(8,128)(2,1)S(1)}, u32[]{:S(2)}, u32[]{:S(2)}) collective-permute-start(bf16[384,384]{1,0:T(8,128)(2,1)S(1)} %add_convert_fusion.1), channel_id=1, source_target_pairs={{0,8},{4,12},{8,0},{12,4},{16,24},{20,28},{24,16},{28,20},{32,40},... | collective-permute-start | bytes 884744 | tf_op jit(solution)/shard_map/ppermute | solution.py:18
  106.3 8.3 %collective-permute-done.10 = bf16[384,384]{1,0:T(8,128)(2,1)S(1)} collective-permute-done((bf16[384,384]{1,0:T(8,128)(2,1)S(1)}, bf16[384,384]{1,0:T(8,128)(2,1)S(1)}, u32[]{:S(2)}, u32[]{:S(2)}) %collective-permute-start.10) | collective-permute-done | bytes 294944 | tf_op jit(solution)/shard_map/ppermute | solution.py:18
  114.6 0.8 fusion.3
  115.5 0.2 fusion.2
  115.7 0.9 slice_bitcast_fusion.2
  (24 shorter events, 0.1 us)
Async XLA Ops:
  0.6 2.5 %copy-start.6 = (f32[1,1,3,384]{3,1,2,0:T(1,128)S(1)}, f32[1,1,3,384]{3,1,2,0:T(1,128)}, u32[]{:S(2)}) copy-start(f32[1,1,3,384]{3,1,2,0:T(1,128)} %param.12) | copy-start | bytes 13828
  0.6 2.5 %copy-start.5 = (f32[1,1,3,384]{3,1,2,0:T(1,128)S(1)}, f32[1,1,3,384]{3,1,2,0:T(1,128)}, u32[]{:S(2)}) copy-start(f32[1,1,3,384]{3,1,2,0:T(1,128)} %param.11) | copy-start | bytes 13828
  0.7 2.6 %copy-start.3 = (bf16[1,1,384,384]{3,2,1,0:T(8,128)(2,1)S(1)}, bf16[1,1,384,384]{3,2,1,0:T(8,128)(2,1)}, u32[]{:S(2)}) copy-start(bf16[1,1,384,384]{3,2,1,0:T(8,128)(2,1)} %param.10) | copy-start | bytes 884740
  0.7 2.6 %copy-start.2 = (bf16[1,1,384,384]{3,2,1,0:T(8,128)(2,1)S(1)}, bf16[1,1,384,384]{3,2,1,0:T(8,128)(2,1)}, u32[]{:S(2)}) copy-start(bf16[1,1,384,384]{3,2,1,0:T(8,128)(2,1)} %param.7) | copy-start | bytes 884740
  0.7 39.5 %copy-start.4 = (s32[32,4,3]{0,1,2:T(4,128)S(1)}, s32[32,4,3]{0,1,2:T(4,128)}, u32[]{:S(2)}) copy-start(s32[32,4,3]{0,1,2:T(4,128)} %param.13) | copy-start | bytes 4612
  1.9 18.2 %collective-permute-start.4 = (bf16[768,384]{1,0:T(8,128)(2,1)S(1)}, bf16[768,384]{1,0:T(8,128)(2,1)}, u32[]{:S(2)}, u32[]{:S(2)}) collective-permute-start(bf16[768,384]{1,0:T(8,128)(2,1)S(1)} %pad_maximum_fusion.kv_a), channel_id=1, source_target_pairs={{112,120},{136,128},{116,124},{140,132},{240,248},{264,256},{244,2... | collective-permute-start | bytes 1769480 | tf_op jit(solution)/shard_map/ppermute | solution.py:18
  3.9 28.1 %collective-permute-start = (bf16[800,384]{1,0:T(8,128)(2,1)S(1)}, bf16[800,384]{1,0:T(8,128)(2,1)S(1)}, u32[]{:S(2)}, u32[]{:S(2)}) collective-permute-start(bf16[800,384]{1,0:T(8,128)(2,1)S(1)} %concatenate.6.mine), channel_id=1, source_target_pairs={{0,8},{4,12},{8,0},{12,4},{16,24},{20,28},{24,16},{28,20},{32,40},... | collective-permute-start | bytes 1843208 | tf_op jit(solution)/shard_map/ppermute | solution.py:18
  9.3 28.1 %collective-permute-start.1 = (bf16[768,384]{1,0:T(8,128)(2,1)S(1)}, bf16[768,384]{1,0:T(8,128)(2,1)S(1)}, u32[]{:S(2)}, u32[]{:S(2)}) collective-permute-start(bf16[768,384]{1,0:T(8,128)(2,1)S(1)} %pad_maximum_fusion.kv_a), channel_id=1, source_target_pairs={{0,4},{4,0},{8,12},{12,8},{16,20},{20,16},{24,28},{28,24},{32,36},... | collective-permute-start | bytes 1769480 | tf_op jit(solution)/shard_map/ppermute | solution.py:18
  11.2 55.3 %collective-permute-start.7 = (bf16[800,384]{1,0:T(8,128)(2,1)S(1)}, bf16[800,384]{1,0:T(8,128)(2,1)S(1)}, u32[]{:S(2)}, u32[]{:S(2)}) collective-permute-start(bf16[800,384]{1,0:T(8,128)(2,1)S(1)} %concatenate.6.mine), channel_id=1, source_target_pairs={{16,0},{24,8},{20,4},{28,12},{32,16},{40,24},{36,20},{44,28},{48,3... | collective-permute-start | bytes 1843208 | tf_op jit(solution)/shard_map/ppermute | solution.py:18
  16.6 50.0 %collective-permute-start.6 = (bf16[800,384]{1,0:T(8,128)(2,1)S(1)}, bf16[800,384]{1,0:T(8,128)(2,1)}, u32[]{:S(2)}, u32[]{:S(2)}) collective-permute-start(bf16[800,384]{1,0:T(8,128)(2,1)S(1)} %concatenate.6.mine), channel_id=1, source_target_pairs={{0,16},{8,24},{4,20},{12,28},{16,32},{24,40},{20,36},{28,44},{32,4... | collective-permute-start | bytes 1843208 | tf_op jit(solution)/shard_map/ppermute | solution.py:18
  20.1 46.5 %collective-permute-start.5 = (bf16[768,384]{1,0:T(8,128)(2,1)}, bf16[768,384]{1,0:T(8,128)(2,1)}, u32[]{:S(2)}, u32[]{:S(2)}) collective-permute-start(bf16[768,384]{1,0:T(8,128)(2,1)} %collective-permute-done.4.kv_c), channel_id=1, source_target_pairs={{120,124},{128,132},{124,120},{132,128},{248,252},{256,260},{252,2... | collective-permute-start | bytes 1769480 | tf_op jit(solution)/shard_map/ppermute | solution.py:18
  32.0 39.6 %collective-permute-start.3 = (bf16[800,384]{1,0:T(8,128)(2,1)S(1)}, bf16[800,384]{1,0:T(8,128)(2,1)S(1)}, u32[]{:S(2)}, u32[]{:S(2)}) collective-permute-start(bf16[800,384]{1,0:T(8,128)(2,1)S(1)} %collective-permute-done.other), channel_id=1, source_target_pairs={{16,0},{24,8},{20,4},{28,12},{32,16},{40,24},{36,20},{44,28},{48,3... | collective-permute-start | bytes 1843208 | tf_op jit(solution)/shard_map/ppermute | solution.py:18
  37.4 0.8 copy-start
  38.2 33.4 %collective-permute-start.2 = (bf16[800,384]{1,0:T(8,128)(2,1)S(1)}, bf16[800,384]{1,0:T(8,128)(2,1)}, u32[]{:S(2)}, u32[]{:S(2)}) collective-permute-start(bf16[800,384]{1,0:T(8,128)(2,1)S(1)} %collective-permute-done.other), channel_id=1, source_target_pairs={{0,16},{8,24},{4,20},{12,28},{16,32},{24,40},{20,36},{28,44},{32,4... | collective-permute-start | bytes 1843208 | tf_op jit(solution)/shard_map/ppermute | solution.py:18
  58.8 1.1 copy-start.1
  75.6 11.2 %collective-permute-start.11 = (bf16[2,768,384]{2,1,0:T(8,128)(2,1)S(1)}, bf16[2,768,384]{2,1,0:T(8,128)(2,1)S(1)}, u32[]{:S(2)}, u32[]{:S(2)}) collective-permute-start(bf16[2,768,384]{2,1,0:T(8,128)(2,1)S(1)} %get-tuple-element.23), channel_id=1, source_target_pairs={{0,4},{4,0},{8,12},{12,8},{16,20},{20,16},{24,28},{28,24},{32,36},... | collective-permute-start | bytes 3538952 | tf_op jit(solution)/shard_map/ppermute | solution.py:18
  77.5 20.5 %collective-permute-start.8 = (bf16[768,384]{1,0:T(8,128)(2,1)S(1)}, bf16[768,384]{1,0:T(8,128)(2,1)S(1)}, u32[]{:S(2)}, u32[]{:S(2)}) collective-permute-start(bf16[768,384]{1,0:T(8,128)(2,1)S(1)} %get-tuple-element.19), channel_id=1, source_target_pairs={{16,0},{24,8},{20,4},{28,12},{32,16},{40,24},{36,20},{44,28},{48,3... | collective-permute-start | bytes 1769480 | tf_op jit(solution)/shard_map/ppermute | solution.py:18
  84.9 19.5 %collective-permute-start.9 = (bf16[768,384]{1,0:T(8,128)(2,1)S(1)}, bf16[768,384]{1,0:T(8,128)(2,1)S(1)}, u32[]{:S(2)}, u32[]{:S(2)}) collective-permute-start(bf16[768,384]{1,0:T(8,128)(2,1)S(1)} %get-tuple-element.20), channel_id=1, source_target_pairs={{0,16},{8,24},{4,20},{12,28},{16,32},{24,40},{20,36},{28,44},{32,4... | collective-permute-start | bytes 1769480 | tf_op jit(solution)/shard_map/ppermute | solution.py:18
  86.9 28.5 %collective-permute-start.12 = (bf16[768,384]{1,0:T(8,128)(2,1)S(1)}, bf16[768,384]{1,0:T(8,128)(2,1)S(1)}, u32[]{:S(2)}, u32[]{:S(2)}) collective-permute-start(bf16[768,384]{1,0:T(8,128)(2,1)S(1)} %fusion), channel_id=1, source_target_pairs={{120,112},{128,136},{124,116},{132,140},{248,240},{256,264},{252,2... | collective-permute-start | bytes 1769480 | tf_op jit(solution)/shard_map/ppermute | solution.py:18
  104.4 10.2 %collective-permute-start.10 = (bf16[384,384]{1,0:T(8,128)(2,1)S(1)}, bf16[384,384]{1,0:T(8,128)(2,1)S(1)}, u32[]{:S(2)}, u32[]{:S(2)}) collective-permute-start(bf16[384,384]{1,0:T(8,128)(2,1)S(1)} %add_convert_fusion.1), channel_id=1, source_target_pairs={{0,8},{4,12},{8,0},{12,4},{16,24},{20,28},{24,16},{28,20},{32,40},... | collective-permute-start | bytes 884744 | tf_op jit(solution)/shard_map/ppermute | solution.py:18

commit v2 on v1

v2 whole, which is shorter than its diff:
```python
import functools

import jax
import jax.numpy as jnp
from jax import lax
from jax.experimental import pallas as pl
from jax.experimental.pallas import tpu as pltpu
from jax.sharding import PartitionSpec as P

RING = 8
LOG2E = 1.4426950408889634
HEAD = 128
BF = jnp.bfloat16
F32 = jnp.float32


def send(block, pairs):
    return lax.ppermute(block, ("tm", "space"), pairs)


def routes(time_all):
    at = lambda t, c, w: t * 4 + c * 2 + w
    ts, cs = range(time_all), range(2)
    core = [(at(t, c, w), at(t, c, 1 - w)) for t in ts for c in cs for w in cs]
    pair = [(at(t, c, w), at(t, 1 - c, w)) for t in ts for c in cs for w in cs]
    up, lend, lent_core = [], [], []
    for t in range(time_all - 1):
        for w in cs:
            if t % RING == RING - 1:
                up.append((at(t, 1, w), at(t + 1, 0, w)))
                lend.append((at(t, 0, w), at(t, 1, w)))
                lend.append((at(t + 1, 1, w), at(t + 1, 0, w)))
                lent_core.append((at(t, 1, w), at(t, 1, 1 - w)))
                lent_core.append((at(t + 1, 0, w), at(t + 1, 0, 1 - w)))
            else:
                up += [(at(t, c, w), at(t + 1, c, w)) for c in cs]
    back = lambda pairs: [(j, i) for i, j in pairs]
    across = lambda pairs: [(j, i ^ 2) for i, j in pairs]
    return dict(
        core=core, pair=pair, up=up, down=back(up), lend=lend, lent_core=lent_core, give=back(lend),
        far_down=across(up), far_up=across(back(up)),
    )


def accumulate(pack, flag, count, kv, acc, dq, rows, factor):
    heads = pack.shape[1] // HEAD
    dq[...] = jnp.zeros_like(dq)
    aux = pack[2 * rows :, :].astype(F32)

    def step(j, carry):
        @pl.when(flag(j))
        def _():
            for h in range(heads):
                cols = slice(h * HEAD, (h + 1) * HEAD)
                part = lambda i: aux[(3 * i) * heads + h : (3 * i) * heads + h + 1] + (
                    aux[(3 * i + 1) * heads + h : (3 * i + 1) * heads + h + 1]
                    + aux[(3 * i + 2) * heads + h : (3 * i + 2) * heads + h + 1]
                )
                norm, delta = part(0) * LOG2E, part(1)
                q, g = pack[0:rows, cols], pack[rows : 2 * rows, cols]
                k, v = kv[j, 0:rows, cols], kv[j, rows : 2 * rows, cols]
                last = (((1,), (1,)), ((), ()))
                st = lax.dot_general(k, q, last, preferred_element_type=F32)
                p = jnp.exp2(st * (factor * LOG2E) - norm)
                dp = lax.dot_general(v, g, last, preferred_element_type=F32)
                ds = (p * (dp - delta)).astype(BF)
                acc[j, rows : 2 * rows, cols] += jnp.dot(p.astype(BF), g, preferred_element_type=F32)
                acc[j, 0:rows, cols] += jnp.dot(ds, q, preferred_element_type=F32)
                dq[:, cols] += lax.dot_general(ds, k, (((0,), (0,)), ((), ())), preferred_element_type=F32)

        return carry

    lax.fori_loop(0, count, step, 0)


def seen(extents, time_all, step, flip):
    time_pos, frame_pos = lax.axis_index("tm"), lax.axis_index("space")
    chip, core = frame_pos // 2, frame_pos % 2
    when = time_pos + step
    place = jnp.clip(when, 0, time_all - 1)
    if step == 0:
        cross, inner = jnp.bool_(False), jnp.bool_(False)
    else:
        edge = 0 if step < 0 else RING - 1
        cross, inner = time_pos % RING == edge, chip == (0 if step < 0 else 1)
    height = jnp.where(cross != bool(flip), 1 - chip, chip)
    extent = [extents[place, height * 2 + core, i] for i in range(3)]
    here = (when >= 0) & (when < time_all) & (abs(step) <= extent[0])

    def flag(j):
        key_height = jnp.where(j >= 2, 1 - chip, chip)
        taken = jnp.where(j >= 2, cross & inner, jnp.logical_not(cross) | inner)
        return here & taken & (jnp.abs(key_height - height) <= extent[1]) & (j % 2 <= extent[2])

    return flag


def frame_kernel(rows, factor, time_all, extents, mine, other, kv_a, kv_b, acc, dq_mine, dq_other, kv, dq):
    kv[0] = kv_a[...]
    kv[1] = kv_b[...]
    acc[...] = jnp.zeros_like(acc)
    accumulate(mine, seen(extents, time_all, 0, 0), 2, kv, acc, dq_mine, rows, factor)
    accumulate(other, seen(extents, time_all, 0, 1), 2, kv, acc, dq, rows, factor)
    dq_mine[...] = dq_mine[...] * factor
    dq_other[...] = (dq[...] * factor).astype(BF)


def near_kernel(rows, factor, time_all, extents, low, high, kv_a, kv_b, kv_c, kv_d, acc_in, acc, dq_low, dq_high, kv, dq):
    for i, ref in enumerate((kv_a, kv_b, kv_c, kv_d)):
        kv[i] = ref[...]
    acc[0:2] = acc_in[...]
    acc[2:4] = jnp.zeros_like(acc[2:4])
    accumulate(low, seen(extents, time_all, -1, 0), 4, kv, acc, dq, rows, factor)
    dq_low[...] = (dq[...] * factor).astype(BF)
    accumulate(high, seen(extents, time_all, 1, 0), 4, kv, acc, dq, rows, factor)
    dq_high[...] = (dq[...] * factor).astype(BF)


def far_kernel(rows, factor, time_all, extents, low, high, kv_a, kv_b, kv_c, kv_d, acc_in,
               dq_low, dq_high, own, lent, sib, kv, acc, dq):
    for i, ref in enumerate((kv_a, kv_b, kv_c, kv_d)):
        kv[i] = ref[...]
    acc[...] = acc_in[...]
    accumulate(low, seen(extents, time_all, -1, 1), 4, kv, acc, dq, rows, factor)
    dq_low[...] = (dq[...] * factor).astype(BF)
    accumulate(high, seen(extents, time_all, 1, 1), 4, kv, acc, dq, rows, factor)
    dq_high[...] = (dq[...] * factor).astype(BF)
    own[0:rows] = acc[0, 0:rows] * factor
    own[rows:] = acc[0, rows:]
    lent[0:rows] = acc[2, 0:rows] * factor
    lent[rows:] = acc[2, rows:]
    for i, j in enumerate((1, 3)):
        sib[i, 0:rows] = (acc[j, 0:rows] * factor).astype(BF)
        sib[i, rows:] = acc[j, rows:].astype(BF)


def call(kernel, shapes, scratch, operands, pairs, name):
    whole = pl.BlockSpec(memory_space=pltpu.VMEM)
    return pl.pallas_call(
        kernel,
        out_shape=shapes,
        in_specs=[pl.BlockSpec(memory_space=pltpu.SMEM)] + [whole] * (len(operands) - 1),
        out_specs=[whole] * len(shapes),
        scratch_shapes=scratch,
        compiler_params=pltpu.CompilerParams(vmem_limit_bytes=40 * 2**20),
        cost_estimate=pl.CostEstimate(flops=1000, bytes_accessed=1000, transcendentals=0),
        name=name,
    )(*operands)


def thirds(x):
    hi = lax.reduce_precision(x, 8, 7)
    mid = lax.reduce_precision(x - hi, 8, 7)
    return [hi.astype(BF), mid.astype(BF), (x - hi - mid).astype(BF)]


def body(query_tiles, key_tiles, value_tiles, grad_output, log_norm, row_delta, extents):
    rows, channels = query_tiles.shape[2:]
    heads = log_norm.shape[2]
    factor = (channels // heads) ** (-0.5)
    time_all = lax.axis_size("tm")
    route = routes(time_all)

    pad = jnp.zeros((32 - 6 * heads, channels), BF)
    mine = jnp.concatenate(
        [query_tiles[0, 0], grad_output[0, 0]] + thirds(log_norm[0, 0]) + thirds(row_delta[0, 0]) + [pad]
    )
    mine, key, value = lax.optimization_barrier((mine, key_tiles[0, 0], value_tiles[0, 0]))
    kv_a = jnp.concatenate([key, value])

    other = send(mine, route["pair"])
    near_low = send(mine, route["up"])
    near_high = send(mine, route["down"])
    kv_b = send(kv_a, route["core"])
    far_low = send(other, route["up"])
    far_high = send(other, route["down"])
    kv_c = send(lax.optimization_barrier((kv_a, kv_b, near_low, near_high))[0], route["lend"])

    tile, two = (rows, channels), (2 * rows, channels)
    out = jax.ShapeDtypeStruct
    with jax.named_scope("frame"):
        acc, dq_mine, dq_other = call(
            functools.partial(frame_kernel, rows, factor, time_all),
            [out((2,) + two, F32), out(tile, F32), out(tile, BF)],
            [pltpu.VMEM((2,) + two, BF), pltpu.VMEM(tile, F32)],
            (extents, mine, other, kv_a, kv_b), 4, "frame",
        )
    kv_c, dq_other = lax.optimization_barrier((kv_c, dq_other))
    kv_d = send(kv_c, route["lent_core"])
    with jax.named_scope("near"):
        acc, dq_low, dq_high = call(
            functools.partial(near_kernel, rows, factor, time_all),
            [out((4,) + two, F32), out(tile, BF), out(tile, BF)],
            [pltpu.VMEM((4,) + two, BF), pltpu.VMEM(tile, F32)],
            (extents, near_low, near_high, kv_a, kv_b, kv_c, kv_d, acc), 6, "near",
        )
    with jax.named_scope("far"):
        far_dq_low, far_dq_high, own, lent, sib = call(
            functools.partial(far_kernel, rows, factor, time_all),
            [out(tile, BF), out(tile, BF), out(two, F32), out(two, F32), out((2,) + two, BF)],
            [pltpu.VMEM((4,) + two, BF), pltpu.VMEM((4,) + two, F32), pltpu.VMEM(tile, F32)],
            (extents, far_low, far_high, kv_a, kv_b, kv_c, kv_d, acc), 6, "far",
        )
    parts = [
        send(dq_other, route["pair"]),
        send(dq_low, route["down"]),
        send(dq_high, route["up"]),
        send(far_dq_low, route["far_down"]),
        send(far_dq_high, route["far_up"]),
    ]
    sib = send(sib, route["core"])
    lent = (lent + sib[1].astype(F32)).astype(BF)
    given = send(lent, route["give"])
    total = dq_mine
    for part in parts:
        total = total + part.astype(F32)
    grad_kv = (own + sib[0].astype(F32) + given.astype(F32)).astype(BF)
    shape = (1, 1, rows, channels)
    return total.astype(BF).reshape(shape), grad_kv[:rows].reshape(shape), grad_kv[rows:].reshape(shape)


def solution(mesh):
    tiles, per_row = P("tm", "space", None, "heads"), P("tm", "space", "heads", None)
    return jax.shard_map(
        body,
        mesh=mesh,
        in_specs=(tiles, tiles, tiles, tiles, per_row, per_row, P()),
        out_specs=(tiles, tiles, tiles),
        check_vma=False,
    )
```

time: 117 us -> 106 us (0.906)
  the two profiles are of different devices: /device:TPU:384 before, /device:TPU:187 now
where the time goes in v2:
time: 106 us
  starting transfers between devices  51.3 us (48%)
  waiting for transfers between devices  32.7 us (31%)
  Pallas kernels  12.9 us (12%)
  local copies, waits for them, and re-layouts  6.04 us (6%)
  other arithmetic  1.99 us (2%)
    ppermute x15, starting transfers between devices, send(): return lax.ppermute(block, ('tm', 'space'), pairs)  51.3 us
    ppermute x15, waiting for transfers between devices, send(): return lax.ppermute(block, ('tm', 'space'), pairs)  32.7 us
    pallas_call x3, Pallas kernels, call(): pl.pallas_call(kernel, out_shape=shapes, in_specs=[pl.BlockSpec(memory_sp...  12.9 us
    concatenate x1, local copies, waits for them, and re-layouts, body(): jnp.concatenate([query_tiles[0, 0], grad_output[0, 0]] + thirds(log_norm[...  4.1 us
  transfers between devices with their start and end apart: 15, of which 8 were waited for; matrix products, arithmetic and copies ran while one was open for 1% of the time, Pallas kernels for 10%

profile of v2, /device:TPU:187, one launch (start us, length us, event | category | flops | bytes accessed | tf_op | source)
XLA Modules:
  0.0 105.8 jit_solution(9873969833513596432)
XLA Ops:
  0.7 0.8 fusion.4
  1.5 4.1 %concatenate.6.mine = bf16[800,384]{1,0:T(8,128)(2,1)S(1)} concatenate(bf16[384,384]{1,0:T(8,128)(2,1)} %bitcast.36, bf16[384,384]{1,0:T(8,128)(2,1)} %bitcast.37, bf16[3,384]{1,0:T(4,128)(2,1)S(1)} %get-tuple-element.44, bf16[3,384]{1,0:T(4,128)(2,1)S(1)} %get-tuple-element.43, bf16[3,384]{1,0:T(4,128)(2,1)S(1)} %get-tuple-element.42, bf16[3,384]{1,0:T(4,128)(2,1)S(1)} %get-tuple-element.45, ...), dimensions={0} | concatenate | bytes 1228800 | tf_op jit(solution)/shard_map/concatenate | solution.py:165
  5.6 3.0 %collective-permute-start.3 = (bf16[800,384]{1,0:T(8,128)(2,1)S(1)}, bf16[800,384]{1,0:T(8,128)(2,1)S(1)}, u32[]{:S(2)}, u32[]{:S(2)}) collective-permute-start(bf16[800,384]{1,0:T(8,128)(2,1)S(1)} %concatenate.6.mine), channel_id=1, source_target_pairs={{16,0},{24,8},{20,4},{28,12},{32,16},{40,24},{36,20},{44,28},{48,3... | collective-permute-start | bytes 1843208 | tf_op jit(solution)/shard_map/ppermute | solution.py:18
  8.6 1.3 %collective-permute-start.2 = (bf16[800,384]{1,0:T(8,128)(2,1)S(1)}, bf16[800,384]{1,0:T(8,128)(2,1)S(1)}, u32[]{:S(2)}, u32[]{:S(2)}) collective-permute-start(bf16[800,384]{1,0:T(8,128)(2,1)S(1)} %concatenate.6.mine), channel_id=1, source_target_pairs={{0,16},{8,24},{4,20},{12,28},{16,32},{24,40},{20,36},{28,44},{32,4... | collective-permute-start | bytes 1843208 | tf_op jit(solution)/shard_map/ppermute | solution.py:18
  10.0 2.9 %collective-permute-start.1 = (bf16[768,384]{1,0:T(8,128)(2,1)S(1)}, bf16[768,384]{1,0:T(8,128)(2,1)S(1)}, u32[]{:S(2)}, u32[]{:S(2)}) collective-permute-start(bf16[768,384]{1,0:T(8,128)(2,1)S(1)} %constant_dynamic-update-slice_fusion.kv_a), channel_id=1, source_target_pairs={{0,4},{4,0},{8,12},{12,8},{16,20},{20,16},{24,28},{28,24},{32,36},... | collective-permute-start | bytes 1769480 | tf_op jit(solution)/shard_map/ppermute | solution.py:18
  12.9 8.6 %collective-permute-start = (bf16[800,384]{1,0:T(8,128)(2,1)S(1)}, bf16[800,384]{1,0:T(8,128)(2,1)}, u32[]{:S(2)}, u32[]{:S(2)}) collective-permute-start(bf16[800,384]{1,0:T(8,128)(2,1)S(1)} %concatenate.6.mine), channel_id=1, source_target_pairs={{0,8},{4,12},{8,0},{12,4},{16,24},{20,28},{24,16},{28,20},{32,40},... | collective-permute-start | bytes 1843208 | tf_op jit(solution)/shard_map/ppermute | solution.py:18
  21.5 3.5 %collective-permute-done.2.low = bf16[800,384]{1,0:T(8,128)(2,1)S(1)} collective-permute-done((bf16[800,384]{1,0:T(8,128)(2,1)S(1)}, bf16[800,384]{1,0:T(8,128)(2,1)S(1)}, u32[]{:S(2)}, u32[]{:S(2)}) %collective-permute-start.2) | collective-permute-done | bytes 614432 | tf_op jit(solution)/shard_map/ppermute | solution.py:18
  25.0 0.9 copy-done
  25.8 5.4 %collective-permute-start.4 = (bf16[768,384]{1,0:T(8,128)(2,1)S(1)}, bf16[768,384]{1,0:T(8,128)(2,1)S(1)}, u32[]{:S(2)}, u32[]{:S(2)}) collective-permute-start(bf16[768,384]{1,0:T(8,128)(2,1)S(1)} %constant_dynamic-update-slice_fusion.kv_a), channel_id=1, source_target_pairs={{112,120},{136,128},{116,124},{140,132},{240,248},{264,256},{244,2... | collective-permute-start | bytes 1769480 | tf_op jit(solution)/shard_map/ppermute | solution.py:18
  31.2 4.5 %collective-permute-done.other = bf16[800,384]{1,0:T(8,128)(2,1)} collective-permute-done((bf16[800,384]{1,0:T(8,128)(2,1)S(1)}, bf16[800,384]{1,0:T(8,128)(2,1)}, u32[]{:S(2)}, u32[]{:S(2)}) %collective-permute-start) | collective-permute-done | bytes 614432 | tf_op jit(solution)/shard_map/ppermute | solution.py:18
  35.8 2.1 %collective-permute-start.10 = (bf16[800,384]{1,0:T(8,128)(2,1)}, bf16[800,384]{1,0:T(8,128)(2,1)}, u32[]{:S(2)}, u32[]{:S(2)}) collective-permute-start(bf16[800,384]{1,0:T(8,128)(2,1)} %collective-permute-done.other), channel_id=1, source_target_pairs={{16,0},{24,8},{20,4},{28,12},{32,16},{40,24},{36,20},{44,28},{48,3... | collective-permute-start | bytes 1843208 | tf_op jit(solution)/shard_map/ppermute | solution.py:18
  37.9 1.3 %collective-permute-start.9 = (bf16[800,384]{1,0:T(8,128)(2,1)}, bf16[800,384]{1,0:T(8,128)(2,1)}, u32[]{:S(2)}, u32[]{:S(2)}) collective-permute-start(bf16[800,384]{1,0:T(8,128)(2,1)} %collective-permute-done.other), channel_id=1, source_target_pairs={{0,16},{8,24},{4,20},{12,28},{16,32},{24,40},{20,36},{28,44},{32,4... | collective-permute-start | bytes 1843208 | tf_op jit(solution)/shard_map/ppermute | solution.py:18
  39.3 4.9 %frame.1 = (f32[2,768,384]{2,1,0:T(8,128)S(1)}, f32[384,384]{1,0:T(8,128)S(1)}, bf16[384,384]{1,0:T(8,128)(2,1)S(1)}) custom-call(s32[32,4,3]{2,1,0:T(4,128)S(1)} %copy.10.extents, bf16[800,384]{1,0:T(8,128)(2,1)S(1)} %concatenate.6.mine, bf16[800,384]{1,0:T(8,128)(2,1)} %collective-permute-done.other, ...), custom_call_target="tpu_custom_call" | custom-call | flops 1000 | bytes 1000 | tf_op jit(solution)/shard_map/frame/frame/pallas_call | solution.py:139
  44.2 3.2 %collective-permute-done.4.kv_c = bf16[768,384]{1,0:T(8,128)(2,1)S(1)} collective-permute-done((bf16[768,384]{1,0:T(8,128)(2,1)S(1)}, bf16[768,384]{1,0:T(8,128)(2,1)S(1)}, u32[]{:S(2)}, u32[]{:S(2)}) %collective-permute-start.4) | collective-permute-done | bytes 589856 | tf_op jit(solution)/shard_map/ppermute | solution.py:18
  47.3 0.7 collective-permute-start.6
  48.1 5.2 %near.1 = (f32[4,768,384]{2,1,0:T(8,128)S(1)}, bf16[384,384]{1,0:T(8,128)(2,1)S(1)}, bf16[384,384]{1,0:T(8,128)(2,1)S(1)}) custom-call(s32[32,4,3]{2,1,0:T(4,128)S(1)} %copy.10.extents, bf16[800,384]{1,0:T(8,128)(2,1)S(1)} %copy-done.1, bf16[800,384]{1,0:T(8,128)(2,1)S(1)} %collective-permute-done.3.high, ...), custom_call_target="tpu_custom_call" | custom-call | flops 1000 | bytes 1000 | tf_op jit(solution)/shard_map/near/near/pallas_call | solution.py:139
  53.3 1.6 %collective-permute-done.9.low = bf16[800,384]{1,0:T(8,128)(2,1)} collective-permute-done((bf16[800,384]{1,0:T(8,128)(2,1)}, bf16[800,384]{1,0:T(8,128)(2,1)}, u32[]{:S(2)}, u32[]{:S(2)}) %collective-permute-start.9) | collective-permute-done | bytes 614432 | tf_op jit(solution)/shard_map/ppermute | solution.py:18
  54.9 2.8 %far.1 = (bf16[384,384]{1,0:T(8,128)(2,1)S(1)}, bf16[384,384]{1,0:T(8,128)(2,1)S(1)}, f32[768,384]{1,0:T(8,128)S(1)}, f32[768,384]{1,0:T(8,128)S(1)}, bf16[2,768,384]{2,1,0:T(8,128)(2,1)S(1)}) custom-call(s32[32,4,3]{2,1,0:T(4,128)S(1)} %copy.10.extents, bf16[800,384]{1,0:T(8,128)(2,1)} %collective-permute-done.9.low, ...), custom_call_target="tpu_custom_call" | custom-call | flops 1000 | bytes 1000 | tf_op jit(solution)/shard_map/far/far/pallas_call | solution.py:139
  57.7 3.4 %collective-permute-start.13 = (bf16[2,768,384]{2,1,0:T(8,128)(2,1)S(1)}, bf16[2,768,384]{2,1,0:T(8,128)(2,1)S(1)}, u32[]{:S(2)}, u32[]{:S(2)}) collective-permute-start(bf16[2,768,384]{2,1,0:T(8,128)(2,1)S(1)} %get-tuple-element.35), channel_id=1, source_target_pairs={{0,4},{4,0},{8,12},{12,8},{16,20},{20,16},{24,28},{28,24},{32,36},... | collective-permute-start | bytes 3538952 | tf_op jit(solution)/shard_map/ppermute | solution.py:18
  61.0 11.1 %collective-permute-start.5 = (bf16[384,384]{1,0:T(8,128)(2,1)S(1)}, bf16[384,384]{1,0:T(8,128)(2,1)S(1)}, u32[]{:S(2)}, u32[]{:S(2)}) collective-permute-start(bf16[384,384]{1,0:T(8,128)(2,1)S(1)} %get-tuple-element.26), channel_id=1, source_target_pairs={{0,8},{4,12},{8,0},{12,4},{16,24},{20,28},{24,16},{28,20},{32,40},... | collective-permute-start | bytes 884744 | tf_op jit(solution)/shard_map/ppermute | solution.py:18
  72.3 1.3 %collective-permute-start.14 = (bf16[768,384]{1,0:T(8,128)(2,1)S(1)}, bf16[768,384]{1,0:T(8,128)(2,1)S(1)}, u32[]{:S(2)}, u32[]{:S(2)}) collective-permute-start(bf16[768,384]{1,0:T(8,128)(2,1)S(1)} %fusion), channel_id=1, source_target_pairs={{120,112},{128,136},{124,116},{132,140},{248,240},{256,264},{252,2... | collective-permute-start | bytes 1769480 | tf_op jit(solution)/shard_map/ppermute | solution.py:18
  73.6 1.3 %collective-permute-start.7 = (bf16[384,384]{1,0:T(8,128)(2,1)S(1)}, bf16[384,384]{1,0:T(8,128)(2,1)S(1)}, u32[]{:S(2)}, u32[]{:S(2)}) collective-permute-start(bf16[384,384]{1,0:T(8,128)(2,1)S(1)} %get-tuple-element.29), channel_id=1, source_target_pairs={{16,0},{24,8},{20,4},{28,12},{32,16},{40,24},{36,20},{44,28},{48,3... | collective-permute-start | bytes 884744 | tf_op jit(solution)/shard_map/ppermute | solution.py:18
  74.9 1.3 %collective-permute-start.8 = (bf16[384,384]{1,0:T(8,128)(2,1)S(1)}, bf16[384,384]{1,0:T(8,128)(2,1)S(1)}, u32[]{:S(2)}, u32[]{:S(2)}) collective-permute-start(bf16[384,384]{1,0:T(8,128)(2,1)S(1)} %get-tuple-element.30), channel_id=1, source_target_pairs={{0,16},{8,24},{4,20},{12,28},{16,32},{24,40},{20,36},{28,44},{32,4... | collective-permute-start | bytes 884744 | tf_op jit(solution)/shard_map/ppermute | solution.py:18
  76.2 6.4 %collective-permute-start.11 = (bf16[384,384]{1,0:T(8,128)(2,1)S(1)}, bf16[384,384]{1,0:T(8,128)(2,1)S(1)}, u32[]{:S(2)}, u32[]{:S(2)}) collective-permute-start(bf16[384,384]{1,0:T(8,128)(2,1)S(1)} %get-tuple-element.32), channel_id=1, source_target_pairs={{16,8},{24,0},{20,12},{28,4},{32,24},{40,16},{36,28},{44,20},{48,4... | collective-permute-start | bytes 884744 | tf_op jit(solution)/shard_map/ppermute | solution.py:18
  82.6 1.3 %collective-permute-start.12 = (bf16[384,384]{1,0:T(8,128)(2,1)S(1)}, bf16[384,384]{1,0:T(8,128)(2,1)S(1)}, u32[]{:S(2)}, u32[]{:S(2)}) collective-permute-start(bf16[384,384]{1,0:T(8,128)(2,1)S(1)} %get-tuple-element.33), channel_id=1, source_target_pairs={{0,24},{8,16},{4,28},{12,20},{16,40},{24,32},{20,44},{28,36},{32,5... | collective-permute-start | bytes 884744 | tf_op jit(solution)/shard_map/ppermute | solution.py:18
  83.9 1.1 %collective-permute-done.8 = bf16[384,384]{1,0:T(8,128)(2,1)S(1)} collective-permute-done((bf16[384,384]{1,0:T(8,128)(2,1)S(1)}, bf16[384,384]{1,0:T(8,128)(2,1)S(1)}, u32[]{:S(2)}, u32[]{:S(2)}) %collective-permute-start.8) | collective-permute-done | bytes 294944 | tf_op jit(solution)/shard_map/ppermute | solution.py:18
  85.1 12.6 %collective-permute-done.11 = bf16[384,384]{1,0:T(8,128)(2,1)S(1)} collective-permute-done((bf16[384,384]{1,0:T(8,128)(2,1)S(1)}, bf16[384,384]{1,0:T(8,128)(2,1)S(1)}, u32[]{:S(2)}, u32[]{:S(2)}) %collective-permute-start.11) | collective-permute-done | bytes 294944 | tf_op jit(solution)/shard_map/ppermute | solution.py:18
  97.7 1.4 %collective-permute-done.12 = bf16[384,384]{1,0:T(8,128)(2,1)S(1)} collective-permute-done((bf16[384,384]{1,0:T(8,128)(2,1)S(1)}, bf16[384,384]{1,0:T(8,128)(2,1)S(1)}, u32[]{:S(2)}, u32[]{:S(2)}) %collective-permute-start.12) | collective-permute-done | bytes 294944 | tf_op jit(solution)/shard_map/ppermute | solution.py:18
  99.1 0.9 fusion.3
  100.1 4.7 %collective-permute-done.14 = bf16[768,384]{1,0:T(8,128)(2,1)S(1)} collective-permute-done((bf16[768,384]{1,0:T(8,128)(2,1)S(1)}, bf16[768,384]{1,0:T(8,128)(2,1)S(1)}, u32[]{:S(2)}, u32[]{:S(2)}) %collective-permute-start.14) | collective-permute-done | bytes 589856 | tf_op jit(solution)/shard_map/ppermute | solution.py:18
  104.8 0.2 fusion.2
  105.0 0.9 slice_bitcast_fusion.2
  (21 shorter events, 0.4 us)
Async XLA Ops:
  0.6 9.3 %copy-start.3 = (bf16[1,1,384,384]{3,2,1,0:T(8,128)(2,1)S(1)}, bf16[1,1,384,384]{3,2,1,0:T(8,128)(2,1)}, u32[]{:S(2)}) copy-start(bf16[1,1,384,384]{3,2,1,0:T(8,128)(2,1)} %param.9) | copy-start | bytes 884740
  0.6 9.2 %copy-start.2 = (bf16[1,1,384,384]{3,2,1,0:T(8,128)(2,1)S(1)}, bf16[1,1,384,384]{3,2,1,0:T(8,128)(2,1)}, u32[]{:S(2)}) copy-start(bf16[1,1,384,384]{3,2,1,0:T(8,128)(2,1)} %param.8) | copy-start | bytes 884740
  1.4 37.7 %copy-start.4 = (s32[32,4,3]{0,1,2:T(4,128)S(1)}, s32[32,4,3]{0,1,2:T(4,128)}, u32[]{:S(2)}) copy-start(s32[32,4,3]{0,1,2:T(4,128)} %param.13) | copy-start | bytes 4612
  5.6 15.9 %collective-permute-start.3 = (bf16[800,384]{1,0:T(8,128)(2,1)S(1)}, bf16[800,384]{1,0:T(8,128)(2,1)S(1)}, u32[]{:S(2)}, u32[]{:S(2)}) collective-permute-start(bf16[800,384]{1,0:T(8,128)(2,1)S(1)} %concatenate.6.mine), channel_id=1, source_target_pairs={{16,0},{24,8},{20,4},{28,12},{32,16},{40,24},{36,20},{44,28},{48,3... | collective-permute-start | bytes 1843208 | tf_op jit(solution)/shard_map/ppermute | solution.py:18
  8.6 16.4 %collective-permute-start.2 = (bf16[800,384]{1,0:T(8,128)(2,1)S(1)}, bf16[800,384]{1,0:T(8,128)(2,1)S(1)}, u32[]{:S(2)}, u32[]{:S(2)}) collective-permute-start(bf16[800,384]{1,0:T(8,128)(2,1)S(1)} %concatenate.6.mine), channel_id=1, source_target_pairs={{0,16},{8,24},{4,20},{12,28},{16,32},{24,40},{20,36},{28,44},{32,4... | collective-permute-start | bytes 1843208 | tf_op jit(solution)/shard_map/ppermute | solution.py:18
  10.0 11.5 %collective-permute-start.1 = (bf16[768,384]{1,0:T(8,128)(2,1)S(1)}, bf16[768,384]{1,0:T(8,128)(2,1)S(1)}, u32[]{:S(2)}, u32[]{:S(2)}) collective-permute-start(bf16[768,384]{1,0:T(8,128)(2,1)S(1)} %constant_dynamic-update-slice_fusion.kv_a), channel_id=1, source_target_pairs={{0,4},{4,0},{8,12},{12,8},{16,20},{20,16},{24,28},{28,24},{32,36},... | collective-permute-start | bytes 1769480 | tf_op jit(solution)/shard_map/ppermute | solution.py:18
  12.9 22.9 %collective-permute-start = (bf16[800,384]{1,0:T(8,128)(2,1)S(1)}, bf16[800,384]{1,0:T(8,128)(2,1)}, u32[]{:S(2)}, u32[]{:S(2)}) collective-permute-start(bf16[800,384]{1,0:T(8,128)(2,1)S(1)} %concatenate.6.mine), channel_id=1, source_target_pairs={{0,8},{4,12},{8,0},{12,4},{16,24},{20,28},{24,16},{28,20},{32,40},... | collective-permute-start | bytes 1843208 | tf_op jit(solution)/shard_map/ppermute | solution.py:18
  25.0 0.9 copy-start
  25.8 21.5 %collective-permute-start.4 = (bf16[768,384]{1,0:T(8,128)(2,1)S(1)}, bf16[768,384]{1,0:T(8,128)(2,1)S(1)}, u32[]{:S(2)}, u32[]{:S(2)}) collective-permute-start(bf16[768,384]{1,0:T(8,128)(2,1)S(1)} %constant_dynamic-update-slice_fusion.kv_a), channel_id=1, source_target_pairs={{112,120},{136,128},{116,124},{140,132},{240,248},{264,256},{244,2... | collective-permute-start | bytes 1769480 | tf_op jit(solution)/shard_map/ppermute | solution.py:18
  35.8 17.5 %collective-permute-start.10 = (bf16[800,384]{1,0:T(8,128)(2,1)}, bf16[800,384]{1,0:T(8,128)(2,1)}, u32[]{:S(2)}, u32[]{:S(2)}) collective-permute-start(bf16[800,384]{1,0:T(8,128)(2,1)} %collective-permute-done.other), channel_id=1, source_target_pairs={{16,0},{24,8},{20,4},{28,12},{32,16},{40,24},{36,20},{44,28},{48,3... | collective-permute-start | bytes 1843208 | tf_op jit(solution)/shard_map/ppermute | solution.py:18
  37.9 17.0 %collective-permute-start.9 = (bf16[800,384]{1,0:T(8,128)(2,1)}, bf16[800,384]{1,0:T(8,128)(2,1)}, u32[]{:S(2)}, u32[]{:S(2)}) collective-permute-start(bf16[800,384]{1,0:T(8,128)(2,1)} %collective-permute-done.other), channel_id=1, source_target_pairs={{0,16},{8,24},{4,20},{12,28},{16,32},{24,40},{20,36},{28,44},{32,4... | collective-permute-start | bytes 1843208 | tf_op jit(solution)/shard_map/ppermute | solution.py:18
  39.3 8.8 %copy-start.1 = (bf16[800,384]{1,0:T(8,128)(2,1)S(1)}, bf16[800,384]{1,0:T(8,128)(2,1)}, u32[]{:S(2)}) copy-start(bf16[800,384]{1,0:T(8,128)(2,1)} %copy-done) | copy-start | bytes 1843204
  47.3 0.7 collective-permute-start.6
  57.7 14.5 %collective-permute-start.13 = (bf16[2,768,384]{2,1,0:T(8,128)(2,1)S(1)}, bf16[2,768,384]{2,1,0:T(8,128)(2,1)S(1)}, u32[]{:S(2)}, u32[]{:S(2)}) collective-permute-start(bf16[2,768,384]{2,1,0:T(8,128)(2,1)S(1)} %get-tuple-element.35), channel_id=1, source_target_pairs={{0,4},{4,0},{8,12},{12,8},{16,20},{20,16},{24,28},{28,24},{32,36},... | collective-permute-start | bytes 3538952 | tf_op jit(solution)/shard_map/ppermute | solution.py:18
  61.0 21.6 %collective-permute-start.5 = (bf16[384,384]{1,0:T(8,128)(2,1)S(1)}, bf16[384,384]{1,0:T(8,128)(2,1)S(1)}, u32[]{:S(2)}, u32[]{:S(2)}) collective-permute-start(bf16[384,384]{1,0:T(8,128)(2,1)S(1)} %get-tuple-element.26), channel_id=1, source_target_pairs={{0,8},{4,12},{8,0},{12,4},{16,24},{20,28},{24,16},{28,20},{32,40},... | collective-permute-start | bytes 884744 | tf_op jit(solution)/shard_map/ppermute | solution.py:18
  72.3 32.5 %collective-permute-start.14 = (bf16[768,384]{1,0:T(8,128)(2,1)S(1)}, bf16[768,384]{1,0:T(8,128)(2,1)S(1)}, u32[]{:S(2)}, u32[]{:S(2)}) collective-permute-start(bf16[768,384]{1,0:T(8,128)(2,1)S(1)} %fusion), channel_id=1, source_target_pairs={{120,112},{128,136},{124,116},{132,140},{248,240},{256,264},{252,2... | collective-permute-start | bytes 1769480 | tf_op jit(solution)/shard_map/ppermute | solution.py:18
  73.6 10.4 %collective-permute-start.7 = (bf16[384,384]{1,0:T(8,128)(2,1)S(1)}, bf16[384,384]{1,0:T(8,128)(2,1)S(1)}, u32[]{:S(2)}, u32[]{:S(2)}) collective-permute-start(bf16[384,384]{1,0:T(8,128)(2,1)S(1)} %get-tuple-element.29), channel_id=1, source_target_pairs={{16,0},{24,8},{20,4},{28,12},{32,16},{40,24},{36,20},{44,28},{48,3... | collective-permute-start | bytes 884744 | tf_op jit(solution)/shard_map/ppermute | solution.py:18
  74.9 10.2 %collective-permute-start.8 = (bf16[384,384]{1,0:T(8,128)(2,1)S(1)}, bf16[384,384]{1,0:T(8,128)(2,1)S(1)}, u32[]{:S(2)}, u32[]{:S(2)}) collective-permute-start(bf16[384,384]{1,0:T(8,128)(2,1)S(1)} %get-tuple-element.30), channel_id=1, source_target_pairs={{0,16},{8,24},{4,20},{12,28},{16,32},{24,40},{20,36},{28,44},{32,4... | collective-permute-start | bytes 884744 | tf_op jit(solution)/shard_map/ppermute | solution.py:18
  76.2 21.5 %collective-permute-start.11 = (bf16[384,384]{1,0:T(8,128)(2,1)S(1)}, bf16[384,384]{1,0:T(8,128)(2,1)S(1)}, u32[]{:S(2)}, u32[]{:S(2)}) collective-permute-start(bf16[384,384]{1,0:T(8,128)(2,1)S(1)} %get-tuple-element.32), channel_id=1, source_target_pairs={{16,8},{24,0},{20,12},{28,4},{32,24},{40,16},{36,28},{44,20},{48,4... | collective-permute-start | bytes 884744 | tf_op jit(solution)/shard_map/ppermute | solution.py:18
  82.6 16.5 %collective-permute-start.12 = (bf16[384,384]{1,0:T(8,128)(2,1)S(1)}, bf16[384,384]{1,0:T(8,128)(2,1)S(1)}, u32[]{:S(2)}, u32[]{:S(2)}) collective-permute-start(bf16[384,384]{1,0:T(8,128)(2,1)S(1)} %get-tuple-element.33), channel_id=1, source_target_pairs={{0,24},{8,16},{4,28},{12,20},{16,40},{24,32},{20,44},{28,36},{32,5... | collective-permute-start | bytes 884744 | tf_op jit(solution)/shard_map/ppermute | solution.py:18

commit v3 on v2

--- a/solution.py
+++ b/solution.py
@@ -95,21 +95,49 @@
     return flag
 
 
-def frame_kernel(rows, factor, time_all, extents, mine, other, kv_a, kv_b, acc, dq_mine, dq_other, kv, dq):
+def pack_kernel(rows, query, grad, norm, delta, out, sems):
+    copies = [pltpu.make_async_copy(r, out.at[pl.ds(i * rows, rows)], sems.at[i]) for i, r in enumerate((query, grad))]
+    for copy in copies:
+        copy.start()
+    pieces = []
+    for x in (norm[...], delta[...]):
+        high = x.astype(BF)
+        rest = x - high.astype(F32)
+        mid = rest.astype(BF)
+        pieces += [high.astype(F32), mid.astype(F32), rest - mid.astype(F32)]
+    heads, channels = norm.shape
+    pieces.append(jnp.zeros((32 - 6 * heads, channels), F32))
+    out[2 * rows :] = jnp.concatenate(pieces).astype(BF)
+    for copy in copies:
+        copy.wait()
+
+
+def stack_kernel(rows, key, value, out, sems):
+    copies = [pltpu.make_async_copy(r, out.at[pl.ds(i * rows, rows)], sems.at[i]) for i, r in enumerate((key, value))]
+    for copy in copies:
+        copy.start()
+    for copy in copies:
+        copy.wait()
+
+
+def own_kernel(rows, factor, time_all, extents, mine, kv_a, kv_b, acc, dq_mine, kv):
     kv[0] = kv_a[...]
     kv[1] = kv_b[...]
     acc[...] = jnp.zeros_like(acc)
     accumulate(mine, seen(extents, time_all, 0, 0), 2, kv, acc, dq_mine, rows, factor)
+    dq_mine[...] = dq_mine[...] * factor
+
+
+def pair_kernel(rows, factor, time_all, extents, other, kv_a, kv_b, acc_in, acc, dq_other, kv, dq):
+    kv[0] = kv_a[...]
+    kv[1] = kv_b[...]
     accumulate(other, seen(extents, time_all, 0, 1), 2, kv, acc, dq, rows, factor)
-    dq_mine[...] = dq_mine[...] * factor
     dq_other[...] = (dq[...] * factor).astype(BF)
 
 
 def near_kernel(rows, factor, time_all, extents, low, high, kv_a, kv_b, kv_c, kv_d, acc_in, acc, dq_low, dq_high, kv, dq):
     for i, ref in enumerate((kv_a, kv_b, kv_c, kv_d)):
         kv[i] = ref[...]
-    acc[0:2] = acc_in[...]
-    acc[2:4] = jnp.zeros_like(acc[2:4])
     accumulate(low, seen(extents, time_all, -1, 0), 4, kv, acc, dq, rows, factor)
     dq_low[...] = (dq[...] * factor).astype(BF)
     accumulate(high, seen(extents, time_all, 1, 0), 4, kv, acc, dq, rows, factor)
@@ -117,10 +145,10 @@
 
 
 def far_kernel(rows, factor, time_all, extents, low, high, kv_a, kv_b, kv_c, kv_d, acc_in,
-               dq_low, dq_high, own, lent, sib, kv, acc, dq):
+               dq_low, dq_high, own, lent, sib, kv, dq):
     for i, ref in enumerate((kv_a, kv_b, kv_c, kv_d)):
         kv[i] = ref[...]
-    acc[...] = acc_in[...]
+    acc = acc_in
     accumulate(low, seen(extents, time_all, -1, 1), 4, kv, acc, dq, rows, factor)
     dq_low[...] = (dq[...] * factor).astype(BF)
     accumulate(high, seen(extents, time_all, 1, 1), 4, kv, acc, dq, rows, factor)
@@ -134,7 +162,7 @@
         sib[i, rows:] = acc[j, rows:].astype(BF)
 
 
-def call(kernel, shapes, scratch, operands, pairs, name):
+def call(kernel, shapes, scratch, operands, micros, name, aliases=None):
     whole = pl.BlockSpec(memory_space=pltpu.VMEM)
     return pl.pallas_call(
         kernel,
@@ -142,16 +170,24 @@
         in_specs=[pl.BlockSpec(memory_space=pltpu.SMEM)] + [whole] * (len(operands) - 1),
         out_specs=[whole] * len(shapes),
         scratch_shapes=scratch,
+        input_output_aliases=aliases or {},
         compiler_params=pltpu.CompilerParams(vmem_limit_bytes=40 * 2**20),
-        cost_estimate=pl.CostEstimate(flops=1000, bytes_accessed=1000, transcendentals=0),
+        cost_estimate=pl.CostEstimate(flops=micros * 10**9 + 1000, bytes_accessed=1000, transcendentals=0),
         name=name,
     )(*operands)
 
 
-def thirds(x):
-    hi = lax.reduce_precision(x, 8, 7)
-    mid = lax.reduce_precision(x - hi, 8, 7)
-    return [hi.astype(BF), mid.astype(BF), (x - hi - mid).astype(BF)]
+def gathered(kernel, shape, blocks, rows, name):
+    hbm, vmem = pl.BlockSpec(memory_space=pltpu.HBM), pl.BlockSpec(memory_space=pltpu.VMEM)
+    return pl.pallas_call(
+        functools.partial(kernel, rows),
+        out_shape=shape,
+        in_specs=[hbm] * 2 + [vmem] * (len(blocks) - 2),
+        out_specs=vmem,
+        scratch_shapes=[pltpu.SemaphoreType.DMA((2,))],
+        cost_estimate=pl.CostEstimate(flops=10**9, bytes_accessed=1000, transcendentals=0),
+        name=name,
+    )(*blocks)
 
 
 def body(query_tiles, key_tiles, value_tiles, grad_output, log_norm, row_delta, extents):
@@ -161,29 +197,37 @@
     time_all = lax.axis_size("tm")
     route = routes(time_all)
 
-    pad = jnp.zeros((32 - 6 * heads, channels), BF)
-    mine = jnp.concatenate(
-        [query_tiles[0, 0], grad_output[0, 0]] + thirds(log_norm[0, 0]) + thirds(row_delta[0, 0]) + [pad]
+    out = jax.ShapeDtypeStruct
+    tile, two = (rows, channels), (2 * rows, channels)
+    mine = gathered(
+        pack_kernel, out((2 * rows + 32, channels), BF),
+        (query_tiles[0, 0], grad_output[0, 0], log_norm[0, 0], row_delta[0, 0]), rows, "pack",
     )
+    other = send(mine, route["pair"])
     mine, key, value = lax.optimization_barrier((mine, key_tiles[0, 0], value_tiles[0, 0]))
-    kv_a = jnp.concatenate([key, value])
-
-    other = send(mine, route["pair"])
+    kv_a = gathered(stack_kernel, out(two, BF), (key, value), rows, "stack")
+    mine, kv_a = lax.optimization_barrier((mine, kv_a))
+    kv_b = send(kv_a, route["core"])
     near_low = send(mine, route["up"])
     near_high = send(mine, route["down"])
-    kv_b = send(kv_a, route["core"])
     far_low = send(other, route["up"])
     far_high = send(other, route["down"])
-    kv_c = send(lax.optimization_barrier((kv_a, kv_b, near_low, near_high))[0], route["lend"])
-
-    tile, two = (rows, channels), (2 * rows, channels)
-    out = jax.ShapeDtypeStruct
-    with jax.named_scope("frame"):
-        acc, dq_mine, dq_other = call(
-            functools.partial(frame_kernel, rows, factor, time_all),
-            [out((2,) + two, F32), out(tile, F32), out(tile, BF)],
+
+    with jax.named_scope("own"):
+        acc, dq_mine = call(
+            functools.partial(own_kernel, rows, factor, time_all),
+            [out((4,) + two, F32), out(tile, F32)],
+            [pltpu.VMEM((2,) + two, BF)],
+            (extents, mine, kv_a, kv_b), 0, "own",
+        )
+    kv_a, dq_mine, *_ = lax.optimization_barrier((kv_a, dq_mine, near_low, near_high, other))
+    kv_c = send(kv_a, route["lend"])
+    with jax.named_scope("other"):
+        acc, dq_other = call(
+            functools.partial(pair_kernel, rows, factor, time_all),
+            [out((4,) + two, F32), out(tile, BF)],
             [pltpu.VMEM((2,) + two, BF), pltpu.VMEM(tile, F32)],
-            (extents, mine, other, kv_a, kv_b), 4, "frame",
+            (extents, other, kv_a, kv_b, acc), 0, "other", {4: 0},
         )
     kv_c, dq_other = lax.optimization_barrier((kv_c, dq_other))
     kv_d = send(kv_c, route["lent_core"])
@@ -192,27 +236,23 @@
             functools.partial(near_kernel, rows, factor, time_all),
             [out((4,) + two, F32), out(tile, BF), out(tile, BF)],
             [pltpu.VMEM((4,) + two, BF), pltpu.VMEM(tile, F32)],
-            (extents, near_low, near_high, kv_a, kv_b, kv_c, kv_d, acc), 6, "near",
+            (extents, near_low, near_high, kv_a, kv_b, kv_c, kv_d, acc), 0, "near", {7: 0},
         )
     with jax.named_scope("far"):
         far_dq_low, far_dq_high, own, lent, sib = call(
             functools.partial(far_kernel, rows, factor, time_all),
             [out(tile, BF), out(tile, BF), out(two, F32), out(two, F32), out((2,) + two, BF)],
-            [pltpu.VMEM((4,) + two, BF), pltpu.VMEM((4,) + two, F32), pltpu.VMEM(tile, F32)],
-            (extents, far_low, far_high, kv_a, kv_b, kv_c, kv_d, acc), 6, "far",
-        )
-    parts = [
-        send(dq_other, route["pair"]),
-        send(dq_low, route["down"]),
-        send(dq_high, route["up"]),
-        send(far_dq_low, route["far_down"]),
-        send(far_dq_high, route["far_up"]),
-    ]
+            [pltpu.VMEM((4,) + two, BF), pltpu.VMEM(tile, F32)],
+            (extents, far_low, far_high, kv_a, kv_b, kv_c, kv_d, acc), 20, "far",
+        )
+    early = [send(dq_other, route["pair"]), send(dq_low, route["down"]), send(dq_high, route["up"])]
+    late = [send(far_dq_low, route["far_down"]), send(far_dq_high, route["far_up"])]
+    sib, *early = lax.optimization_barrier((sib, *early))
     sib = send(sib, route["core"])
     lent = (lent + sib[1].astype(F32)).astype(BF)
     given = send(lent, route["give"])
     total = dq_mine
-    for part in parts:
+    for part in early + late:
         total = total + part.astype(F32)
     grad_kv = (own + sib[0].astype(F32) + given.astype(F32)).astype(BF)
     shape = (1, 1, rows, channels)

time: 106 us -> 113 us (1.066)
  Pallas kernels: 12.9 us -> 18.7 us
  waiting for transfers between devices: 32.7 us -> 37.9 us
  local copies, waits for them, and re-layouts: 6.04 us -> 2.3 us
    ppermute x15, waiting for transfers between devices: 32.7 us -> 37.9 us  [send(): return lax.ppermute(block, ('tm', 'space'), pairs)]
    pallas_call x0 -> x2, Pallas kernels: none -> 4.57 us  [gathered(): pl.pallas_call(functools.partial(kernel, rows), out_shape=shape, in_specs...]
    concatenate x2 -> x0, local copies, waits for them, and re-layouts: 4.15 us -> none  [the longest x1 4.1 us: body(): jnp.concatenate([query_tiles[0, 0], grad_output[0, 0]] + thirds(log_norm[...]
    pallas_call x3 -> x4, Pallas kernels: 12.9 us -> 14.1 us  [call(): pl.pallas_call(kernel, out_shape=shapes, in_specs=[pl.BlockSpec(memory_sp...]
  transfers between devices with their start and end apart: 15 -> 15, of which waited for: 8 -> 8; matrix products, arithmetic and copies ran while one was open for 1% -> 1% of each run, Pallas kernels for 10% -> 13%
where the time goes in v3:
time: 113 us; the launch traced here: 112 us
  starting transfers between devices  50.8 us (45%)
  waiting for transfers between devices  37.9 us (34%)
  Pallas kernels  18.7 us (17%)
  local copies, waits for them, and re-layouts  2.3 us (2%)
  other arithmetic  1.23 us (1%)
    ppermute x15, starting transfers between devices, send(): return lax.ppermute(block, ('tm', 'space'), pairs)  50.8 us
    ppermute x15, waiting for transfers between devices, send(): return lax.ppermute(block, ('tm', 'space'), pairs)  37.9 us
    pallas_call x4, Pallas kernels, call(): pl.pallas_call(kernel, out_shape=shapes, in_specs=[pl.BlockSpec(memory_sp...  14.1 us
    pallas_call x2, Pallas kernels, gathered(): pl.pallas_call(functools.partial(kernel, rows), out_shape=shape, in_specs...  4.57 us
  transfers between devices with their start and end apart: 15, of which 8 were waited for; matrix products, arithmetic and copies ran while one was open for 1% of the time, Pallas kernels for 13%

profile of v3, /device:TPU:187, one launch (start us, length us, event | category | flops | bytes accessed | tf_op | source)
XLA Modules:
  0.0 111.8 jit_solution(3864769508040488616)
XLA Ops:
  0.6 1.3 %copy_bitcast_fusion = (f32[3,384]{1,0:T(4,128)}, f32[3,384]{1,0:T(4,128)}) fusion(f32[1,1,3,384]{3,1,2,0:T(1,128)} %param.12, f32[1,1,3,384]{3,1,2,0:T(1,128)} %param.11), kind=kLoop, calls=%fused_computation.11 | loop fusion | bytes 18432
  1.9 2.6 %pack.1.mine = bf16[800,384]{1,0:T(8,128)(2,1)} custom-call(bf16[384,384]{1,0:T(8,128)(2,1)} %bitcast.24, bf16[384,384]{1,0:T(8,128)(2,1)} %bitcast.25, f32[3,384]{1,0:T(4,128)} %get-tuple-element.56.norm, f32[3,384]{1,0:T(4,128)} %get-tuple-element.55.delta), custom_call_target="tpu_custom_call" | custom-call | flops 1000000000 | bytes 1000 | tf_op jit(solution)/shard_map/pack/pallas_call | solution.py:182
  4.6 2.0 %stack.1.kv_a = bf16[768,384]{1,0:T(8,128)(2,1)} custom-call(bf16[384,384]{1,0:T(8,128)(2,1)} %bitcast.26, bf16[384,384]{1,0:T(8,128)(2,1)} %bitcast.27), custom_call_target="tpu_custom_call" | custom-call | flops 1000000000 | bytes 1000 | tf_op jit(solution)/shard_map/stack/pallas_call | solution.py:182
  6.6 1.3 %collective-permute-start.1 = (bf16[800,384]{1,0:T(8,128)(2,1)S(1)}, bf16[800,384]{1,0:T(8,128)(2,1)S(1)}, u32[]{:S(2)}, u32[]{:S(2)}) collective-permute-start(bf16[800,384]{1,0:T(8,128)(2,1)S(1)} %copy-done), channel_id=1, source_target_pairs={{0,16},{8,24},{4,20},{12,28},{16,32},{24,40},{20,36},{28,44},{32,4... | collective-permute-start | bytes 1843208 | tf_op jit(solution)/shard_map/ppermute | solution.py:18
  7.9 4.0 %collective-permute-start.2 = (bf16[800,384]{1,0:T(8,128)(2,1)S(1)}, bf16[800,384]{1,0:T(8,128)(2,1)S(1)}, u32[]{:S(2)}, u32[]{:S(2)}) collective-permute-start(bf16[800,384]{1,0:T(8,128)(2,1)S(1)} %copy-done), channel_id=1, source_target_pairs={{16,0},{24,8},{20,4},{28,12},{32,16},{40,24},{36,20},{44,28},{48,3... | collective-permute-start | bytes 1843208 | tf_op jit(solution)/shard_map/ppermute | solution.py:18
  11.9 5.0 %collective-permute-start.3 = (bf16[800,384]{1,0:T(8,128)(2,1)S(1)}, bf16[800,384]{1,0:T(8,128)(2,1)S(1)}, u32[]{:S(2)}, u32[]{:S(2)}) collective-permute-start(bf16[800,384]{1,0:T(8,128)(2,1)S(1)} %copy-done), channel_id=1, source_target_pairs={{0,8},{4,12},{8,0},{12,4},{16,24},{20,28},{24,16},{28,20},{32,40},... | collective-permute-start | bytes 1843208 | tf_op jit(solution)/shard_map/ppermute | solution.py:18
  16.9 3.1 %collective-permute-start = (bf16[768,384]{1,0:T(8,128)(2,1)}, bf16[768,384]{1,0:T(8,128)(2,1)S(1)}, u32[]{:S(2)}, u32[]{:S(2)}) collective-permute-start(bf16[768,384]{1,0:T(8,128)(2,1)} %stack.1.kv_a), channel_id=1, source_target_pairs={{0,4},{4,0},{8,12},{12,8},{16,20},{20,16},{24,28},{28,24},{32,36},... | collective-permute-start | bytes 1769480 | tf_op jit(solution)/shard_map/ppermute | solution.py:18
  20.2 1.7 %collective-permute-done.kv_b = bf16[768,384]{1,0:T(8,128)(2,1)S(1)} collective-permute-done((bf16[768,384]{1,0:T(8,128)(2,1)}, bf16[768,384]{1,0:T(8,128)(2,1)S(1)}, u32[]{:S(2)}, u32[]{:S(2)}) %collective-permute-start) | collective-permute-done | bytes 589856 | tf_op jit(solution)/shard_map/ppermute | solution.py:18
  21.9 3.5 %own.1 = (f32[4,768,384]{2,1,0:T(8,128)S(1)}, f32[384,384]{1,0:T(8,128)S(1)}) custom-call(s32[32,4,3]{2,1,0:T(4,128)S(1)} %copy.12.extents, bf16[800,384]{1,0:T(8,128)(2,1)S(1)} %copy-done, bf16[768,384]{1,0:T(8,128)(2,1)} %stack.1.kv_a, bf16[768,384]{1,0:T(8,128)(2,1)S(1)} %collective-permute-done.kv_b), custom_call_target="tpu_custom_call" | custom-call | flops 1000 | bytes 1000 | tf_op jit(solution)/shard_map/own/own/pallas_call | solution.py:167
  25.4 4.7 %collective-permute-done.3.other = bf16[800,384]{1,0:T(8,128)(2,1)S(1)} collective-permute-done((bf16[800,384]{1,0:T(8,128)(2,1)S(1)}, bf16[800,384]{1,0:T(8,128)(2,1)S(1)}, u32[]{:S(2)}, u32[]{:S(2)}) %collective-permute-start.3) | collective-permute-done | bytes 614432 | tf_op jit(solution)/shard_map/ppermute | solution.py:18
  30.2 4.5 %collective-permute-start.6 = (bf16[768,384]{1,0:T(8,128)(2,1)}, bf16[768,384]{1,0:T(8,128)(2,1)S(1)}, u32[]{:S(2)}, u32[]{:S(2)}) collective-permute-start(bf16[768,384]{1,0:T(8,128)(2,1)} %stack.1.kv_a), channel_id=1, source_target_pairs={{112,120},{136,128},{116,124},{140,132},{240,248},{264,256},{244,2... | collective-permute-start | bytes 1769480 | tf_op jit(solution)/shard_map/ppermute | solution.py:18
  34.6 1.3 %collective-permute-start.4 = (bf16[800,384]{1,0:T(8,128)(2,1)S(1)}, bf16[800,384]{1,0:T(8,128)(2,1)S(1)}, u32[]{:S(2)}, u32[]{:S(2)}) collective-permute-start(bf16[800,384]{1,0:T(8,128)(2,1)S(1)} %collective-permute-done.3.other), channel_id=1, source_target_pairs={{0,16},{8,24},{4,20},{12,28},{16,32},{24,40},{20,36},{28,44},{32,4... | collective-permute-start | bytes 1843208 | tf_op jit(solution)/shard_map/ppermute | solution.py:18
  35.9 4.0 %collective-permute-start.5 = (bf16[800,384]{1,0:T(8,128)(2,1)S(1)}, bf16[800,384]{1,0:T(8,128)(2,1)S(1)}, u32[]{:S(2)}, u32[]{:S(2)}) collective-permute-start(bf16[800,384]{1,0:T(8,128)(2,1)S(1)} %collective-permute-done.3.other), channel_id=1, source_target_pairs={{16,0},{24,8},{20,4},{28,12},{32,16},{40,24},{36,20},{44,28},{48,3... | collective-permute-start | bytes 1843208 | tf_op jit(solution)/shard_map/ppermute | solution.py:18
  40.0 3.2 %other.1 = (f32[4,768,384]{2,1,0:T(8,128)S(1)}, bf16[384,384]{1,0:T(8,128)(2,1)S(1)}) custom-call(s32[32,4,3]{2,1,0:T(4,128)S(1)} %copy.12.extents, bf16[800,384]{1,0:T(8,128)(2,1)S(1)} %collective-permute-done.3.other, bf16[768,384]{1,0:T(8,128)(2,1)} %stack.1.kv_a, ...), custom_call_target="tpu_custom_call", output_to_operand_aliasing={{0}: (4, {})} | custom-call | flops 1000 | bytes 1000 | tf_op jit(solution)/shard_map/other/other/pallas_call | solution.py:167
  43.2 2.5 %collective-permute-done.6.kv_c = bf16[768,384]{1,0:T(8,128)(2,1)S(1)} collective-permute-done((bf16[768,384]{1,0:T(8,128)(2,1)}, bf16[768,384]{1,0:T(8,128)(2,1)S(1)}, u32[]{:S(2)}, u32[]{:S(2)}) %collective-permute-start.6) | collective-permute-done | bytes 589856 | tf_op jit(solution)/shard_map/ppermute | solution.py:18
  45.6 0.7 collective-permute-start.7
  46.3 8.0 %collective-permute-start.8 = (bf16[384,384]{1,0:T(8,128)(2,1)S(1)}, bf16[384,384]{1,0:T(8,128)(2,1)S(1)}, u32[]{:S(2)}, u32[]{:S(2)}) collective-permute-start(bf16[384,384]{1,0:T(8,128)(2,1)S(1)} %get-tuple-element.42), channel_id=1, source_target_pairs={{0,8},{4,12},{8,0},{12,4},{16,24},{20,28},{24,16},{28,20},{32,40},... | collective-permute-start | bytes 884744 | tf_op jit(solution)/shard_map/ppermute | solution.py:18
  54.4 2.1 %near.1 = (f32[4,768,384]{2,1,0:T(8,128)S(1)}, bf16[384,384]{1,0:T(8,128)(2,1)S(1)}, bf16[384,384]{1,0:T(8,128)(2,1)S(1)}) custom-call(s32[32,4,3]{2,1,0:T(4,128)S(1)} %copy.12.extents, bf16[800,384]{1,0:T(8,128)(2,1)S(1)} %collective-permute-done.1.low, bf16[800,384]{1,0:T(8,128)(2,1)S(1)} %collective-permute-done.2.high, ...), custom_call_target="tpu_custom_call", output_to_operand_aliasing={{0}: (7, {})} | custom-call | flops 1000 | bytes 1000 | tf_op jit(solution)/shard_map/near/near/pallas_call | solution.py:167
  56.5 1.3 %collective-permute-start.10 = (bf16[384,384]{1,0:T(8,128)(2,1)S(1)}, bf16[384,384]{1,0:T(8,128)(2,1)S(1)}, u32[]{:S(2)}, u32[]{:S(2)}) collective-permute-start(bf16[384,384]{1,0:T(8,128)(2,1)S(1)} %get-tuple-element.44), channel_id=1, source_target_pairs={{0,16},{8,24},{4,20},{12,28},{16,32},{24,40},{20,36},{28,44},{32,4... | collective-permute-start | bytes 884744 | tf_op jit(solution)/shard_map/ppermute | solution.py:18
  57.8 4.0 %collective-permute-start.9 = (bf16[384,384]{1,0:T(8,128)(2,1)S(1)}, bf16[384,384]{1,0:T(8,128)(2,1)S(1)}, u32[]{:S(2)}, u32[]{:S(2)}) collective-permute-start(bf16[384,384]{1,0:T(8,128)(2,1)S(1)} %get-tuple-element.43), channel_id=1, source_target_pairs={{16,0},{24,8},{20,4},{28,12},{32,16},{40,24},{36,20},{44,28},{48,3... | collective-permute-start | bytes 884744 | tf_op jit(solution)/shard_map/ppermute | solution.py:18
  61.8 5.2 %far.1 = (bf16[384,384]{1,0:T(8,128)(2,1)S(1)}, bf16[384,384]{1,0:T(8,128)(2,1)S(1)}, f32[768,384]{1,0:T(8,128)S(1)}, f32[768,384]{1,0:T(8,128)S(1)}, bf16[2,768,384]{2,1,0:T(8,128)(2,1)S(1)}) custom-call(s32[32,4,3]{2,1,0:T(4,128)S(1)} %copy.12.extents, bf16[800,384]{1,0:T(8,128)(2,1)S(1)} %collective-permute-done.4.low, ...), custom_call_target="tpu_custom_call" | custom-call | flops 20000000000 | bytes 1000 | tf_op jit(solution)/shard_map/far/far/pallas_call | solution.py:167
  67.1 0.5 collective-permute-done.9
  67.6 3.3 %collective-permute-start.13 = (bf16[2,768,384]{2,1,0:T(8,128)(2,1)S(1)}, bf16[2,768,384]{2,1,0:T(8,128)(2,1)S(1)}, u32[]{:S(2)}, u32[]{:S(2)}) collective-permute-start(bf16[2,768,384]{2,1,0:T(8,128)(2,1)S(1)} %get-tuple-element.51), channel_id=1, source_target_pairs={{0,4},{4,0},{8,12},{12,8},{16,20},{20,16},{24,28},{28,24},{32,36},... | collective-permute-start | bytes 3538952 | tf_op jit(solution)/shard_map/ppermute | solution.py:18
  70.9 2.5 %collective-permute-done.13 = bf16[2,768,384]{2,1,0:T(8,128)(2,1)S(1)} collective-permute-done((bf16[2,768,384]{2,1,0:T(8,128)(2,1)S(1)}, bf16[2,768,384]{2,1,0:T(8,128)(2,1)S(1)}, u32[]{:S(2)}, u32[]{:S(2)}) %collective-permute-start.13) | collective-permute-done | bytes 1179680 | tf_op jit(solution)/shard_map/ppermute | solution.py:18
  73.5 1.3 %collective-permute-start.14 = (bf16[768,384]{1,0:T(8,128)(2,1)S(1)}, bf16[768,384]{1,0:T(8,128)(2,1)S(1)}, u32[]{:S(2)}, u32[]{:S(2)}) collective-permute-start(bf16[768,384]{1,0:T(8,128)(2,1)S(1)} %fusion), channel_id=1, source_target_pairs={{120,112},{128,136},{124,116},{132,140},{248,240},{256,264},{252,2... | collective-permute-start | bytes 1769480 | tf_op jit(solution)/shard_map/ppermute | solution.py:18
  74.8 7.7 %collective-permute-start.11 = (bf16[384,384]{1,0:T(8,128)(2,1)S(1)}, bf16[384,384]{1,0:T(8,128)(2,1)S(1)}, u32[]{:S(2)}, u32[]{:S(2)}) collective-permute-start(bf16[384,384]{1,0:T(8,128)(2,1)S(1)} %get-tuple-element.48), channel_id=1, source_target_pairs={{16,8},{24,0},{20,12},{28,4},{32,24},{40,16},{36,28},{44,20},{48,4... | collective-permute-start | bytes 884744 | tf_op jit(solution)/shard_map/ppermute | solution.py:18
  82.4 1.3 %collective-permute-start.12 = (bf16[384,384]{1,0:T(8,128)(2,1)S(1)}, bf16[384,384]{1,0:T(8,128)(2,1)S(1)}, u32[]{:S(2)}, u32[]{:S(2)}) collective-permute-start(bf16[384,384]{1,0:T(8,128)(2,1)S(1)} %get-tuple-element.49), channel_id=1, source_target_pairs={{0,24},{8,16},{4,28},{12,20},{16,40},{24,32},{20,44},{28,36},{32,5... | collective-permute-start | bytes 884744 | tf_op jit(solution)/shard_map/ppermute | solution.py:18
  83.7 11.7 %collective-permute-done.11 = bf16[384,384]{1,0:T(8,128)(2,1)S(1)} collective-permute-done((bf16[384,384]{1,0:T(8,128)(2,1)S(1)}, bf16[384,384]{1,0:T(8,128)(2,1)S(1)}, u32[]{:S(2)}, u32[]{:S(2)}) %collective-permute-start.11) | collective-permute-done | bytes 294944 | tf_op jit(solution)/shard_map/ppermute | solution.py:18
  95.5 3.0 %collective-permute-done.12 = bf16[384,384]{1,0:T(8,128)(2,1)S(1)} collective-permute-done((bf16[384,384]{1,0:T(8,128)(2,1)S(1)}, bf16[384,384]{1,0:T(8,128)(2,1)S(1)}, u32[]{:S(2)}, u32[]{:S(2)}) %collective-permute-start.12) | collective-permute-done | bytes 294944 | tf_op jit(solution)/shard_map/ppermute | solution.py:18
  98.5 0.9 fusion.3
  99.5 11.3 %collective-permute-done.14 = bf16[768,384]{1,0:T(8,128)(2,1)S(1)} collective-permute-done((bf16[768,384]{1,0:T(8,128)(2,1)S(1)}, bf16[768,384]{1,0:T(8,128)(2,1)S(1)}, u32[]{:S(2)}, u32[]{:S(2)}) %collective-permute-start.14) | collective-permute-done | bytes 589856 | tf_op jit(solution)/shard_map/ppermute | solution.py:18
  110.9 0.9 slice_bitcast_fusion.2
  (14 shorter events, 0.4 us)
Async XLA Ops:
  4.6 2.0 %copy-start = (bf16[800,384]{1,0:T(8,128)(2,1)S(1)}, bf16[800,384]{1,0:T(8,128)(2,1)}, u32[]{:S(2)}) copy-start(bf16[800,384]{1,0:T(8,128)(2,1)} %pack.1.mine) | copy-start | bytes 1843204
  4.6 15.5 %copy-start.1 = (s32[32,4,3]{0,1,2:T(4,128)S(1)}, s32[32,4,3]{0,1,2:T(4,128)}, u32[]{:S(2)}) copy-start(s32[32,4,3]{0,1,2:T(4,128)} %param.13) | copy-start | bytes 4612
  6.6 18.9 %collective-permute-start.1 = (bf16[800,384]{1,0:T(8,128)(2,1)S(1)}, bf16[800,384]{1,0:T(8,128)(2,1)S(1)}, u32[]{:S(2)}, u32[]{:S(2)}) collective-permute-start(bf16[800,384]{1,0:T(8,128)(2,1)S(1)} %copy-done), channel_id=1, source_target_pairs={{0,16},{8,24},{4,20},{12,28},{16,32},{24,40},{20,36},{28,44},{32,4... | collective-permute-start | bytes 1843208 | tf_op jit(solution)/shard_map/ppermute | solution.py:18
  7.9 17.6 %collective-permute-start.2 = (bf16[800,384]{1,0:T(8,128)(2,1)S(1)}, bf16[800,384]{1,0:T(8,128)(2,1)S(1)}, u32[]{:S(2)}, u32[]{:S(2)}) collective-permute-start(bf16[800,384]{1,0:T(8,128)(2,1)S(1)} %copy-done), channel_id=1, source_target_pairs={{16,0},{24,8},{20,4},{28,12},{32,16},{40,24},{36,20},{44,28},{48,3... | collective-permute-start | bytes 1843208 | tf_op jit(solution)/shard_map/ppermute | solution.py:18
  11.9 18.3 %collective-permute-start.3 = (bf16[800,384]{1,0:T(8,128)(2,1)S(1)}, bf16[800,384]{1,0:T(8,128)(2,1)S(1)}, u32[]{:S(2)}, u32[]{:S(2)}) collective-permute-start(bf16[800,384]{1,0:T(8,128)(2,1)S(1)} %copy-done), channel_id=1, source_target_pairs={{0,8},{4,12},{8,0},{12,4},{16,24},{20,28},{24,16},{28,20},{32,40},... | collective-permute-start | bytes 1843208 | tf_op jit(solution)/shard_map/ppermute | solution.py:18
  16.9 5.0 %collective-permute-start = (bf16[768,384]{1,0:T(8,128)(2,1)}, bf16[768,384]{1,0:T(8,128)(2,1)S(1)}, u32[]{:S(2)}, u32[]{:S(2)}) collective-permute-start(bf16[768,384]{1,0:T(8,128)(2,1)} %stack.1.kv_a), channel_id=1, source_target_pairs={{0,4},{4,0},{8,12},{12,8},{16,20},{20,16},{24,28},{28,24},{32,36},... | collective-permute-start | bytes 1769480 | tf_op jit(solution)/shard_map/ppermute | solution.py:18
  30.2 15.5 %collective-permute-start.6 = (bf16[768,384]{1,0:T(8,128)(2,1)}, bf16[768,384]{1,0:T(8,128)(2,1)S(1)}, u32[]{:S(2)}, u32[]{:S(2)}) collective-permute-start(bf16[768,384]{1,0:T(8,128)(2,1)} %stack.1.kv_a), channel_id=1, source_target_pairs={{112,120},{136,128},{116,124},{140,132},{240,248},{264,256},{244,2... | collective-permute-start | bytes 1769480 | tf_op jit(solution)/shard_map/ppermute | solution.py:18
  34.6 27.2 %collective-permute-start.4 = (bf16[800,384]{1,0:T(8,128)(2,1)S(1)}, bf16[800,384]{1,0:T(8,128)(2,1)S(1)}, u32[]{:S(2)}, u32[]{:S(2)}) collective-permute-start(bf16[800,384]{1,0:T(8,128)(2,1)S(1)} %collective-permute-done.3.other), channel_id=1, source_target_pairs={{0,16},{8,24},{4,20},{12,28},{16,32},{24,40},{20,36},{28,44},{32,4... | collective-permute-start | bytes 1843208 | tf_op jit(solution)/shard_map/ppermute | solution.py:18
  35.9 25.9 %collective-permute-start.5 = (bf16[800,384]{1,0:T(8,128)(2,1)S(1)}, bf16[800,384]{1,0:T(8,128)(2,1)S(1)}, u32[]{:S(2)}, u32[]{:S(2)}) collective-permute-start(bf16[800,384]{1,0:T(8,128)(2,1)S(1)} %collective-permute-done.3.other), channel_id=1, source_target_pairs={{16,0},{24,8},{20,4},{28,12},{32,16},{40,24},{36,20},{44,28},{48,3... | collective-permute-start | bytes 1843208 | tf_op jit(solution)/shard_map/ppermute | solution.py:18
  45.6 8.7 %collective-permute-start.7 = (bf16[768,384]{1,0:T(8,128)(2,1)S(1)}, bf16[768,384]{1,0:T(8,128)(2,1)S(1)}, u32[]{:S(2)}, u32[]{:S(2)}) collective-permute-start(bf16[768,384]{1,0:T(8,128)(2,1)S(1)} %collective-permute-done.6.kv_c), channel_id=1, source_target_pairs={{120,124},{128,132},{124,120},{132,128},{248,252},{256,260},{252,2... | collective-permute-start | bytes 1769480 | tf_op jit(solution)/shard_map/ppermute | solution.py:18
  46.3 20.7 %collective-permute-start.8 = (bf16[384,384]{1,0:T(8,128)(2,1)S(1)}, bf16[384,384]{1,0:T(8,128)(2,1)S(1)}, u32[]{:S(2)}, u32[]{:S(2)}) collective-permute-start(bf16[384,384]{1,0:T(8,128)(2,1)S(1)} %get-tuple-element.42), channel_id=1, source_target_pairs={{0,8},{4,12},{8,0},{12,4},{16,24},{20,28},{24,16},{28,20},{32,40},... | collective-permute-start | bytes 884744 | tf_op jit(solution)/shard_map/ppermute | solution.py:18
  56.5 10.6 %collective-permute-start.10 = (bf16[384,384]{1,0:T(8,128)(2,1)S(1)}, bf16[384,384]{1,0:T(8,128)(2,1)S(1)}, u32[]{:S(2)}, u32[]{:S(2)}) collective-permute-start(bf16[384,384]{1,0:T(8,128)(2,1)S(1)} %get-tuple-element.44), channel_id=1, source_target_pairs={{0,16},{8,24},{4,20},{12,28},{16,32},{24,40},{20,36},{28,44},{32,4... | collective-permute-start | bytes 884744 | tf_op jit(solution)/shard_map/ppermute | solution.py:18
  57.8 9.8 %collective-permute-start.9 = (bf16[384,384]{1,0:T(8,128)(2,1)S(1)}, bf16[384,384]{1,0:T(8,128)(2,1)S(1)}, u32[]{:S(2)}, u32[]{:S(2)}) collective-permute-start(bf16[384,384]{1,0:T(8,128)(2,1)S(1)} %get-tuple-element.43), channel_id=1, source_target_pairs={{16,0},{24,8},{20,4},{28,12},{32,16},{40,24},{36,20},{44,28},{48,3... | collective-permute-start | bytes 884744 | tf_op jit(solution)/shard_map/ppermute | solution.py:18
  67.6 5.8 %collective-permute-start.13 = (bf16[2,768,384]{2,1,0:T(8,128)(2,1)S(1)}, bf16[2,768,384]{2,1,0:T(8,128)(2,1)S(1)}, u32[]{:S(2)}, u32[]{:S(2)}) collective-permute-start(bf16[2,768,384]{2,1,0:T(8,128)(2,1)S(1)} %get-tuple-element.51), channel_id=1, source_target_pairs={{0,4},{4,0},{8,12},{12,8},{16,20},{20,16},{24,28},{28,24},{32,36},... | collective-permute-start | bytes 3538952 | tf_op jit(solution)/shard_map/ppermute | solution.py:18
  73.5 37.3 %collective-permute-start.14 = (bf16[768,384]{1,0:T(8,128)(2,1)S(1)}, bf16[768,384]{1,0:T(8,128)(2,1)S(1)}, u32[]{:S(2)}, u32[]{:S(2)}) collective-permute-start(bf16[768,384]{1,0:T(8,128)(2,1)S(1)} %fusion), channel_id=1, source_target_pairs={{120,112},{128,136},{124,116},{132,140},{248,240},{256,264},{252,2... | collective-permute-start | bytes 1769480 | tf_op jit(solution)/shard_map/ppermute | solution.py:18
  74.8 20.7 %collective-permute-start.11 = (bf16[384,384]{1,0:T(8,128)(2,1)S(1)}, bf16[384,384]{1,0:T(8,128)(2,1)S(1)}, u32[]{:S(2)}, u32[]{:S(2)}) collective-permute-start(bf16[384,384]{1,0:T(8,128)(2,1)S(1)} %get-tuple-element.48), channel_id=1, source_target_pairs={{16,8},{24,0},{20,12},{28,4},{32,24},{40,16},{36,28},{44,20},{48,4... | collective-permute-start | bytes 884744 | tf_op jit(solution)/shard_map/ppermute | solution.py:18
  82.4 16.1 %collective-permute-start.12 = (bf16[384,384]{1,0:T(8,128)(2,1)S(1)}, bf16[384,384]{1,0:T(8,128)(2,1)S(1)}, u32[]{:S(2)}, u32[]{:S(2)}) collective-permute-start(bf16[384,384]{1,0:T(8,128)(2,1)S(1)} %get-tuple-element.49), channel_id=1, source_target_pairs={{0,24},{8,16},{4,28},{12,20},{16,40},{24,32},{20,44},{28,36},{32,5... | collective-permute-start | bytes 884744 | tf_op jit(solution)/shard_map/ppermute | solution.py:18

commit v4 on v1

v4 whole, which is shorter than its diff:
```python
import functools

import jax
import jax.numpy as jnp
from jax import lax
from jax.experimental import pallas as pl
from jax.experimental.pallas import tpu as pltpu
from jax.sharding import PartitionSpec as P

LOG2E = 1.4426950408889634
HEAD = 128
AUX = 32
NEVER = 1e30
BF = jnp.bfloat16
F32 = jnp.float32


def send(block, pairs):
    return lax.ppermute(block, ("tm", "space"), pairs)


def routes(time_all):
    at = lambda t, c, w: t * 4 + c * 2 + w
    every = [(t, c, w) for t in range(time_all) for c in range(2) for w in range(2)]
    near = {0: [], 1: []}
    for t, c, w in every:
        if t + 1 < time_all:
            near[t % 2] += [(at(t, c, w), at(t + 1, c, w)), (at(t + 1, c, w), at(t, c, w))]
    core = [(at(t, c, w), at(t, c, 1 - w)) for t, c, w in every]
    pair = [(at(t, c, w), at(t, 1 - c, w)) for t, c, w in every]
    return core, pair, near[0], near[1]


def pack_kernel(half, query, grad, norm, delta, pack, msg):
    chip = lax.axis_index("space") // 2
    rows = 2 * half
    keep = pl.ds(pl.multiple_of(chip * half, half), half)
    give = pl.ds(pl.multiple_of((1 - chip) * half, half), half)
    pack[0:half] = query[keep]
    pack[rows : rows + half] = grad[keep]
    msg[0:half] = query[give]
    msg[half:rows] = grad[give]
    pieces = []
    for ref in (norm, delta):
        x = ref[:, 0, :]
        high = x.astype(BF)
        rest = x - high.astype(F32)
        mid = rest.astype(BF)
        pieces += [high.astype(F32), mid.astype(F32), rest - mid.astype(F32)]
    heads, _, channels = norm.shape
    pieces.append(jnp.zeros((AUX - 6 * heads, channels), F32))
    aux = jnp.concatenate(pieces)
    turned = jnp.concatenate([aux[:, half:], aux[:, :half]], axis=1)
    aux = jnp.where(chip == 0, aux, turned).astype(BF)
    pack[2 * rows :] = aux
    msg[rows:] = aux


def join_kernel(half, msg, pack_in, pack):
    rows = 2 * half
    pack[half:rows] = msg[0:half]
    pack[rows + half : 2 * rows] = msg[half:rows]
    lane = lax.broadcasted_iota(jnp.int32, (AUX, pack.shape[1]), 1)
    own, got = pack_in[2 * rows :].astype(F32), msg[rows:].astype(F32)
    pack[2 * rows :] = jnp.where(lane < half, own, got).astype(BF)


def stack_kernel(rows, key, value, out):
    out[0:rows] = key[...]
    out[rows:] = value[...]


def seen(extents, time_all, step):
    time_pos, frame_pos = lax.axis_index("tm"), lax.axis_index("space")
    chip, core = frame_pos // 2, frame_pos % 2
    when = time_pos + step(time_pos)
    place = jnp.clip(when, 0, time_all - 1)
    inside = (when >= 0) & (when < time_all)
    gap = jnp.abs(when - time_pos)

    def flag(j, part):
        height = chip if part == 0 else 1 - chip
        extent = [extents[place, height * 2 + core, i] for i in range(3)]
        height_gap = jnp.where(j >= 2, 1 - part, part)
        return inside & (gap <= extent[0]) & (height_gap <= extent[1]) & (j % 2 <= extent[2])

    return flag


def accumulate(pack, flag, kv, acc, dq, factor):
    channels = pack.shape[1]
    rows = (pack.shape[0] - AUX) // 2
    heads = channels // HEAD
    dq[...] = jnp.zeros_like(dq)
    aux = pack[2 * rows :, :].astype(F32)
    first = lax.broadcasted_iota(jnp.int32, (1, rows), 1) < rows // 2
    last = (((1,), (1,)), ((), ()))

    def step(j, carry):
        own, other = flag(j, 0), flag(j, 1)

        @pl.when(own | other)
        def _():
            hide = jnp.where(first, jnp.where(own, 0.0, NEVER), jnp.where(other, 0.0, NEVER))
            for h in range(heads):
                cols = slice(h * HEAD, (h + 1) * HEAD)
                row = lambda i: aux[i * heads + h : i * heads + h + 1]
                norm = (row(0) + (row(1) + row(2))) * LOG2E + hide
                delta = row(3) + (row(4) + row(5))
                q, g = pack[0:rows, cols], pack[rows : 2 * rows, cols]
                k, v = kv[j, 0:rows, cols], kv[j, rows : 2 * rows, cols]
                st = lax.dot_general(k, q, last, preferred_element_type=F32)
                p = jnp.exp2(st * (factor * LOG2E) - norm)
                dp = lax.dot_general(v, g, last, preferred_element_type=F32)
                ds = (p * (dp - delta)).astype(BF)
                acc[j, rows : 2 * rows, cols] += jnp.dot(p.astype(BF), g, preferred_element_type=F32)
                acc[j, 0:rows, cols] += jnp.dot(ds, q, preferred_element_type=F32)
                dq[:, cols] += lax.dot_general(ds, k, (((0,), (0,)), ((), ())), preferred_element_type=F32)

        return carry

    lax.fori_loop(0, 4, step, 0)


def own_kernel(factor, time_all, extents, pack, kv_a, kv_b, kv_c, kv_d, acc, dq, kv):
    for i, ref in enumerate((kv_a, kv_b, kv_c, kv_d)):
        kv[i] = ref[...]
    acc[...] = jnp.zeros_like(acc)
    accumulate(pack, seen(extents, time_all, lambda t: 0), kv, acc, dq, factor)
    dq[...] = dq[...] * factor


def even_kernel(factor, time_all, extents, pack, kv, acc_in, acc, dq_out, dq):
    accumulate(pack, seen(extents, time_all, lambda t: 1 - 2 * (t % 2)), kv, acc, dq, factor)
    dq_out[...] = (dq[...] * factor).astype(BF)


def odd_kernel(factor, time_all, extents, pack, kv, acc, dq_out, own, lent, sib, dq):
    accumulate(pack, seen(extents, time_all, lambda t: 2 * (t % 2) - 1), kv, acc, dq, factor)
    dq_out[...] = (dq[...] * factor).astype(BF)
    rows = dq.shape[0]
    own[0:rows] = acc[0, 0:rows] * factor
    own[rows:] = acc[0, rows:]
    lent[0:rows] = acc[2, 0:rows] * factor
    lent[rows:] = acc[2, rows:]
    for i, j in enumerate((1, 3)):
        sib[i, 0:rows] = (acc[j, 0:rows] * factor).astype(BF)
        sib[i, rows:] = acc[j, rows:].astype(BF)


def sum_kernel(half, own, even, odd, mine, msg):
    total = own[...] + even[...].astype(F32) + odd[...].astype(F32)
    mine[...] = total[:half].astype(BF)
    msg[...] = total[half:].astype(BF)


def place_kernel(half, mine, got, out):
    chip = lax.axis_index("space") // 2
    out[pl.ds(pl.multiple_of(chip * half, half), half)] = mine[...]
    out[pl.ds(pl.multiple_of((1 - chip) * half, half), half)] = got[...]


def lend_kernel(lent, sib, out):
    out[...] = (lent[...] + sib[1].astype(F32)).astype(BF)


def close_kernel(rows, own, sib, given, key, value):
    total = own[...] + sib[0].astype(F32) + given[...].astype(F32)
    key[...] = total[:rows].astype(BF)
    value[...] = total[rows:].astype(BF)


def call(kernel, shapes, operands, micros, name, scratch=(), aliases=None, scalars=0):
    whole = pl.BlockSpec(memory_space=pltpu.VMEM)
    return pl.pallas_call(
        kernel,
        out_shape=shapes,
        in_specs=[pl.BlockSpec(memory_space=pltpu.SMEM)] * scalars + [whole] * (len(operands) - scalars),
        out_specs=[whole] * len(shapes),
        scratch_shapes=scratch,
        input_output_aliases=aliases or {},
        compiler_params=pltpu.CompilerParams(vmem_limit_bytes=40 * 2**20),
        cost_estimate=pl.CostEstimate(flops=micros * 10**9 + 1000, bytes_accessed=1000, transcendentals=0),
        name=name,
    )(*operands)


def body(query_tiles, key_tiles, value_tiles, grad_output, log_norm, row_delta, extents):
    rows, channels = query_tiles.shape[2:]
    heads, half = log_norm.shape[2], rows // 2
    factor = (channels // heads) ** (-0.5)
    time_all = lax.axis_size("tm")
    core, pair, even, odd = routes(time_all)
    out = jax.ShapeDtypeStruct
    tile, two = (rows, channels), (2 * rows, channels)

    pack, msg = call(
        functools.partial(pack_kernel, half),
        [out((2 * rows + AUX, channels), BF), out((rows + AUX, channels), BF)],
        (query_tiles[0, 0], grad_output[0, 0], log_norm.reshape(heads, 1, rows), row_delta.reshape(heads, 1, rows)),
        0, "pack",
    )
    msg = send(msg, pair)
    pack, key, value = lax.optimization_barrier((pack, key_tiles[0, 0], value_tiles[0, 0]))
    (kv_a,) = call(functools.partial(stack_kernel, rows), [out(two, BF)], (key, value), 0, "stack")
    kv_c = send(kv_a, pair)
    kv_b = send(kv_a, core)
    (pack,) = call(
        functools.partial(join_kernel, half), [out((2 * rows + AUX, channels), BF)], (msg, pack), 20, "join", aliases={1: 0}
    )
    odd_pack = send(pack, odd)
    even_pack = send(pack, even)
    kv_d = send(kv_c, core)

    with jax.named_scope("own"):
        acc, dq, kv = call(
            functools.partial(own_kernel, factor, time_all),
            [out((4,) + two, F32), out(tile, F32), out((4,) + two, BF)],
            (extents, pack, kv_a, kv_b, kv_c, kv_d), 0, "own", scalars=1,
        )
    with jax.named_scope("even"):
        acc, even_dq = call(
            functools.partial(even_kernel, factor, time_all),
            [out((4,) + two, F32), out(tile, BF)],
            (extents, even_pack, kv, acc), 0, "even", [pltpu.VMEM(tile, F32)], {3: 0}, scalars=1,
        )
    with jax.named_scope("odd"):
        odd_dq, own, lent, sib = call(
            functools.partial(odd_kernel, factor, time_all),
            [out(tile, BF), out(two, F32), out(two, F32), out((2,) + two, BF)],
            (extents, odd_pack, kv, acc), 20, "odd", [pltpu.VMEM(tile, F32)], scalars=1,
        )
    odd_back = send(odd_dq, odd)
    even_back = send(even_dq, even)
    sib, even_back = lax.optimization_barrier((sib, even_back))
    sib = send(sib, core)
    (lent,) = call(lend_kernel, [out(two, BF)], (lent, sib), 0, "lend")
    given = send(lent, pair)
    mine, msg = call(
        functools.partial(sum_kernel, half), [out((half, channels), BF)] * 2, (dq, even_back, odd_back), 20, "sum"
    )
    msg = send(msg, pair)
    (grad_query,) = call(functools.partial(place_kernel, half), [out(tile, BF)], (mine, msg), 0, "place")
    grad_key, grad_value = call(functools.partial(close_kernel, rows), [out(tile, BF)] * 2, (own, sib, given), 0, "close")
    shape = (1, 1, rows, channels)
    return grad_query.reshape(shape), grad_key.reshape(shape), grad_value.reshape(shape)


def solution(mesh):
    tiles, per_row = P("tm", "space", None, "heads"), P("tm", "space", "heads", None)
    return jax.shard_map(
        body,
        mesh=mesh,
        in_specs=(tiles, tiles, tiles, tiles, per_row, per_row, P()),
        out_specs=(tiles, tiles, tiles),
        check_vma=False,
    )
```

time: 117 us -> 122 us (1.043)
  the two profiles are of different devices: /device:TPU:384 before, /device:TPU:193 now
where the time goes in v4:
time: 122 us
  waiting for transfers between devices  64.3 us (53%)
  starting transfers between devices  30.2 us (25%)
  Pallas kernels  21.1 us (17%)
  local copies, waits for them, and re-layouts  5.33 us (4%)
    ppermute x11, waiting for transfers between devices, send(): return lax.ppermute(block, ('tm', 'space'), pairs)  64.3 us
    ppermute x11, starting transfers between devices, send(): return lax.ppermute(block, ('tm', 'space'), pairs)  30.2 us
    pallas_call x10, Pallas kernels, call(): pl.pallas_call(kernel, out_shape=shapes, in_specs=[pl.BlockSpec(memory_sp...  21.1 us
    unnamed x15, local copies, waits for them, and re-layouts  5.33 us
  transfers between devices with their start and end apart: 11, of which 7 were waited for; matrix products, arithmetic and copies ran while one was open for 0% of the time, Pallas kernels for 16%

profile of v4, /device:TPU:193, one launch (start us, length us, event | category | flops | bytes accessed | tf_op | source)
XLA Modules:
  0.0 121.7 jit_solution(3903023743859992494)
XLA Ops:
  0.6 1.0 copy-done
  1.6 1.0 copy-done.1
  2.6 0.7 copy-done.4
  3.2 0.7 copy-done.5
  3.9 0.1 pack.1
  4.1 1.9 %collective-permute-start = (bf16[416,384]{1,0:T(8,128)(2,1)S(1)}, bf16[416,384]{1,0:T(8,128)(2,1)S(1)}, u32[]{:S(2)}, u32[]{:S(2)}) collective-permute-start(bf16[416,384]{1,0:T(8,128)(2,1)S(1)} %get-tuple-element.23), channel_id=1, source_target_pairs={{0,8},{4,12},{8,0},{12,4},{16,24},{20,28},{24,16},{28,20},{32,40},... | collective-permute-start | bytes 958472 | tf_op jit(solution)/shard_map/ppermute | solution.py:19
  6.0 1.0 copy-done.2
  6.9 1.0 copy-done.3
  8.0 3.4 %collective-permute-start.2 = (bf16[768,384]{1,0:T(8,128)(2,1)S(1)}, bf16[768,384]{1,0:T(8,128)(2,1)S(1)}, u32[]{:S(2)}, u32[]{:S(2)}) collective-permute-start(bf16[768,384]{1,0:T(8,128)(2,1)S(1)} %stack.1.kv_a), channel_id=1, source_target_pairs={{0,8},{4,12},{8,0},{12,4},{16,24},{20,28},{24,16},{28,20},{32,40},... | collective-permute-start | bytes 1769480 | tf_op jit(solution)/shard_map/ppermute | solution.py:19
  11.3 3.0 %collective-permute-done.msg = bf16[416,384]{1,0:T(8,128)(2,1)S(1)} collective-permute-done((bf16[416,384]{1,0:T(8,128)(2,1)S(1)}, bf16[416,384]{1,0:T(8,128)(2,1)S(1)}, u32[]{:S(2)}, u32[]{:S(2)}) %collective-permute-start) | collective-permute-done | bytes 319520 | tf_op jit(solution)/shard_map/ppermute | solution.py:19
  14.4 3.2 %collective-permute-start.5 = (bf16[800,384]{1,0:T(8,128)(2,1)S(1)}, bf16[800,384]{1,0:T(8,128)(2,1)S(1)}, u32[]{:S(2)}, u32[]{:S(2)}) collective-permute-start(bf16[800,384]{1,0:T(8,128)(2,1)S(1)} %join.1.pack), channel_id=1, source_target_pairs={{0,16},{16,0},{4,20},{20,4},{8,24},{24,8},{12,28},{28,12},{32,48},... | collective-permute-start | bytes 1843208 | tf_op jit(solution)/shard_map/ppermute | solution.py:19
  17.6 3.1 %collective-permute-start.4 = (bf16[800,384]{1,0:T(8,128)(2,1)S(1)}, bf16[800,384]{1,0:T(8,128)(2,1)}, u32[]{:S(2)}, u32[]{:S(2)}) collective-permute-start(bf16[800,384]{1,0:T(8,128)(2,1)S(1)} %join.1.pack), channel_id=1, source_target_pairs={{16,32},{32,16},{20,36},{36,20},{24,40},{40,24},{28,44},{44,28},{4... | collective-permute-start | bytes 1843208 | tf_op jit(solution)/shard_map/ppermute | solution.py:19
  20.7 5.2 %collective-permute-start.1 = (bf16[768,384]{1,0:T(8,128)(2,1)S(1)}, bf16[768,384]{1,0:T(8,128)(2,1)S(1)}, u32[]{:S(2)}, u32[]{:S(2)}) collective-permute-start(bf16[768,384]{1,0:T(8,128)(2,1)S(1)} %stack.1.kv_a), channel_id=1, source_target_pairs={{0,4},{4,0},{8,12},{12,8},{16,20},{20,16},{24,28},{28,24},{32,36},... | collective-permute-start | bytes 1769480 | tf_op jit(solution)/shard_map/ppermute | solution.py:19
  25.8 27.2 %collective-permute-done.2.kv_c = bf16[768,384]{1,0:T(8,128)(2,1)S(1)} collective-permute-done((bf16[768,384]{1,0:T(8,128)(2,1)S(1)}, bf16[768,384]{1,0:T(8,128)(2,1)S(1)}, u32[]{:S(2)}, u32[]{:S(2)}) %collective-permute-start.2) | collective-permute-done | bytes 589856 | tf_op jit(solution)/shard_map/ppermute | solution.py:19
  53.0 3.8 %collective-permute-start.3 = (bf16[768,384]{1,0:T(8,128)(2,1)S(1)}, bf16[768,384]{1,0:T(8,128)(2,1)}, u32[]{:S(2)}, u32[]{:S(2)}) collective-permute-start(bf16[768,384]{1,0:T(8,128)(2,1)S(1)} %collective-permute-done.2.kv_c), channel_id=1, source_target_pairs={{0,4},{4,0},{8,12},{12,8},{16,20},{20,16},{24,28},{28,24},{32,36},... | collective-permute-start | bytes 1769480 | tf_op jit(solution)/shard_map/ppermute | solution.py:19
  56.8 0.1 copy.12.extents
  56.9 1.6 %collective-permute-done.3.kv_d = bf16[768,384]{1,0:T(8,128)(2,1)} collective-permute-done((bf16[768,384]{1,0:T(8,128)(2,1)S(1)}, bf16[768,384]{1,0:T(8,128)(2,1)}, u32[]{:S(2)}, u32[]{:S(2)}) %collective-permute-start.3) | collective-permute-done | bytes 589856 | tf_op jit(solution)/shard_map/ppermute | solution.py:19
  58.5 8.0 %own.1 = (f32[4,768,384]{2,1,0:T(8,128)S(1)}, f32[384,384]{1,0:T(8,128)S(1)}, bf16[4,768,384]{2,1,0:T(8,128)(2,1)S(1)}) custom-call(s32[32,4,3]{2,1,0:T(4,128)S(1)} %copy.12.extents, bf16[800,384]{1,0:T(8,128)(2,1)S(1)} %join.1.pack, bf16[768,384]{1,0:T(8,128)(2,1)S(1)} %stack.1.kv_a, bf16[768,384]{1,0:T(8,128)(2,1)S(1)} %collective-permute-done.1.kv_b, ...), custom_call_target="tpu_custom_call" | custom-call | flops 1000 | bytes 1000 | tf_op jit(solution)/shard_map/own/own/pallas_call | solution.py:175
  66.5 6.0 %even.1 = (f32[4,768,384]{2,1,0:T(8,128)S(1)}, bf16[384,384]{1,0:T(8,128)(2,1)S(1)}) custom-call(s32[32,4,3]{2,1,0:T(4,128)S(1)} %copy.12.extents, bf16[800,384]{1,0:T(8,128)(2,1)S(1)} %collective-permute-done.5.pack, bf16[4,768,384]{2,1,0:T(8,128)(2,1)S(1)} %get-tuple-element.29.kv, ...), custom_call_target="tpu_custom_call", output_to_operand_aliasing={{0}: (3, {})} | custom-call | flops 1000 | bytes 1000 | tf_op jit(solution)/shard_map/even/even/pallas_call | solution.py:175
  72.5 1.9 %collective-permute-start.6 = (bf16[384,384]{1,0:T(8,128)(2,1)S(1)}, bf16[384,384]{1,0:T(8,128)(2,1)S(1)}, u32[]{:S(2)}, u32[]{:S(2)}) collective-permute-start(bf16[384,384]{1,0:T(8,128)(2,1)S(1)} %get-tuple-element.33), channel_id=1, source_target_pairs={{0,16},{16,0},{4,20},{20,4},{8,24},{24,8},{12,28},{28,12},{32,48},... | collective-permute-start | bytes 884744 | tf_op jit(solution)/shard_map/ppermute | solution.py:19
  74.5 5.0 %odd.1 = (bf16[384,384]{1,0:T(8,128)(2,1)S(1)}, f32[768,384]{1,0:T(8,128)S(1)}, f32[768,384]{1,0:T(8,128)S(1)}, bf16[2,768,384]{2,1,0:T(8,128)(2,1)S(1)}) custom-call(s32[32,4,3]{2,1,0:T(4,128)S(1)} %copy.12.extents, bf16[800,384]{1,0:T(8,128)(2,1)} %collective-permute-done.4.pack, bf16[4,768,384]{2,1,0:T(8,128)(2,1)S(1)} %get-tuple-element.29.kv, ...), custom_call_target="tpu_custom_call" | custom-call | flops 20000000000 | bytes 1000 | tf_op jit(solution)/shard_map/odd/odd/pallas_call | solution.py:175
  79.4 3.1 %collective-permute-done.6.even = bf16[384,384]{1,0:T(8,128)(2,1)S(1)} collective-permute-done((bf16[384,384]{1,0:T(8,128)(2,1)S(1)}, bf16[384,384]{1,0:T(8,128)(2,1)S(1)}, u32[]{:S(2)}, u32[]{:S(2)}) %collective-permute-start.6) | collective-permute-done | bytes 294944 | tf_op jit(solution)/shard_map/ppermute | solution.py:19
  82.5 2.0 %collective-permute-start.9 = (bf16[2,768,384]{2,1,0:T(8,128)(2,1)S(1)}, bf16[2,768,384]{2,1,0:T(8,128)(2,1)S(1)}, u32[]{:S(2)}, u32[]{:S(2)}) collective-permute-start(bf16[2,768,384]{2,1,0:T(8,128)(2,1)S(1)} %get-tuple-element.39), channel_id=1, source_target_pairs={{0,4},{4,0},{8,12},{12,8},{16,20},{20,16},{24,28},{28,24},{32,36},... | collective-permute-start | bytes 3538952 | tf_op jit(solution)/shard_map/ppermute | solution.py:19
  84.6 1.9 %collective-permute-start.7 = (bf16[384,384]{1,0:T(8,128)(2,1)S(1)}, bf16[384,384]{1,0:T(8,128)(2,1)S(1)}, u32[]{:S(2)}, u32[]{:S(2)}) collective-permute-start(bf16[384,384]{1,0:T(8,128)(2,1)S(1)} %get-tuple-element.35), channel_id=1, source_target_pairs={{16,32},{32,16},{20,36},{36,20},{24,40},{40,24},{28,44},{44,28},{4... | collective-permute-start | bytes 884744 | tf_op jit(solution)/shard_map/ppermute | solution.py:19
  86.5 0.8 collective-permute-done.9.sib
  87.3 0.2 lend.1
  87.4 1.9 %collective-permute-start.10 = (bf16[768,384]{1,0:T(8,128)(2,1)S(1)}, bf16[768,384]{1,0:T(8,128)(2,1)S(1)}, u32[]{:S(2)}, u32[]{:S(2)}) collective-permute-start(bf16[768,384]{1,0:T(8,128)(2,1)S(1)} %lend.1), channel_id=1, source_target_pairs={{0,8},{4,12},{8,0},{12,4},{16,24},{20,28},{24,16},{28,20},{32,40},... | collective-permute-start | bytes 1769480 | tf_op jit(solution)/shard_map/ppermute | solution.py:19
  89.4 13.9 %collective-permute-done.7.odd = bf16[384,384]{1,0:T(8,128)(2,1)S(1)} collective-permute-done((bf16[384,384]{1,0:T(8,128)(2,1)S(1)}, bf16[384,384]{1,0:T(8,128)(2,1)S(1)}, u32[]{:S(2)}, u32[]{:S(2)}) %collective-permute-start.7) | collective-permute-done | bytes 294944 | tf_op jit(solution)/shard_map/ppermute | solution.py:19
  103.4 1.9 %collective-permute-start.8 = (bf16[192,384]{1,0:T(8,128)(2,1)S(1)}, bf16[192,384]{1,0:T(8,128)(2,1)S(1)}, u32[]{:S(2)}, u32[]{:S(2)}) collective-permute-start(bf16[192,384]{1,0:T(8,128)(2,1)S(1)} %get-tuple-element.37), channel_id=1, source_target_pairs={{0,8},{4,12},{8,0},{12,4},{16,24},{20,28},{24,16},{28,20},{32,40},... | collective-permute-start | bytes 442376 | tf_op jit(solution)/shard_map/ppermute | solution.py:19
  105.3 14.7 %collective-permute-done.8.got = bf16[192,384]{1,0:T(8,128)(2,1)S(1)} collective-permute-done((bf16[192,384]{1,0:T(8,128)(2,1)S(1)}, bf16[192,384]{1,0:T(8,128)(2,1)S(1)}, u32[]{:S(2)}, u32[]{:S(2)}) %collective-permute-start.8) | collective-permute-done | bytes 147488 | tf_op jit(solution)/shard_map/ppermute | solution.py:19
  120.0 0.8 place.1
  120.8 1.0 close.1
  (15 shorter events, 0.2 us)
Async XLA Ops:
  0.6 1.0 copy-start
  1.6 1.0 copy-start.1
  2.6 0.7 copy-start.4
  3.2 0.7 copy-start.5
  4.1 10.3 %collective-permute-start = (bf16[416,384]{1,0:T(8,128)(2,1)S(1)}, bf16[416,384]{1,0:T(8,128)(2,1)S(1)}, u32[]{:S(2)}, u32[]{:S(2)}) collective-permute-start(bf16[416,384]{1,0:T(8,128)(2,1)S(1)} %get-tuple-element.23), channel_id=1, source_target_pairs={{0,8},{4,12},{8,0},{12,4},{16,24},{20,28},{24,16},{28,20},{32,40},... | collective-permute-start | bytes 958472 | tf_op jit(solution)/shard_map/ppermute | solution.py:19
  6.0 1.0 copy-start.2
  6.9 1.0 copy-start.3
  8.0 48.8 %copy-start.6 = (s32[32,4,3]{0,1,2:T(4,128)S(1)}, s32[32,4,3]{0,1,2:T(4,128)}, u32[]{:S(2)}) copy-start(s32[32,4,3]{0,1,2:T(4,128)} %param.13) | copy-start | bytes 4612
  8.0 45.0 %collective-permute-start.2 = (bf16[768,384]{1,0:T(8,128)(2,1)S(1)}, bf16[768,384]{1,0:T(8,128)(2,1)S(1)}, u32[]{:S(2)}, u32[]{:S(2)}) collective-permute-start(bf16[768,384]{1,0:T(8,128)(2,1)S(1)} %stack.1.kv_a), channel_id=1, source_target_pairs={{0,8},{4,12},{8,0},{12,4},{16,24},{20,28},{24,16},{28,20},{32,40},... | collective-permute-start | bytes 1769480 | tf_op jit(solution)/shard_map/ppermute | solution.py:19
  14.4 52.1 %collective-permute-start.5 = (bf16[800,384]{1,0:T(8,128)(2,1)S(1)}, bf16[800,384]{1,0:T(8,128)(2,1)S(1)}, u32[]{:S(2)}, u32[]{:S(2)}) collective-permute-start(bf16[800,384]{1,0:T(8,128)(2,1)S(1)} %join.1.pack), channel_id=1, source_target_pairs={{0,16},{16,0},{4,20},{20,4},{8,24},{24,8},{12,28},{28,12},{32,48},... | collective-permute-start | bytes 1843208 | tf_op jit(solution)/shard_map/ppermute | solution.py:19
  17.6 56.9 %collective-permute-start.4 = (bf16[800,384]{1,0:T(8,128)(2,1)S(1)}, bf16[800,384]{1,0:T(8,128)(2,1)}, u32[]{:S(2)}, u32[]{:S(2)}) collective-permute-start(bf16[800,384]{1,0:T(8,128)(2,1)S(1)} %join.1.pack), channel_id=1, source_target_pairs={{16,32},{32,16},{20,36},{36,20},{24,40},{40,24},{28,44},{44,28},{4... | collective-permute-start | bytes 1843208 | tf_op jit(solution)/shard_map/ppermute | solution.py:19
  20.7 36.2 %collective-permute-start.1 = (bf16[768,384]{1,0:T(8,128)(2,1)S(1)}, bf16[768,384]{1,0:T(8,128)(2,1)S(1)}, u32[]{:S(2)}, u32[]{:S(2)}) collective-permute-start(bf16[768,384]{1,0:T(8,128)(2,1)S(1)} %stack.1.kv_a), channel_id=1, source_target_pairs={{0,4},{4,0},{8,12},{12,8},{16,20},{20,16},{24,28},{28,24},{32,36},... | collective-permute-start | bytes 1769480 | tf_op jit(solution)/shard_map/ppermute | solution.py:19
  53.0 5.5 %collective-permute-start.3 = (bf16[768,384]{1,0:T(8,128)(2,1)S(1)}, bf16[768,384]{1,0:T(8,128)(2,1)}, u32[]{:S(2)}, u32[]{:S(2)}) collective-permute-start(bf16[768,384]{1,0:T(8,128)(2,1)S(1)} %collective-permute-done.2.kv_c), channel_id=1, source_target_pairs={{0,4},{4,0},{8,12},{12,8},{16,20},{20,16},{24,28},{28,24},{32,36},... | collective-permute-start | bytes 1769480 | tf_op jit(solution)/shard_map/ppermute | solution.py:19
  72.5 10.0 %collective-permute-start.6 = (bf16[384,384]{1,0:T(8,128)(2,1)S(1)}, bf16[384,384]{1,0:T(8,128)(2,1)S(1)}, u32[]{:S(2)}, u32[]{:S(2)}) collective-permute-start(bf16[384,384]{1,0:T(8,128)(2,1)S(1)} %get-tuple-element.33), channel_id=1, source_target_pairs={{0,16},{16,0},{4,20},{20,4},{8,24},{24,8},{12,28},{28,12},{32,48},... | collective-permute-start | bytes 884744 | tf_op jit(solution)/shard_map/ppermute | solution.py:19
  82.5 4.7 %collective-permute-start.9 = (bf16[2,768,384]{2,1,0:T(8,128)(2,1)S(1)}, bf16[2,768,384]{2,1,0:T(8,128)(2,1)S(1)}, u32[]{:S(2)}, u32[]{:S(2)}) collective-permute-start(bf16[2,768,384]{2,1,0:T(8,128)(2,1)S(1)} %get-tuple-element.39), channel_id=1, source_target_pairs={{0,4},{4,0},{8,12},{12,8},{16,20},{20,16},{24,28},{28,24},{32,36},... | collective-permute-start | bytes 3538952 | tf_op jit(solution)/shard_map/ppermute | solution.py:19
  84.6 18.7 %collective-permute-start.7 = (bf16[384,384]{1,0:T(8,128)(2,1)S(1)}, bf16[384,384]{1,0:T(8,128)(2,1)S(1)}, u32[]{:S(2)}, u32[]{:S(2)}) collective-permute-start(bf16[384,384]{1,0:T(8,128)(2,1)S(1)} %get-tuple-element.35), channel_id=1, source_target_pairs={{16,32},{32,16},{20,36},{36,20},{24,40},{40,24},{28,44},{44,28},{4... | collective-permute-start | bytes 884744 | tf_op jit(solution)/shard_map/ppermute | solution.py:19
  87.4 33.4 %collective-permute-start.10 = (bf16[768,384]{1,0:T(8,128)(2,1)S(1)}, bf16[768,384]{1,0:T(8,128)(2,1)S(1)}, u32[]{:S(2)}, u32[]{:S(2)}) collective-permute-start(bf16[768,384]{1,0:T(8,128)(2,1)S(1)} %lend.1), channel_id=1, source_target_pairs={{0,8},{4,12},{8,0},{12,4},{16,24},{20,28},{24,16},{28,20},{32,40},... | collective-permute-start | bytes 1769480 | tf_op jit(solution)/shard_map/ppermute | solution.py:19
  103.4 16.6 %collective-permute-start.8 = (bf16[192,384]{1,0:T(8,128)(2,1)S(1)}, bf16[192,384]{1,0:T(8,128)(2,1)S(1)}, u32[]{:S(2)}, u32[]{:S(2)}) collective-permute-start(bf16[192,384]{1,0:T(8,128)(2,1)S(1)} %get-tuple-element.37), channel_id=1, source_target_pairs={{0,8},{4,12},{8,0},{12,4},{16,24},{20,28},{24,16},{28,20},{32,40},... | collective-permute-start | bytes 442376 | tf_op jit(solution)/shard_map/ppermute | solution.py:19

commit v5 on v4

v5 whole, which is shorter than its diff:
```python
import functools

import jax
import jax.numpy as jnp
from jax import lax
from jax.experimental import pallas as pl
from jax.experimental.pallas import tpu as pltpu
from jax.sharding import PartitionSpec as P

LOG2E = 1.4426950408889634
HEAD = 128
RING = 8
AUX = 32
NEVER = 1e30
BF = jnp.bfloat16
F32 = jnp.float32


def send(block, pairs):
    return lax.ppermute(block, ("tm", "space"), pairs)


def routes(time_all):
    at = lambda t, c, w: t * 4 + c * 2 + w
    every = [(t, c, w) for t in range(time_all) for c in range(2) for w in range(2)]
    both = lambda a, b: [(a, b), (b, a)]
    even, odd, cross, lift = [], [], [], []
    for t, c, w in every:
        if t + 1 >= time_all:
            continue
        if (t + 1) % RING:
            (odd if t % 2 else even).extend(both(at(t, c, w), at(t + 1, c, w)))
        elif c:
            cross += both(at(t, 1, w), at(t + 1, 0, w))
            lift += [(at(t, 0, w), at(t, 1, w)), (at(t + 1, 1, w), at(t + 1, 0, w))]
    core = [(at(t, c, w), at(t, c, 1 - w)) for t, c, w in every]
    pair = [(at(t, c, w), at(t, 1 - c, w)) for t, c, w in every]
    home = [(a, b ^ 2) for a, b in cross]
    return core, pair, even, odd, cross, lift, home


def position(time_all):
    time_pos, frame_pos = lax.axis_index("tm"), lax.axis_index("space")
    chip, core = frame_pos // 2, frame_pos % 2
    low = (time_pos % RING == 0) & (time_pos > 0)
    high = (time_pos % RING == RING - 1) & (time_pos < time_all - 1)
    return time_pos, chip, core, low | high, (low & (chip == 0)) | (high & (chip == 1))


def pack_kernel(half, query, grad, norm, delta, pack, msg, extra, whole, q, g, n, d, sems):
    copies = [pltpu.make_async_copy(a, b, sems.at[i]) for i, (a, b) in enumerate(((query, q), (grad, g), (norm, n), (delta, d)))]
    for copy in copies:
        copy.start()
    for copy in copies:
        copy.wait()
    chip = lax.axis_index("space") // 2
    rows = 2 * half
    keep = pl.ds(pl.multiple_of(chip * half, half), half)
    give = pl.ds(pl.multiple_of((1 - chip) * half, half), half)
    pieces = []
    for ref in (n, d):
        x = ref[:, 0, :]
        high = x.astype(BF)
        rest = x - high.astype(F32)
        mid = rest.astype(BF)
        pieces += [high.astype(F32), mid.astype(F32), rest - mid.astype(F32)]
    heads, _, channels = norm.shape
    pieces.append(jnp.zeros((AUX - 6 * heads, channels), F32))
    aux = jnp.concatenate(pieces)
    turned = jnp.concatenate([aux[:, half:], aux[:, :half]], axis=1)
    whole[2 * rows :] = aux.astype(BF)
    aux = jnp.where(chip == 0, aux, turned).astype(BF)
    whole[0:rows] = q[...]
    whole[rows : 2 * rows] = g[...]
    pack[0:half] = q[keep]
    pack[rows : rows + half] = g[keep]
    pack[2 * rows :] = aux
    msg[0:half] = q[give]
    msg[half:rows] = g[give]
    msg[rows:] = aux
    extra[0:half] = q[keep]
    extra[half:rows] = g[keep]
    extra[rows:] = aux


def join_kernel(half, msg, pack_in, pack):
    rows = 2 * half
    pack[0:half] = pack_in[0:half]
    pack[rows : rows + half] = pack_in[rows : rows + half]
    pack[half:rows] = msg[0:half]
    pack[rows + half : 2 * rows] = msg[half:rows]
    lane = lax.broadcasted_iota(jnp.int32, (AUX, pack.shape[1]), 1)
    own, got = pack_in[2 * rows :].astype(F32), msg[rows:].astype(F32)
    pack[2 * rows :] = jnp.where(lane < half, own, got).astype(BF)


def odd_join_kernel(half, time_all, msg, extra, pack, out):
    rows = 2 * half
    _, chip, _, _, inner = position(time_all)

    @pl.when(jnp.logical_not(inner))
    def _():
        out[...] = pack[...]

    @pl.when(inner)
    def _():
        for ref, part in ((msg, chip), (extra, 1 - chip)):
            out[pl.ds(pl.multiple_of(part * half, half), half)] = ref[0:half]
            out[pl.ds(pl.multiple_of(rows + part * half, half), half)] = ref[half:rows]
        aux = msg[rows:].astype(F32)
        turned = jnp.concatenate([aux[:, half:], aux[:, :half]], axis=1)
        out[2 * rows :] = jnp.where(chip == 1, aux, turned).astype(BF)


def stack_kernel(rows, key, value, out):
    out[0:rows] = key[...]
    out[rows:] = value[...]


def seen(extents, time_all, kind):
    time_pos, chip, core, end, inner = position(time_all)
    toward = 2 * (time_pos % 2) - 1
    when = time_pos + {"own": 0, "even": -toward, "odd": toward, "cross": toward}[kind]
    heights = [chip, 1 - chip]
    inside = (when >= 0) & (when < time_all)
    if kind == "odd":
        inside = inside & (jnp.logical_not(end) | inner)
        heights = [jnp.where(end, chip, height) for height in heights]
    if kind == "cross":
        inside = inside & inner
        heights = [1 - chip, 1 - chip]
    place = jnp.clip(when, 0, time_all - 1)
    gap = jnp.abs(when - time_pos)

    def flag(j, part):
        extent = [extents[place, heights[part] * 2 + core, i] for i in range(3)]
        height_gap = jnp.abs(jnp.where(j >= 2, 1 - chip, chip) - heights[part])
        return inside & (gap <= extent[0]) & (height_gap <= extent[1]) & (j % 2 <= extent[2])

    return flag


def row_terms(pack, rows, heads):
    aux = pack[2 * rows :, :].astype(F32)
    row = lambda i: aux[i * heads : (i + 1) * heads]
    return jnp.concatenate([(row(0) + (row(1) + row(2))) * LOG2E, row(3) + (row(4) + row(5))])


def hidden(own, other, rows):
    first = lax.broadcasted_iota(jnp.int32, (1, rows), 1) < rows // 2
    return jnp.where(first, jnp.where(own, 0.0, NEVER), jnp.where(other, 0.0, NEVER))


def pair_terms(q, g, k, v, norm, delta, factor):
    last, first = (((1,), (1,)), ((), ())), (((0,), (0,)), ((), ()))
    st = lax.dot_general(k, q, last, preferred_element_type=F32)
    p = jnp.exp2(st * (factor * LOG2E) - norm)
    dp = lax.dot_general(v, g, last, preferred_element_type=F32)
    ds = (p * (dp - delta)).astype(BF)
    value_term = jnp.dot(p.astype(BF), g, preferred_element_type=F32)
    key_term = jnp.dot(ds, q, preferred_element_type=F32)
    return lax.dot_general(ds, k, first, preferred_element_type=F32), key_term, value_term


def own_kernel(factor, time_all, extents, pack, kv_a, kv_b, acc, dq, kv):
    rows, channels = dq.shape
    heads = channels // HEAD
    kv[0] = kv_a[...]
    kv[1] = kv_b[...]
    acc[...] = jnp.zeros_like(acc)
    dq[...] = jnp.zeros_like(dq)
    flag = seen(extents, time_all, "own")
    terms = row_terms(pack, rows, heads)

    def step(j, carry):
        own, other = flag(j, 0), flag(j, 1)

        @pl.when(own | other)
        def _():
            hide = hidden(own, other, rows)
            for h in range(heads):
                cols = slice(h * HEAD, (h + 1) * HEAD)
                query_term, key_term, value_term = pair_terms(
                    pack[0:rows, cols], pack[rows : 2 * rows, cols], kv[j, 0:rows, cols], kv[j, rows:, cols],
                    terms[h : h + 1] + hide, terms[heads + h : heads + h + 1], factor,
                )
                dq[:, cols] += query_term
                acc[j, 0:rows, cols] += key_term
                acc[j, rows:, cols] += value_term

        return carry

    lax.fori_loop(0, 2, step, 0)


def frame_kernel(factor, time_all, extents, even, cross, own, kv_a, kv_b, kv_c, kv_d, acc_in, dq_in,
                 acc, dq_own, dq_even, dq_cross, kv, packs, terms, hide, dq):
    rows, channels = dq_own.shape
    heads = channels // HEAD
    for i, ref in enumerate((kv_a, kv_b, kv_c, kv_d)):
        kv[i] = ref[...]
    for i, ref in enumerate((even, cross, own)):
        packs[i] = ref[0 : 2 * rows]
        terms[i, 0 : 2 * heads] = row_terms(ref, rows, heads)
    acc[0:2] = acc_in[...]
    acc[2:4] = jnp.zeros_like(acc[2:4])
    dq[0:2] = jnp.zeros_like(dq[0:2])
    dq[2] = dq_in[...]
    see = [seen(extents, time_all, kind) for kind in ("even", "cross", "own")]

    def add(j, members):
        each = lambda pick, axis: jnp.concatenate([pick(m) for m in members], axis=axis) if len(members) > 1 else pick(members[0])
        for h in range(heads):
            cols = slice(h * HEAD, (h + 1) * HEAD)
            query_term, key_term, value_term = pair_terms(
                each(lambda m: packs[m, 0:rows, cols], 0), each(lambda m: packs[m, rows:, cols], 0),
                kv[j, 0:rows, cols], kv[j, rows:, cols],
                each(lambda m: terms[m, h : h + 1] + hide[m, 0:1], 1),
                each(lambda m: terms[m, heads + h : heads + h + 1], 1), factor,
            )
            for i, m in enumerate(members):
                dq[m, :, cols] += query_term[i * rows : (i + 1) * rows]
            acc[j, 0:rows, cols] += key_term
            acc[j, rows:, cols] += value_term

    def step(j, carry):
        on = []
        for i, flag in enumerate(see):
            parts = flag(j, 0), flag(j, 1)
            hide[i, 0:1] = hidden(*parts, rows)
            on.append(parts[0] | parts[1] if i < 2 else (parts[0] | parts[1]) & (j >= 2))
        count = sum(x.astype(jnp.int32) for x in on)
        one = jnp.where(on[0], 0, jnp.where(on[1], 1, 2))
        two = jnp.where(on[0] & on[1], 1, 2)

        @pl.when(count >= 2)
        def _():
            add(j, [one, two])

        @pl.when(count % 2 == 1)
        def _():
            add(j, [jnp.where(count == 3, 2, one)])

        return carry

    lax.fori_loop(0, 4, step, 0)
    dq_own[...] = dq[2] * factor
    dq_even[...] = (dq[0] * factor).astype(BF)
    dq_cross[...] = (dq[1] * factor).astype(BF)


def odd_kernel(factor, time_all, extents, pack, kv, acc_in, dq_out, own, lent, sib, acc, dq):
    rows, channels = dq.shape
    heads = channels // HEAD
    dq[...] = jnp.zeros_like(dq)
    flag = seen(extents, time_all, "odd")
    terms = row_terms(pack, rows, heads)

    def step(j, carry):
        first, second = flag(j, 0), flag(j, 1)

        @pl.when(jnp.logical_not(first | second))
        def _():
            acc[j] = acc_in[j]

        @pl.when(first | second)
        def _():
            hide = hidden(first, second, rows)
            for h in range(heads):
                cols = slice(h * HEAD, (h + 1) * HEAD)
                query_term, key_term, value_term = pair_terms(
                    pack[0:rows, cols], pack[rows : 2 * rows, cols], kv[j, 0:rows, cols], kv[j, rows:, cols],
                    terms[h : h + 1] + hide, terms[heads + h : heads + h + 1], factor,
                )
                dq[:, cols] += query_term
                acc[j, 0:rows, cols] = acc_in[j, 0:rows, cols] + key_term
                acc[j, rows:, cols] = acc_in[j, rows:, cols] + value_term

        return carry

    lax.fori_loop(0, 4, step, 0)
    dq_out[...] = (dq[...] * factor).astype(BF)
    own[0:rows] = acc[0, 0:rows] * factor
    own[rows:] = acc[0, rows:]
    lent[0:rows] = acc[2, 0:rows] * factor
    lent[rows:] = acc[2, rows:]
    for i, j in enumerate((1, 3)):
        sib[i, 0:rows] = (acc[j, 0:rows] * factor).astype(BF)
        sib[i, rows:] = acc[j, rows:].astype(BF)


def sum_kernel(half, own, even, odd, mine, msg):
    total = own[...] + even[...].astype(F32) + odd[...].astype(F32)
    mine[...] = total[:half]
    msg[...] = total[half:].astype(BF)


def settle_kernel(cross, far, out):
    out[...] = cross[...].astype(F32) + far[...].astype(F32)


def place_kernel(half, mine, got, ended, out):
    chip = lax.axis_index("space") // 2
    for ref, part in ((mine, chip), (got, 1 - chip)):
        at = pl.ds(pl.multiple_of(part * half, half), half)
        out[at] = (ref[...].astype(F32) + ended[at]).astype(BF)


def lend_kernel(lent, sib, out):
    out[...] = (lent[...] + sib[1].astype(F32)).astype(BF)


def close_kernel(rows, own, sib, given, key, value):
    total = own[...] + sib[0].astype(F32) + given[...].astype(F32)
    key[...] = total[:rows].astype(BF)
    value[...] = total[rows:].astype(BF)


def call(kernel, shapes, operands, micros, name, scratch=(), scalars=0):
    whole = pl.BlockSpec(memory_space=pltpu.VMEM)
    return pl.pallas_call(
        kernel,
        out_shape=shapes,
        in_specs=[pl.BlockSpec(memory_space=pltpu.SMEM)] * scalars + [whole] * (len(operands) - scalars),
        out_specs=[whole] * len(shapes),
        scratch_shapes=scratch,
        compiler_params=pltpu.CompilerParams(vmem_limit_bytes=24 * 2**20),
        cost_estimate=pl.CostEstimate(flops=micros * 10**9 + 1000, bytes_accessed=1000, transcendentals=0),
        name=name,
    )(*operands)


def body(query_tiles, key_tiles, value_tiles, grad_output, log_norm, row_delta, extents):
    rows, channels = query_tiles.shape[2:]
    heads, half = log_norm.shape[2], rows // 2
    factor = (channels // heads) ** (-0.5)
    time_all = lax.axis_size("tm")
    core, pair, even, odd, cross, lift, home = routes(time_all)
    out = jax.ShapeDtypeStruct
    tile, two, packet, part = (rows, channels), (2 * rows, channels), (2 * rows + AUX, channels), (rows + AUX, channels)
    lanes = (heads, 1, rows)

    pack, msg, extra, whole = pl.pallas_call(
        functools.partial(pack_kernel, half),
        out_shape=[out(packet, BF), out(part, BF), out(part, BF), out(packet, BF)],
        in_specs=[pl.BlockSpec(memory_space=pl.ANY)] * 4,
        out_specs=[pl.BlockSpec(memory_space=pltpu.VMEM)] * 4,
        scratch_shapes=[pltpu.VMEM(tile, BF)] * 2 + [pltpu.VMEM(lanes, F32)] * 2 + [pltpu.SemaphoreType.DMA((4,))],
        compiler_params=pltpu.CompilerParams(vmem_limit_bytes=60 * 2**20),
        cost_estimate=pl.CostEstimate(flops=1000, bytes_accessed=1000, transcendentals=0),
        name="pack",
    )(query_tiles[0, 0], grad_output[0, 0], log_norm.reshape(lanes), row_delta.reshape(lanes))
    msg = send(msg, pair)
    extra = send(extra, lift)
    whole = send(whole, cross)
    pack, key, value = lax.optimization_barrier((pack, key_tiles[0, 0], value_tiles[0, 0]))
    (kv_a,) = call(functools.partial(stack_kernel, rows), [out(two, BF)], (key, value), 0, "stack")
    kv_b = send(kv_a, core)
    kv_a, msg = lax.optimization_barrier((kv_a, msg))
    kv_c = send(kv_a, pair)
    (pack,) = call(functools.partial(join_kernel, half), [out(packet, BF)], (msg, pack), 20, "join")
    even_pack = send(pack, even)

    with jax.named_scope("own"):
        acc, dq = call(
            functools.partial(own_kernel, factor, time_all),
            [out((2,) + two, F32), out(tile, F32)],
            (extents, pack, kv_a, kv_b), 0, "own", [pltpu.VMEM((2,) + two, BF)], scalars=1,
        )
    extra, whole, dq = lax.optimization_barrier((extra, whole, dq))
    (odd_pack,) = call(functools.partial(odd_join_kernel, half, time_all), [out(packet, BF)], (msg, extra, pack), 100, "odd_join")
    odd_pack = send(odd_pack, odd + cross)
    kv_c, dq = lax.optimization_barrier((kv_c, dq))
    kv_d = send(kv_c, core)
    with jax.named_scope("frame"):
        acc, dq, even_dq, cross_dq, kv = call(
            functools.partial(frame_kernel, factor, time_all),
            [out((4,) + two, F32), out(tile, F32), out(tile, BF), out(tile, BF), out((4,) + two, BF)],
            (extents, even_pack, whole, pack, kv_a, kv_b, kv_c, kv_d, acc, dq), 0, "frame",
            [pltpu.VMEM((3,) + two, BF), pltpu.VMEM((3, 8, rows), F32), pltpu.VMEM((3, 8, rows), F32), pltpu.VMEM((3,) + tile, F32)],
            scalars=1,
        )
    with jax.named_scope("odd"):
        odd_dq, own, lent, sib = call(
            functools.partial(odd_kernel, factor, time_all),
            [out(tile, BF), out(two, F32), out(two, F32), out((2,) + two, BF)],
            (extents, odd_pack, kv, acc), 20, "odd", [pltpu.VMEM((4,) + two, F32), pltpu.VMEM(tile, F32)], scalars=1,
        )
    far_back = send(odd_dq, home)
    odd_back = send(odd_dq, odd)
    even_back = send(even_dq, even)
    cross_back = send(cross_dq, cross)
    sib, even_back, cross_back = lax.optimization_barrier((sib, even_back, cross_back))
    sib = send(sib, core)
    (lent,) = call(lend_kernel, [out(two, BF)], (lent, sib), 0, "lend")
    given = send(lent, pair)
    mine, msg = call(
        functools.partial(sum_kernel, half),
        [out((half, channels), F32), out((half, channels), BF)], (dq, even_back, odd_back), 20, "sum"
    )
    msg = send(msg, pair)
    (ended,) = call(settle_kernel, [out(tile, F32)], (cross_back, far_back), 100, "settle")
    (grad_query,) = call(functools.partial(place_kernel, half), [out(tile, BF)], (mine, msg, ended), 0, "place")
    grad_key, grad_value = call(functools.partial(close_kernel, rows), [out(tile, BF)] * 2, (own, sib, given), 0, "close")
    shape = (1, 1, rows, channels)
    return grad_query.reshape(shape), grad_key.reshape(shape), grad_value.reshape(shape)


def solution(mesh):
    tiles, per_row = P("tm", "space", None, "heads"), P("tm", "space", "heads", None)
    return jax.shard_map(
        body,
        mesh=mesh,
        in_specs=(tiles, tiles, tiles, tiles, per_row, per_row, P()),
        out_specs=(tiles, tiles, tiles),
        check_vma=False,
    )
```

time: 122 us -> 93.4 us (0.77)
  the two profiles are of different devices: /device:TPU:193 before, /device:TPU:190 now
where the time goes in v5:
time: 93.4 us; the launch traced here: 92.9 us
  starting transfers between devices  43.5 us (47%)
  waiting for transfers between devices  27.8 us (30%)
  Pallas kernels  18.7 us (20%)
  local copies, waits for them, and re-layouts  2.04 us (2%)
    ppermute x15, starting transfers between devices, send(): return lax.ppermute(block, ('tm', 'space'), pairs)  43.5 us
    ppermute x15, waiting for transfers between devices, send(): return lax.ppermute(block, ('tm', 'space'), pairs)  27.8 us
    pallas_call x11, Pallas kernels, call(): pl.pallas_call(kernel, out_shape=shapes, in_specs=[pl.BlockSpec(memory_sp...  16.2 us
    pallas_call x1, Pallas kernels, body(): pl.pallas_call(functools.partial(pack_kernel, half), out_shape=[out(packe...  2.51 us
    unnamed x9, local copies, waits for them, and re-layouts  2.04 us
  transfers between devices with their start and end apart: 15, of which 6 were waited for; matrix products, arithmetic and copies ran while one was open for 0% of the time, Pallas kernels for 16%

profile of v5, /device:TPU:190, one launch (start us, length us, event | category | flops | bytes accessed | tf_op | source)
XLA Modules:
  0.0 92.9 jit_solution(3118308186394017434)
XLA Ops:
  0.6 2.5 %pack.1 = (bf16[800,384]{1,0:T(8,128)(2,1)}, bf16[416,384]{1,0:T(8,128)(2,1)}, bf16[416,384]{1,0:T(8,128)(2,1)}, bf16[800,384]{1,0:T(8,128)(2,1)}) custom-call(bf16[384,384]{1,0:T(8,128)(2,1)} %bitcast.11, bf16[384,384]{1,0:T(8,128)(2,1)} %bitcast.12, f32[3,1,384]{2,1,0:T(1,128)} %bitcast.14, f32[3,1,384]{2,1,0:T(1,128)} %bitcast.15), custom_call_target="tpu_custom_call" | custom-call | flops 1000 | bytes 1000 | tf_op jit(solution)/shard_map/pack/pallas_call | solution.py:343
  3.2 4.3 %collective-permute-start = (bf16[416,384]{1,0:T(8,128)(2,1)}, bf16[416,384]{1,0:T(8,128)(2,1)S(1)}, u32[]{:S(2)}, u32[]{:S(2)}) collective-permute-start(bf16[416,384]{1,0:T(8,128)(2,1)} %get-tuple-element.38), channel_id=1, source_target_pairs={{0,8},{4,12},{8,0},{12,4},{16,24},{20,28},{24,16},{28,20},{32,40},... | collective-permute-start | bytes 958472 | tf_op jit(solution)/shard_map/ppermute | solution.py:20
  7.4 1.9 %collective-permute-start.2 = (bf16[416,384]{1,0:T(8,128)(2,1)}, bf16[416,384]{1,0:T(8,128)(2,1)S(1)}, u32[]{:S(2)}, u32[]{:S(2)}) collective-permute-start(bf16[416,384]{1,0:T(8,128)(2,1)} %get-tuple-element.41), channel_id=1, source_target_pairs={{112,120},{136,128},{116,124},{140,132},{240,248},{264,256},{244,2... | collective-permute-start | bytes 958472 | tf_op jit(solution)/shard_map/ppermute | solution.py:20
  9.4 1.0 %copy-done = bf16[1,1,384,384]{3,2,1,0:T(8,128)(2,1)S(1)} copy-done((bf16[1,1,384,384]{3,2,1,0:T(8,128)(2,1)S(1)}, bf16[1,1,384,384]{3,2,1,0:T(8,128)(2,1)}, u32[]{:S(2)}) %copy-start) | copy-done | bytes 294936
  10.4 1.0 %copy-done.1 = bf16[1,1,384,384]{3,2,1,0:T(8,128)(2,1)S(1)} copy-done((bf16[1,1,384,384]{3,2,1,0:T(8,128)(2,1)S(1)}, bf16[1,1,384,384]{3,2,1,0:T(8,128)(2,1)}, u32[]{:S(2)}) %copy-start.1) | copy-done | bytes 294936
  11.4 2.1 %collective-permute-start.4 = (bf16[768,384]{1,0:T(8,128)(2,1)S(1)}, bf16[768,384]{1,0:T(8,128)(2,1)S(1)}, u32[]{:S(2)}, u32[]{:S(2)}) collective-permute-start(bf16[768,384]{1,0:T(8,128)(2,1)S(1)} %stack.1.kv_a), channel_id=1, source_target_pairs={{0,4},{4,0},{8,12},{12,8},{16,20},{20,16},{24,28},{28,24},{32,36},... | collective-permute-start | bytes 1769480 | tf_op jit(solution)/shard_map/ppermute | solution.py:20
  13.4 0.7 collective-permute-start.3
  14.1 0.1 copy.11.extents
  14.3 1.4 %collective-permute-done.msg = bf16[416,384]{1,0:T(8,128)(2,1)S(1)} collective-permute-done((bf16[416,384]{1,0:T(8,128)(2,1)}, bf16[416,384]{1,0:T(8,128)(2,1)S(1)}, u32[]{:S(2)}, u32[]{:S(2)}) %collective-permute-start) | collective-permute-done | bytes 319520 | tf_op jit(solution)/shard_map/ppermute | solution.py:20
  15.7 5.3 %collective-permute-start.5 = (bf16[768,384]{1,0:T(8,128)(2,1)S(1)}, bf16[768,384]{1,0:T(8,128)(2,1)S(1)}, u32[]{:S(2)}, u32[]{:S(2)}) collective-permute-start(bf16[768,384]{1,0:T(8,128)(2,1)S(1)} %stack.1.kv_a), channel_id=1, source_target_pairs={{0,8},{4,12},{8,0},{12,4},{16,24},{20,28},{24,16},{28,20},{32,40},... | collective-permute-start | bytes 1769480 | tf_op jit(solution)/shard_map/ppermute | solution.py:20
  21.1 1.9 %collective-permute-start.1 = (bf16[800,384]{1,0:T(8,128)(2,1)S(1)}, bf16[800,384]{1,0:T(8,128)(2,1)S(1)}, u32[]{:S(2)}, u32[]{:S(2)}) collective-permute-start(bf16[800,384]{1,0:T(8,128)(2,1)S(1)} %join.1.pack.own), channel_id=1, source_target_pairs={{0,16},{16,0},{4,20},{20,4},{8,24},{24,8},{12,28},{28,12},{32,48},... | collective-permute-start | bytes 1843208 | tf_op jit(solution)/shard_map/ppermute | solution.py:20
  23.0 4.7 %own.1 = (f32[2,768,384]{2,1,0:T(8,128)S(1)}, f32[384,384]{1,0:T(8,128)S(1)}) custom-call(s32[32,4,3]{2,1,0:T(4,128)S(1)} %copy.11.extents, bf16[800,384]{1,0:T(8,128)(2,1)S(1)} %join.1.pack.own, bf16[768,384]{1,0:T(8,128)(2,1)S(1)} %stack.1.kv_a, bf16[768,384]{1,0:T(8,128)(2,1)S(1)} %collective-permute-done.4.kv_b), custom_call_target="tpu_custom_call" | custom-call | flops 1000 | bytes 1000 | tf_op jit(solution)/shard_map/own/own/pallas_call | solution.py:321
  27.9 0.7 collective-permute-start.7
  28.6 6.1 %collective-permute-done.5.kv_c = bf16[768,384]{1,0:T(8,128)(2,1)S(1)} collective-permute-done((bf16[768,384]{1,0:T(8,128)(2,1)S(1)}, bf16[768,384]{1,0:T(8,128)(2,1)S(1)}, u32[]{:S(2)}, u32[]{:S(2)}) %collective-permute-start.5) | collective-permute-done | bytes 589856 | tf_op jit(solution)/shard_map/ppermute | solution.py:20
  34.7 1.9 %collective-permute-start.6 = (bf16[768,384]{1,0:T(8,128)(2,1)S(1)}, bf16[768,384]{1,0:T(8,128)(2,1)S(1)}, u32[]{:S(2)}, u32[]{:S(2)}) collective-permute-start(bf16[768,384]{1,0:T(8,128)(2,1)S(1)} %collective-permute-done.5.kv_c), channel_id=1, source_target_pairs={{0,4},{4,0},{8,12},{12,8},{16,20},{20,16},{24,28},{28,24},{32,36},... | collective-permute-start | bytes 1769480 | tf_op jit(solution)/shard_map/ppermute | solution.py:20
  36.6 2.1 %collective-permute-done.1.even = bf16[800,384]{1,0:T(8,128)(2,1)S(1)} collective-permute-done((bf16[800,384]{1,0:T(8,128)(2,1)S(1)}, bf16[800,384]{1,0:T(8,128)(2,1)S(1)}, u32[]{:S(2)}, u32[]{:S(2)}) %collective-permute-start.1) | collective-permute-done | bytes 614432 | tf_op jit(solution)/shard_map/ppermute | solution.py:20
  38.7 6.7 %frame.1 = (f32[4,768,384]{2,1,0:T(8,128)S(1)}, f32[384,384]{1,0:T(8,128)S(1)}, bf16[384,384]{1,0:T(8,128)(2,1)S(1)}, bf16[384,384]{1,0:T(8,128)(2,1)S(1)}, bf16[4,768,384]{2,1,0:T(8,128)(2,1)S(1)}) custom-call(s32[32,4,3]{2,1,0:T(4,128)S(1)} %copy.11.extents, bf16[800,384]{1,0:T(8,128)(2,1)S(1)} %collective-permute-done.1.even, ...), custom_call_target="tpu_custom_call" | custom-call | flops 1000 | bytes 1000 | tf_op jit(solution)/shard_map/frame/frame/pallas_call | solution.py:321
  45.4 1.9 %collective-permute-start.8 = (bf16[384,384]{1,0:T(8,128)(2,1)S(1)}, bf16[384,384]{1,0:T(8,128)(2,1)S(1)}, u32[]{:S(2)}, u32[]{:S(2)}) collective-permute-start(bf16[384,384]{1,0:T(8,128)(2,1)S(1)} %get-tuple-element.55), channel_id=1, source_target_pairs={{0,16},{16,0},{4,20},{20,4},{8,24},{24,8},{12,28},{28,12},{32,48},... | collective-permute-start | bytes 884744 | tf_op jit(solution)/shard_map/ppermute | solution.py:20
  47.3 0.7 collective-permute-start.9
  48.0 2.5 %odd.1 = (bf16[384,384]{1,0:T(8,128)(2,1)S(1)}, f32[768,384]{1,0:T(8,128)S(1)}, f32[768,384]{1,0:T(8,128)S(1)}, bf16[2,768,384]{2,1,0:T(8,128)(2,1)S(1)}) custom-call(s32[32,4,3]{2,1,0:T(4,128)S(1)} %copy.11.extents, bf16[800,384]{1,0:T(8,128)(2,1)S(1)} %collective-permute-done.7.pack, bf16[4,768,384]{2,1,0:T(8,128)(2,1)S(1)} %get-tuple-element.52.kv, ...), custom_call_target="tpu_custom_call" | custom-call | flops 20000000000 | bytes 1000 | tf_op jit(solution)/shard_map/odd/odd/pallas_call | solution.py:321
  50.5 0.7 collective-permute-start.10
  51.2 1.3 %collective-permute-start.12 = (bf16[384,384]{1,0:T(8,128)(2,1)S(1)}, bf16[384,384]{1,0:T(8,128)(2,1)S(1)}, u32[]{:S(2)}, u32[]{:S(2)}) collective-permute-start(bf16[384,384]{1,0:T(8,128)(2,1)S(1)} %get-tuple-element.58), channel_id=1, source_target_pairs={{120,136},{128,112},{124,140},{132,116},{248,264},{256,240},{252,2... | collective-permute-start | bytes 884744 | tf_op jit(solution)/shard_map/ppermute | solution.py:20
  52.5 4.3 %collective-permute-done.8.even = bf16[384,384]{1,0:T(8,128)(2,1)S(1)} collective-permute-done((bf16[384,384]{1,0:T(8,128)(2,1)S(1)}, bf16[384,384]{1,0:T(8,128)(2,1)S(1)}, u32[]{:S(2)}, u32[]{:S(2)}) %collective-permute-start.8) | collective-permute-done | bytes 294944 | tf_op jit(solution)/shard_map/ppermute | solution.py:20
  56.8 2.1 %collective-permute-start.13 = (bf16[2,768,384]{2,1,0:T(8,128)(2,1)S(1)}, bf16[2,768,384]{2,1,0:T(8,128)(2,1)S(1)}, u32[]{:S(2)}, u32[]{:S(2)}) collective-permute-start(bf16[2,768,384]{2,1,0:T(8,128)(2,1)S(1)} %get-tuple-element.63), channel_id=1, source_target_pairs={{0,4},{4,0},{8,12},{12,8},{16,20},{20,16},{24,28},{28,24},{32,36},... | collective-permute-start | bytes 3538952 | tf_op jit(solution)/shard_map/ppermute | solution.py:20
  58.9 0.1 sum.1
  59.0 15.3 %collective-permute-start.11 = (bf16[192,384]{1,0:T(8,128)(2,1)S(1)}, bf16[192,384]{1,0:T(8,128)(2,1)S(1)}, u32[]{:S(2)}, u32[]{:S(2)}) collective-permute-start(bf16[192,384]{1,0:T(8,128)(2,1)S(1)} %get-tuple-element.60), channel_id=1, source_target_pairs={{0,8},{4,12},{8,0},{12,4},{16,24},{20,28},{24,16},{28,20},{32,40},... | collective-permute-start | bytes 442376 | tf_op jit(solution)/shard_map/ppermute | solution.py:20
  74.3 0.2 lend.1
  74.5 2.7 %collective-permute-start.14 = (bf16[768,384]{1,0:T(8,128)(2,1)S(1)}, bf16[768,384]{1,0:T(8,128)(2,1)S(1)}, u32[]{:S(2)}, u32[]{:S(2)}) collective-permute-start(bf16[768,384]{1,0:T(8,128)(2,1)S(1)} %lend.1), channel_id=1, source_target_pairs={{0,8},{4,12},{8,0},{12,4},{16,24},{20,28},{24,16},{28,20},{32,40},... | collective-permute-start | bytes 1769480 | tf_op jit(solution)/shard_map/ppermute | solution.py:20
  77.3 2.0 %collective-permute-done.11.got = bf16[192,384]{1,0:T(8,128)(2,1)S(1)} collective-permute-done((bf16[192,384]{1,0:T(8,128)(2,1)S(1)}, bf16[192,384]{1,0:T(8,128)(2,1)S(1)}, u32[]{:S(2)}, u32[]{:S(2)}) %collective-permute-start.11) | collective-permute-done | bytes 147488 | tf_op jit(solution)/shard_map/ppermute | solution.py:20
  79.3 0.8 place.1
  80.1 11.9 %collective-permute-done.14.given = bf16[768,384]{1,0:T(8,128)(2,1)S(1)} collective-permute-done((bf16[768,384]{1,0:T(8,128)(2,1)S(1)}, bf16[768,384]{1,0:T(8,128)(2,1)S(1)}, u32[]{:S(2)}, u32[]{:S(2)}) %collective-permute-start.14) | collective-permute-done | bytes 589856 | tf_op jit(solution)/shard_map/ppermute | solution.py:20
  91.9 1.0 %close.1 = (bf16[384,384]{1,0:T(8,128)(2,1)}, bf16[384,384]{1,0:T(8,128)(2,1)}) custom-call(f32[768,384]{1,0:T(8,128)S(1)} %get-tuple-element.62.own, bf16[2,768,384]{2,1,0:T(8,128)(2,1)S(1)} %collective-permute-done.13.sib, bf16[768,384]{1,0:T(8,128)(2,1)S(1)} %collective-permute-done.14.given), custom_call_target="tpu_custom_call" | custom-call | flops 1000 | bytes 1000 | tf_op jit(solution)/shard_map/close/pallas_call | solution.py:321
  (19 shorter events, 0.3 us)
Async XLA Ops:
  0.6 13.5 %copy-start.3 = (s32[32,4,3]{0,1,2:T(4,128)S(1)}, s32[32,4,3]{0,1,2:T(4,128)}, u32[]{:S(2)}) copy-start(s32[32,4,3]{0,1,2:T(4,128)} %param.13) | copy-start | bytes 4612
  3.2 12.5 %collective-permute-start = (bf16[416,384]{1,0:T(8,128)(2,1)}, bf16[416,384]{1,0:T(8,128)(2,1)S(1)}, u32[]{:S(2)}, u32[]{:S(2)}) collective-permute-start(bf16[416,384]{1,0:T(8,128)(2,1)} %get-tuple-element.38), channel_id=1, source_target_pairs={{0,8},{4,12},{8,0},{12,4},{16,24},{20,28},{24,16},{28,20},{32,40},... | collective-permute-start | bytes 958472 | tf_op jit(solution)/shard_map/ppermute | solution.py:20
  7.4 20.3 %collective-permute-start.2 = (bf16[416,384]{1,0:T(8,128)(2,1)}, bf16[416,384]{1,0:T(8,128)(2,1)S(1)}, u32[]{:S(2)}, u32[]{:S(2)}) collective-permute-start(bf16[416,384]{1,0:T(8,128)(2,1)} %get-tuple-element.41), channel_id=1, source_target_pairs={{112,120},{136,128},{116,124},{140,132},{240,248},{264,256},{244,2... | collective-permute-start | bytes 958472 | tf_op jit(solution)/shard_map/ppermute | solution.py:20
  9.4 1.0 %copy-start = (bf16[1,1,384,384]{3,2,1,0:T(8,128)(2,1)S(1)}, bf16[1,1,384,384]{3,2,1,0:T(8,128)(2,1)}, u32[]{:S(2)}) copy-start(bf16[1,1,384,384]{3,2,1,0:T(8,128)(2,1)} %param.8) | copy-start | bytes 884740
  10.4 1.0 %copy-start.1 = (bf16[1,1,384,384]{3,2,1,0:T(8,128)(2,1)S(1)}, bf16[1,1,384,384]{3,2,1,0:T(8,128)(2,1)}, u32[]{:S(2)}) copy-start(bf16[1,1,384,384]{3,2,1,0:T(8,128)(2,1)} %param.9) | copy-start | bytes 884740
  11.3 9.7 %copy-start.2 = (bf16[800,384]{1,0:T(8,128)(2,1)S(1)}, bf16[800,384]{1,0:T(8,128)(2,1)}, u32[]{:S(2)}) copy-start(bf16[800,384]{1,0:T(8,128)(2,1)} %get-tuple-element.40.pack_in) | copy-start | bytes 1843204
  11.4 11.6 %collective-permute-start.4 = (bf16[768,384]{1,0:T(8,128)(2,1)S(1)}, bf16[768,384]{1,0:T(8,128)(2,1)S(1)}, u32[]{:S(2)}, u32[]{:S(2)}) collective-permute-start(bf16[768,384]{1,0:T(8,128)(2,1)S(1)} %stack.1.kv_a), channel_id=1, source_target_pairs={{0,4},{4,0},{8,12},{12,8},{16,20},{20,16},{24,28},{28,24},{32,36},... | collective-permute-start | bytes 1769480 | tf_op jit(solution)/shard_map/ppermute | solution.py:20
  13.4 14.4 %collective-permute-start.3 = (bf16[800,384]{1,0:T(8,128)(2,1)}, bf16[800,384]{1,0:T(8,128)(2,1)S(1)}, u32[]{:S(2)}, u32[]{:S(2)}) collective-permute-start(bf16[800,384]{1,0:T(8,128)(2,1)} %get-tuple-element.42), channel_id=1, source_target_pairs={{120,128},{128,120},{124,132},{132,124},{248,256},{256,248},{252,2... | collective-permute-start | bytes 1843208 | tf_op jit(solution)/shard_map/ppermute | solution.py:20
  15.7 19.0 %collective-permute-start.5 = (bf16[768,384]{1,0:T(8,128)(2,1)S(1)}, bf16[768,384]{1,0:T(8,128)(2,1)S(1)}, u32[]{:S(2)}, u32[]{:S(2)}) collective-permute-start(bf16[768,384]{1,0:T(8,128)(2,1)S(1)} %stack.1.kv_a), channel_id=1, source_target_pairs={{0,8},{4,12},{8,0},{12,4},{16,24},{20,28},{24,16},{28,20},{32,40},... | collective-permute-start | bytes 1769480 | tf_op jit(solution)/shard_map/ppermute | solution.py:20
  21.1 17.6 %collective-permute-start.1 = (bf16[800,384]{1,0:T(8,128)(2,1)S(1)}, bf16[800,384]{1,0:T(8,128)(2,1)S(1)}, u32[]{:S(2)}, u32[]{:S(2)}) collective-permute-start(bf16[800,384]{1,0:T(8,128)(2,1)S(1)} %join.1.pack.own), channel_id=1, source_target_pairs={{0,16},{16,0},{4,20},{20,4},{8,24},{24,8},{12,28},{28,12},{32,48},... | collective-permute-start | bytes 1843208 | tf_op jit(solution)/shard_map/ppermute | solution.py:20
  27.9 20.1 %collective-permute-start.7 = (bf16[800,384]{1,0:T(8,128)(2,1)S(1)}, bf16[800,384]{1,0:T(8,128)(2,1)S(1)}, u32[]{:S(2)}, u32[]{:S(2)}) collective-permute-start(bf16[800,384]{1,0:T(8,128)(2,1)S(1)} %odd_join.1), channel_id=1, source_target_pairs={{16,32},{32,16},{20,36},{36,20},{24,40},{40,24},{28,44},{44,28},{4... | collective-permute-start | bytes 1843208 | tf_op jit(solution)/shard_map/ppermute | solution.py:20
  34.7 4.0 %collective-permute-start.6 = (bf16[768,384]{1,0:T(8,128)(2,1)S(1)}, bf16[768,384]{1,0:T(8,128)(2,1)S(1)}, u32[]{:S(2)}, u32[]{:S(2)}) collective-permute-start(bf16[768,384]{1,0:T(8,128)(2,1)S(1)} %collective-permute-done.5.kv_c), channel_id=1, source_target_pairs={{0,4},{4,0},{8,12},{12,8},{16,20},{20,16},{24,28},{28,24},{32,36},... | collective-permute-start | bytes 1769480 | tf_op jit(solution)/shard_map/ppermute | solution.py:20
  45.4 11.4 %collective-permute-start.8 = (bf16[384,384]{1,0:T(8,128)(2,1)S(1)}, bf16[384,384]{1,0:T(8,128)(2,1)S(1)}, u32[]{:S(2)}, u32[]{:S(2)}) collective-permute-start(bf16[384,384]{1,0:T(8,128)(2,1)S(1)} %get-tuple-element.55), channel_id=1, source_target_pairs={{0,16},{16,0},{4,20},{20,4},{8,24},{24,8},{12,28},{28,12},{32,48},... | collective-permute-start | bytes 884744 | tf_op jit(solution)/shard_map/ppermute | solution.py:20
  47.3 9.5 %collective-permute-start.9 = (bf16[384,384]{1,0:T(8,128)(2,1)S(1)}, bf16[384,384]{1,0:T(8,128)(2,1)S(1)}, u32[]{:S(2)}, u32[]{:S(2)}) collective-permute-start(bf16[384,384]{1,0:T(8,128)(2,1)S(1)} %get-tuple-element.56), channel_id=1, source_target_pairs={{120,128},{128,120},{124,132},{132,124},{248,256},{256,248},{252,2... | collective-permute-start | bytes 884744 | tf_op jit(solution)/shard_map/ppermute | solution.py:20
  50.5 8.4 %collective-permute-start.10 = (bf16[384,384]{1,0:T(8,128)(2,1)S(1)}, bf16[384,384]{1,0:T(8,128)(2,1)S(1)}, u32[]{:S(2)}, u32[]{:S(2)}) collective-permute-start(bf16[384,384]{1,0:T(8,128)(2,1)S(1)} %get-tuple-element.58), channel_id=1, source_target_pairs={{16,32},{32,16},{20,36},{36,20},{24,40},{40,24},{28,44},{44,28},{4... | collective-permute-start | bytes 884744 | tf_op jit(solution)/shard_map/ppermute | solution.py:20
  51.2 26.0 %collective-permute-start.12 = (bf16[384,384]{1,0:T(8,128)(2,1)S(1)}, bf16[384,384]{1,0:T(8,128)(2,1)S(1)}, u32[]{:S(2)}, u32[]{:S(2)}) collective-permute-start(bf16[384,384]{1,0:T(8,128)(2,1)S(1)} %get-tuple-element.58), channel_id=1, source_target_pairs={{120,136},{128,112},{124,140},{132,116},{248,264},{256,240},{252,2... | collective-permute-start | bytes 884744 | tf_op jit(solution)/shard_map/ppermute | solution.py:20
  56.8 17.6 %collective-permute-start.13 = (bf16[2,768,384]{2,1,0:T(8,128)(2,1)S(1)}, bf16[2,768,384]{2,1,0:T(8,128)(2,1)S(1)}, u32[]{:S(2)}, u32[]{:S(2)}) collective-permute-start(bf16[2,768,384]{2,1,0:T(8,128)(2,1)S(1)} %get-tuple-element.63), channel_id=1, source_target_pairs={{0,4},{4,0},{8,12},{12,8},{16,20},{20,16},{24,28},{28,24},{32,36},... | collective-permute-start | bytes 3538952 | tf_op jit(solution)/shard_map/ppermute | solution.py:20
  59.0 20.3 %collective-permute-start.11 = (bf16[192,384]{1,0:T(8,128)(2,1)S(1)}, bf16[192,384]{1,0:T(8,128)(2,1)S(1)}, u32[]{:S(2)}, u32[]{:S(2)}) collective-permute-start(bf16[192,384]{1,0:T(8,128)(2,1)S(1)} %get-tuple-element.60), channel_id=1, source_target_pairs={{0,8},{4,12},{8,0},{12,4},{16,24},{20,28},{24,16},{28,20},{32,40},... | collective-permute-start | bytes 442376 | tf_op jit(solution)/shard_map/ppermute | solution.py:20
  74.5 17.4 %collective-permute-start.14 = (bf16[768,384]{1,0:T(8,128)(2,1)S(1)}, bf16[768,384]{1,0:T(8,128)(2,1)S(1)}, u32[]{:S(2)}, u32[]{:S(2)}) collective-permute-start(bf16[768,384]{1,0:T(8,128)(2,1)S(1)} %lend.1), channel_id=1, source_target_pairs={{0,8},{4,12},{8,0},{12,4},{16,24},{20,28},{24,16},{28,20},{32,40},... | collective-permute-start | bytes 1769480 | tf_op jit(solution)/shard_map/ppermute | solution.py:20

commit v6 on v5

--- a/solution.py
+++ b/solution.py
@@ -36,7 +36,8 @@
     core = [(at(t, c, w), at(t, c, 1 - w)) for t, c, w in every]
     pair = [(at(t, c, w), at(t, 1 - c, w)) for t, c, w in every]
     home = [(a, b ^ 2) for a, b in cross]
-    return core, pair, even, odd, cross, lift, home
+    straight, diagonal = odd + home, [(a, b ^ 2) for a, b in odd] + home
+    return core, pair, even, odd + cross, cross, lift, straight, diagonal
 
 
 def position(time_all):
@@ -249,7 +250,7 @@
     dq_cross[...] = (dq[1] * factor).astype(BF)
 
 
-def odd_kernel(factor, time_all, extents, pack, kv, acc_in, dq_out, own, lent, sib, acc, dq):
+def odd_kernel(factor, time_all, extents, pack, kv, acc_in, dq_straight, dq_diagonal, own, lent, sib, acc, dq):
     rows, channels = dq.shape
     heads = channels // HEAD
     dq[...] = jnp.zeros_like(dq)
@@ -279,7 +280,11 @@
         return carry
 
     lax.fori_loop(0, 4, step, 0)
-    dq_out[...] = (dq[...] * factor).astype(BF)
+    half = rows // 2
+    _, chip, _, _, inner = position(time_all)
+    turn = jnp.where(inner, chip, 0)
+    for ref, part in ((dq_straight, turn), (dq_diagonal, 1 - turn)):
+        ref[...] = (dq[pl.ds(pl.multiple_of(part * half, half), half)] * factor).astype(BF)
     own[0:rows] = acc[0, 0:rows] * factor
     own[rows:] = acc[0, rows:]
     lent[0:rows] = acc[2, 0:rows] * factor
@@ -289,21 +294,17 @@
         sib[i, rows:] = acc[j, rows:].astype(BF)
 
 
-def sum_kernel(half, own, even, odd, mine, msg):
-    total = own[...] + even[...].astype(F32) + odd[...].astype(F32)
+def sum_kernel(half, own, even, mine, msg):
+    total = own[...] + even[...].astype(F32)
     mine[...] = total[:half]
     msg[...] = total[half:].astype(BF)
 
 
-def settle_kernel(cross, far, out):
-    out[...] = cross[...].astype(F32) + far[...].astype(F32)
-
-
-def place_kernel(half, mine, got, ended, out):
+def place_kernel(half, mine, got, straight, diagonal, cross, out):
     chip = lax.axis_index("space") // 2
-    for ref, part in ((mine, chip), (got, 1 - chip)):
+    for ref, back, part in ((mine, straight, chip), (got, diagonal, 1 - chip)):
         at = pl.ds(pl.multiple_of(part * half, half), half)
-        out[at] = (ref[...].astype(F32) + ended[at]).astype(BF)
+        out[at] = (ref[...].astype(F32) + back[...].astype(F32) + cross[at].astype(F32)).astype(BF)
 
 
 def lend_kernel(lent, sib, out):
@@ -335,7 +336,7 @@
     heads, half = log_norm.shape[2], rows // 2
     factor = (channels // heads) ** (-0.5)
     time_all = lax.axis_size("tm")
-    core, pair, even, odd, cross, lift, home = routes(time_all)
+    core, pair, even, odd, cross, lift, straight, diagonal = routes(time_all)
     out = jax.ShapeDtypeStruct
     tile, two, packet, part = (rows, channels), (2 * rows, channels), (2 * rows + AUX, channels), (rows + AUX, channels)
     lanes = (heads, 1, rows)
@@ -353,10 +354,9 @@
     msg = send(msg, pair)
     extra = send(extra, lift)
     whole = send(whole, cross)
-    pack, key, value = lax.optimization_barrier((pack, key_tiles[0, 0], value_tiles[0, 0]))
-    (kv_a,) = call(functools.partial(stack_kernel, rows), [out(two, BF)], (key, value), 0, "stack")
+    (kv_a,) = call(functools.partial(stack_kernel, rows), [out(two, BF)], (key_tiles[0, 0], value_tiles[0, 0]), 0, "stack")
+    kv_a, msg = lax.optimization_barrier((kv_a, msg))
     kv_b = send(kv_a, core)
-    kv_a, msg = lax.optimization_barrier((kv_a, msg))
     kv_c = send(kv_a, pair)
     (pack,) = call(functools.partial(join_kernel, half), [out(packet, BF)], (msg, pack), 20, "join")
     even_pack = send(pack, even)
@@ -369,7 +369,7 @@
         )
     extra, whole, dq = lax.optimization_barrier((extra, whole, dq))
     (odd_pack,) = call(functools.partial(odd_join_kernel, half, time_all), [out(packet, BF)], (msg, extra, pack), 100, "odd_join")
-    odd_pack = send(odd_pack, odd + cross)
+    odd_pack = send(odd_pack, odd)
     kv_c, dq = lax.optimization_barrier((kv_c, dq))
     kv_d = send(kv_c, core)
     with jax.named_scope("frame"):
@@ -381,26 +381,26 @@
             scalars=1,
         )
     with jax.named_scope("odd"):
-        odd_dq, own, lent, sib = call(
+        straight_dq, diagonal_dq, own, lent, sib = call(
             functools.partial(odd_kernel, factor, time_all),
-            [out(tile, BF), out(two, F32), out(two, F32), out((2,) + two, BF)],
+            [out((half, channels), BF)] * 2 + [out(two, F32), out(two, F32), out((2,) + two, BF)],
             (extents, odd_pack, kv, acc), 20, "odd", [pltpu.VMEM((4,) + two, F32), pltpu.VMEM(tile, F32)], scalars=1,
         )
-    far_back = send(odd_dq, home)
-    odd_back = send(odd_dq, odd)
     even_back = send(even_dq, even)
+    sib, even_back = lax.optimization_barrier((sib, even_back))
+    straight_back = send(straight_dq, straight)
+    diagonal_back = send(diagonal_dq, diagonal)
     cross_back = send(cross_dq, cross)
-    sib, even_back, cross_back = lax.optimization_barrier((sib, even_back, cross_back))
     sib = send(sib, core)
     (lent,) = call(lend_kernel, [out(two, BF)], (lent, sib), 0, "lend")
     given = send(lent, pair)
     mine, msg = call(
-        functools.partial(sum_kernel, half),
-        [out((half, channels), F32), out((half, channels), BF)], (dq, even_back, odd_back), 20, "sum"
+        functools.partial(sum_kernel, half), [out((half, channels), F32), out((half, channels), BF)], (dq, even_back), 0, "sum"
     )
     msg = send(msg, pair)
-    (ended,) = call(settle_kernel, [out(tile, F32)], (cross_back, far_back), 100, "settle")
-    (grad_query,) = call(functools.partial(place_kernel, half), [out(tile, BF)], (mine, msg, ended), 0, "place")
+    (grad_query,) = call(
+        functools.partial(place_kernel, half), [out(tile, BF)], (mine, msg, straight_back, diagonal_back, cross_back), 0, "place"
+    )
     grad_key, grad_value = call(functools.partial(close_kernel, rows), [out(tile, BF)] * 2, (own, sib, given), 0, "close")
     shape = (1, 1, rows, channels)
     return grad_query.reshape(shape), grad_key.reshape(shape), grad_value.reshape(shape)

time: 93.4 us -> 95.1 us (1.018)
  the two profiles are of different devices: /device:TPU:190 before, /device:TPU:62 now
where the time goes in v6:
time: 95.1 us; the launch traced here: 93.3 us
  waiting for transfers between devices  35.5 us (37%)
  starting transfers between devices  34.9 us (37%)
  Pallas kernels  20 us (21%)
  local copies, waits for them, and re-layouts  2.04 us (2%)
    ppermute x15, waiting for transfers between devices, send(): return lax.ppermute(block, ('tm', 'space'), pairs)  35.5 us
    ppermute x15, starting transfers between devices, send(): return lax.ppermute(block, ('tm', 'space'), pairs)  34.9 us
    pallas_call x10, Pallas kernels, call(): pl.pallas_call(kernel, out_shape=shapes, in_specs=[pl.BlockSpec(memory_sp...  17.5 us
    pallas_call x1, Pallas kernels, body(): pl.pallas_call(functools.partial(pack_kernel, half), out_shape=[out(packe...  2.51 us
    unnamed x9, local copies, waits for them, and re-layouts  2.04 us
  transfers between devices with their start and end apart: 15, of which 8 were waited for; matrix products, arithmetic and copies ran while one was open for 0% of the time, Pallas kernels for 18%

profile of v6, /device:TPU:62, one launch (start us, length us, event | category | flops | bytes accessed | tf_op | source)
XLA Modules:
  0.0 93.3 jit_solution(3250451396277095572)
XLA Ops:
  0.6 2.5 %pack.1 = (bf16[800,384]{1,0:T(8,128)(2,1)}, bf16[416,384]{1,0:T(8,128)(2,1)}, bf16[416,384]{1,0:T(8,128)(2,1)}, bf16[800,384]{1,0:T(8,128)(2,1)}) custom-call(bf16[384,384]{1,0:T(8,128)(2,1)} %bitcast.11, bf16[384,384]{1,0:T(8,128)(2,1)} %bitcast.12, f32[3,1,384]{2,1,0:T(1,128)} %bitcast.14, f32[3,1,384]{2,1,0:T(1,128)} %bitcast.15), custom_call_target="tpu_custom_call" | custom-call | flops 1000 | bytes 1000 | tf_op jit(solution)/shard_map/pack/pallas_call | solution.py:344
  3.2 4.3 %collective-permute-start = (bf16[416,384]{1,0:T(8,128)(2,1)}, bf16[416,384]{1,0:T(8,128)(2,1)S(1)}, u32[]{:S(2)}, u32[]{:S(2)}) collective-permute-start(bf16[416,384]{1,0:T(8,128)(2,1)} %get-tuple-element.32), channel_id=1, source_target_pairs={{0,8},{4,12},{8,0},{12,4},{16,24},{20,28},{24,16},{28,20},{32,40},... | collective-permute-start | bytes 958472 | tf_op jit(solution)/shard_map/ppermute | solution.py:20
  7.4 1.9 %collective-permute-start.2 = (bf16[416,384]{1,0:T(8,128)(2,1)}, bf16[416,384]{1,0:T(8,128)(2,1)S(1)}, u32[]{:S(2)}, u32[]{:S(2)}) collective-permute-start(bf16[416,384]{1,0:T(8,128)(2,1)} %get-tuple-element.35), channel_id=1, source_target_pairs={{112,120},{136,128},{116,124},{140,132},{240,248},{264,256},{244,2... | collective-permute-start | bytes 958472 | tf_op jit(solution)/shard_map/ppermute | solution.py:20
  9.4 0.7 collective-permute-start.3
  10.1 1.0 %copy-done = bf16[1,1,384,384]{3,2,1,0:T(8,128)(2,1)S(1)} copy-done((bf16[1,1,384,384]{3,2,1,0:T(8,128)(2,1)S(1)}, bf16[1,1,384,384]{3,2,1,0:T(8,128)(2,1)}, u32[]{:S(2)}) %copy-start) | copy-done | bytes 294936
  11.1 1.0 %copy-done.1 = bf16[1,1,384,384]{3,2,1,0:T(8,128)(2,1)S(1)} copy-done((bf16[1,1,384,384]{3,2,1,0:T(8,128)(2,1)S(1)}, bf16[1,1,384,384]{3,2,1,0:T(8,128)(2,1)}, u32[]{:S(2)}) %copy-start.1) | copy-done | bytes 294936
  12.2 3.5 %collective-permute-done.msg = bf16[416,384]{1,0:T(8,128)(2,1)S(1)} collective-permute-done((bf16[416,384]{1,0:T(8,128)(2,1)}, bf16[416,384]{1,0:T(8,128)(2,1)S(1)}, u32[]{:S(2)}, u32[]{:S(2)}) %collective-permute-start) | collective-permute-done | bytes 319520 | tf_op jit(solution)/shard_map/ppermute | solution.py:20
  15.7 4.3 %collective-permute-start.5 = (bf16[768,384]{1,0:T(8,128)(2,1)S(1)}, bf16[768,384]{1,0:T(8,128)(2,1)S(1)}, u32[]{:S(2)}, u32[]{:S(2)}) collective-permute-start(bf16[768,384]{1,0:T(8,128)(2,1)S(1)} %stack.1.kv_a), channel_id=1, source_target_pairs={{0,8},{4,12},{8,0},{12,4},{16,24},{20,28},{24,16},{28,20},{32,40},... | collective-permute-start | bytes 1769480 | tf_op jit(solution)/shard_map/ppermute | solution.py:20
  20.0 1.9 %collective-permute-start.4 = (bf16[768,384]{1,0:T(8,128)(2,1)S(1)}, bf16[768,384]{1,0:T(8,128)(2,1)S(1)}, u32[]{:S(2)}, u32[]{:S(2)}) collective-permute-start(bf16[768,384]{1,0:T(8,128)(2,1)S(1)} %stack.1.kv_a), channel_id=1, source_target_pairs={{0,4},{4,0},{8,12},{12,8},{16,20},{20,16},{24,28},{28,24},{32,36},... | collective-permute-start | bytes 1769480 | tf_op jit(solution)/shard_map/ppermute | solution.py:20
  22.0 2.1 %collective-permute-start.1 = (bf16[800,384]{1,0:T(8,128)(2,1)S(1)}, bf16[800,384]{1,0:T(8,128)(2,1)S(1)}, u32[]{:S(2)}, u32[]{:S(2)}) collective-permute-start(bf16[800,384]{1,0:T(8,128)(2,1)S(1)} %join.1.pack.own), channel_id=1, source_target_pairs={{0,16},{16,0},{4,20},{20,4},{8,24},{24,8},{12,28},{28,12},{32,48},... | collective-permute-start | bytes 1843208 | tf_op jit(solution)/shard_map/ppermute | solution.py:20
  24.1 3.4 %own.1 = (f32[2,768,384]{2,1,0:T(8,128)S(1)}, f32[384,384]{1,0:T(8,128)S(1)}) custom-call(s32[32,4,3]{2,1,0:T(4,128)S(1)} %copy.11.extents, bf16[800,384]{1,0:T(8,128)(2,1)S(1)} %join.1.pack.own, bf16[768,384]{1,0:T(8,128)(2,1)S(1)} %stack.1.kv_a, bf16[768,384]{1,0:T(8,128)(2,1)S(1)} %collective-permute-done.4.kv_b), custom_call_target="tpu_custom_call" | custom-call | flops 1000 | bytes 1000 | tf_op jit(solution)/shard_map/own/own/pallas_call | solution.py:322
  27.6 0.7 collective-permute-start.7
  28.3 5.6 %collective-permute-done.5.kv_c = bf16[768,384]{1,0:T(8,128)(2,1)S(1)} collective-permute-done((bf16[768,384]{1,0:T(8,128)(2,1)S(1)}, bf16[768,384]{1,0:T(8,128)(2,1)S(1)}, u32[]{:S(2)}, u32[]{:S(2)}) %collective-permute-start.5) | collective-permute-done | bytes 589856 | tf_op jit(solution)/shard_map/ppermute | solution.py:20
  33.9 1.9 %collective-permute-start.6 = (bf16[768,384]{1,0:T(8,128)(2,1)S(1)}, bf16[768,384]{1,0:T(8,128)(2,1)S(1)}, u32[]{:S(2)}, u32[]{:S(2)}) collective-permute-start(bf16[768,384]{1,0:T(8,128)(2,1)S(1)} %collective-permute-done.5.kv_c), channel_id=1, source_target_pairs={{0,4},{4,0},{8,12},{12,8},{16,20},{20,16},{24,28},{28,24},{32,36},... | collective-permute-start | bytes 1769480 | tf_op jit(solution)/shard_map/ppermute | solution.py:20
  35.8 4.3 %collective-permute-done.1.even = bf16[800,384]{1,0:T(8,128)(2,1)S(1)} collective-permute-done((bf16[800,384]{1,0:T(8,128)(2,1)S(1)}, bf16[800,384]{1,0:T(8,128)(2,1)S(1)}, u32[]{:S(2)}, u32[]{:S(2)}) %collective-permute-start.1) | collective-permute-done | bytes 614432 | tf_op jit(solution)/shard_map/ppermute | solution.py:20
  40.1 9.5 %frame.1 = (f32[4,768,384]{2,1,0:T(8,128)S(1)}, f32[384,384]{1,0:T(8,128)S(1)}, bf16[384,384]{1,0:T(8,128)(2,1)S(1)}, bf16[384,384]{1,0:T(8,128)(2,1)S(1)}, bf16[4,768,384]{2,1,0:T(8,128)(2,1)S(1)}) custom-call(s32[32,4,3]{2,1,0:T(4,128)S(1)} %copy.11.extents, bf16[800,384]{1,0:T(8,128)(2,1)S(1)} %collective-permute-done.1.even, ...), custom_call_target="tpu_custom_call" | custom-call | flops 1000 | bytes 1000 | tf_op jit(solution)/shard_map/frame/frame/pallas_call | solution.py:322
  49.6 1.9 %collective-permute-start.8 = (bf16[384,384]{1,0:T(8,128)(2,1)S(1)}, bf16[384,384]{1,0:T(8,128)(2,1)S(1)}, u32[]{:S(2)}, u32[]{:S(2)}) collective-permute-start(bf16[384,384]{1,0:T(8,128)(2,1)S(1)} %get-tuple-element.49), channel_id=1, source_target_pairs={{0,16},{16,0},{4,20},{20,4},{8,24},{24,8},{12,28},{28,12},{32,48},... | collective-permute-start | bytes 884744 | tf_op jit(solution)/shard_map/ppermute | solution.py:20
  51.6 2.5 %odd.1 = (bf16[192,384]{1,0:T(8,128)(2,1)S(1)}, bf16[192,384]{1,0:T(8,128)(2,1)S(1)}, f32[768,384]{1,0:T(8,128)S(1)}, f32[768,384]{1,0:T(8,128)S(1)}, bf16[2,768,384]{2,1,0:T(8,128)(2,1)S(1)}) custom-call(s32[32,4,3]{2,1,0:T(4,128)S(1)} %copy.11.extents, bf16[800,384]{1,0:T(8,128)(2,1)S(1)} %collective-permute-done.7.pack, ...), custom_call_target="tpu_custom_call" | custom-call | flops 20000000000 | bytes 1000 | tf_op jit(solution)/shard_map/odd/odd/pallas_call | solution.py:322
  54.1 5.8 %collective-permute-done.8.even = bf16[384,384]{1,0:T(8,128)(2,1)S(1)} collective-permute-done((bf16[384,384]{1,0:T(8,128)(2,1)S(1)}, bf16[384,384]{1,0:T(8,128)(2,1)S(1)}, u32[]{:S(2)}, u32[]{:S(2)}) %collective-permute-start.8) | collective-permute-done | bytes 294944 | tf_op jit(solution)/shard_map/ppermute | solution.py:20
  59.9 1.9 %collective-permute-start.13 = (bf16[2,768,384]{2,1,0:T(8,128)(2,1)S(1)}, bf16[2,768,384]{2,1,0:T(8,128)(2,1)S(1)}, u32[]{:S(2)}, u32[]{:S(2)}) collective-permute-start(bf16[2,768,384]{2,1,0:T(8,128)(2,1)S(1)} %get-tuple-element.57), channel_id=1, source_target_pairs={{0,4},{4,0},{8,12},{12,8},{16,20},{20,16},{24,28},{28,24},{32,36},... | collective-permute-start | bytes 3538952 | tf_op jit(solution)/shard_map/ppermute | solution.py:20
  61.8 2.8 %collective-permute-done.13.sib = bf16[2,768,384]{2,1,0:T(8,128)(2,1)S(1)} collective-permute-done((bf16[2,768,384]{2,1,0:T(8,128)(2,1)S(1)}, bf16[2,768,384]{2,1,0:T(8,128)(2,1)S(1)}, u32[]{:S(2)}, u32[]{:S(2)}) %collective-permute-start.13) | collective-permute-done | bytes 1179680 | tf_op jit(solution)/shard_map/ppermute | solution.py:20
  64.6 0.2 lend.1
  64.8 2.9 %collective-permute-start.14 = (bf16[768,384]{1,0:T(8,128)(2,1)S(1)}, bf16[768,384]{1,0:T(8,128)(2,1)S(1)}, u32[]{:S(2)}, u32[]{:S(2)}) collective-permute-start(bf16[768,384]{1,0:T(8,128)(2,1)S(1)} %lend.1), channel_id=1, source_target_pairs={{0,8},{4,12},{8,0},{12,4},{16,24},{20,28},{24,16},{28,20},{32,40},... | collective-permute-start | bytes 1769480 | tf_op jit(solution)/shard_map/ppermute | solution.py:20
  67.7 0.7 collective-permute-start.12
  68.4 1.3 %collective-permute-start.10 = (bf16[192,384]{1,0:T(8,128)(2,1)S(1)}, bf16[192,384]{1,0:T(8,128)(2,1)S(1)}, u32[]{:S(2)}, u32[]{:S(2)}) collective-permute-start(bf16[192,384]{1,0:T(8,128)(2,1)S(1)} %get-tuple-element.53), channel_id=1, source_target_pairs={{16,32},{32,16},{20,36},{36,20},{24,40},{40,24},{28,44},{44,28},{4... | collective-permute-start | bytes 442376 | tf_op jit(solution)/shard_map/ppermute | solution.py:20
  69.7 1.3 %collective-permute-start.11 = (bf16[192,384]{1,0:T(8,128)(2,1)S(1)}, bf16[192,384]{1,0:T(8,128)(2,1)S(1)}, u32[]{:S(2)}, u32[]{:S(2)}) collective-permute-start(bf16[192,384]{1,0:T(8,128)(2,1)S(1)} %get-tuple-element.54), channel_id=1, source_target_pairs={{16,40},{32,24},{20,44},{36,28},{24,32},{40,16},{28,36},{44,20},{4... | collective-permute-start | bytes 442376 | tf_op jit(solution)/shard_map/ppermute | solution.py:20
  71.1 7.0 %collective-permute-start.9 = (bf16[192,384]{1,0:T(8,128)(2,1)S(1)}, bf16[192,384]{1,0:T(8,128)(2,1)S(1)}, u32[]{:S(2)}, u32[]{:S(2)}) collective-permute-start(bf16[192,384]{1,0:T(8,128)(2,1)S(1)} %get-tuple-element.52), channel_id=1, source_target_pairs={{0,8},{4,12},{8,0},{12,4},{16,24},{20,28},{24,16},{28,20},{32,40},... | collective-permute-start | bytes 442376 | tf_op jit(solution)/shard_map/ppermute | solution.py:20
  78.1 7.2 %collective-permute-done.10.straight = bf16[192,384]{1,0:T(8,128)(2,1)S(1)} collective-permute-done((bf16[192,384]{1,0:T(8,128)(2,1)S(1)}, bf16[192,384]{1,0:T(8,128)(2,1)S(1)}, u32[]{:S(2)}, u32[]{:S(2)}) %collective-permute-start.10) | collective-permute-done | bytes 147488 | tf_op jit(solution)/shard_map/ppermute | solution.py:20
  85.3 2.0 %collective-permute-done.11.diagonal = bf16[192,384]{1,0:T(8,128)(2,1)S(1)} collective-permute-done((bf16[192,384]{1,0:T(8,128)(2,1)S(1)}, bf16[192,384]{1,0:T(8,128)(2,1)S(1)}, u32[]{:S(2)}, u32[]{:S(2)}) %collective-permute-start.11) | collective-permute-done | bytes 147488 | tf_op jit(solution)/shard_map/ppermute | solution.py:20
  87.3 4.2 %collective-permute-done.9.got = bf16[192,384]{1,0:T(8,128)(2,1)S(1)} collective-permute-done((bf16[192,384]{1,0:T(8,128)(2,1)S(1)}, bf16[192,384]{1,0:T(8,128)(2,1)S(1)}, u32[]{:S(2)}, u32[]{:S(2)}) %collective-permute-start.9) | collective-permute-done | bytes 147488 | tf_op jit(solution)/shard_map/ppermute | solution.py:20
  91.5 0.8 place.1
  92.3 1.0 %close.1 = (bf16[384,384]{1,0:T(8,128)(2,1)}, bf16[384,384]{1,0:T(8,128)(2,1)}) custom-call(f32[768,384]{1,0:T(8,128)S(1)} %get-tuple-element.56.own, bf16[2,768,384]{2,1,0:T(8,128)(2,1)S(1)} %collective-permute-done.13.sib, bf16[768,384]{1,0:T(8,128)(2,1)S(1)} %collective-permute-done.14.given), custom_call_target="tpu_custom_call" | custom-call | flops 1000 | bytes 1000 | tf_op jit(solution)/shard_map/close/pallas_call | solution.py:322
  (18 shorter events, 0.4 us)
Async XLA Ops:
  0.6 11.4 %copy-start.3 = (s32[32,4,3]{0,1,2:T(4,128)S(1)}, s32[32,4,3]{0,1,2:T(4,128)}, u32[]{:S(2)}) copy-start(s32[32,4,3]{0,1,2:T(4,128)} %param.13) | copy-start | bytes 4612
  3.2 12.5 %collective-permute-start = (bf16[416,384]{1,0:T(8,128)(2,1)}, bf16[416,384]{1,0:T(8,128)(2,1)S(1)}, u32[]{:S(2)}, u32[]{:S(2)}) collective-permute-start(bf16[416,384]{1,0:T(8,128)(2,1)} %get-tuple-element.32), channel_id=1, source_target_pairs={{0,8},{4,12},{8,0},{12,4},{16,24},{20,28},{24,16},{28,20},{32,40},... | collective-permute-start | bytes 958472 | tf_op jit(solution)/shard_map/ppermute | solution.py:20
  7.4 20.0 %collective-permute-start.2 = (bf16[416,384]{1,0:T(8,128)(2,1)}, bf16[416,384]{1,0:T(8,128)(2,1)S(1)}, u32[]{:S(2)}, u32[]{:S(2)}) collective-permute-start(bf16[416,384]{1,0:T(8,128)(2,1)} %get-tuple-element.35), channel_id=1, source_target_pairs={{112,120},{136,128},{116,124},{140,132},{240,248},{264,256},{244,2... | collective-permute-start | bytes 958472 | tf_op jit(solution)/shard_map/ppermute | solution.py:20
  9.4 18.1 %collective-permute-start.3 = (bf16[800,384]{1,0:T(8,128)(2,1)}, bf16[800,384]{1,0:T(8,128)(2,1)S(1)}, u32[]{:S(2)}, u32[]{:S(2)}) collective-permute-start(bf16[800,384]{1,0:T(8,128)(2,1)} %get-tuple-element.36), channel_id=1, source_target_pairs={{120,128},{128,120},{124,132},{132,124},{248,256},{256,248},{252,2... | collective-permute-start | bytes 1843208 | tf_op jit(solution)/shard_map/ppermute | solution.py:20
  10.1 1.0 %copy-start = (bf16[1,1,384,384]{3,2,1,0:T(8,128)(2,1)S(1)}, bf16[1,1,384,384]{3,2,1,0:T(8,128)(2,1)}, u32[]{:S(2)}) copy-start(bf16[1,1,384,384]{3,2,1,0:T(8,128)(2,1)} %param.8) | copy-start | bytes 884740
  11.1 1.0 %copy-start.1 = (bf16[1,1,384,384]{3,2,1,0:T(8,128)(2,1)S(1)}, bf16[1,1,384,384]{3,2,1,0:T(8,128)(2,1)}, u32[]{:S(2)}) copy-start(bf16[1,1,384,384]{3,2,1,0:T(8,128)(2,1)} %param.9) | copy-start | bytes 884740
  12.0 9.9 %copy-start.2 = (bf16[800,384]{1,0:T(8,128)(2,1)S(1)}, bf16[800,384]{1,0:T(8,128)(2,1)}, u32[]{:S(2)}) copy-start(bf16[800,384]{1,0:T(8,128)(2,1)} %get-tuple-element.34.pack_in) | copy-start | bytes 1843204
  15.7 18.2 %collective-permute-start.5 = (bf16[768,384]{1,0:T(8,128)(2,1)S(1)}, bf16[768,384]{1,0:T(8,128)(2,1)S(1)}, u32[]{:S(2)}, u32[]{:S(2)}) collective-permute-start(bf16[768,384]{1,0:T(8,128)(2,1)S(1)} %stack.1.kv_a), channel_id=1, source_target_pairs={{0,8},{4,12},{8,0},{12,4},{16,24},{20,28},{24,16},{28,20},{32,40},... | collective-permute-start | bytes 1769480 | tf_op jit(solution)/shard_map/ppermute | solution.py:20
  20.0 4.1 %collective-permute-start.4 = (bf16[768,384]{1,0:T(8,128)(2,1)S(1)}, bf16[768,384]{1,0:T(8,128)(2,1)S(1)}, u32[]{:S(2)}, u32[]{:S(2)}) collective-permute-start(bf16[768,384]{1,0:T(8,128)(2,1)S(1)} %stack.1.kv_a), channel_id=1, source_target_pairs={{0,4},{4,0},{8,12},{12,8},{16,20},{20,16},{24,28},{28,24},{32,36},... | collective-permute-start | bytes 1769480 | tf_op jit(solution)/shard_map/ppermute | solution.py:20
  22.0 18.2 %collective-permute-start.1 = (bf16[800,384]{1,0:T(8,128)(2,1)S(1)}, bf16[800,384]{1,0:T(8,128)(2,1)S(1)}, u32[]{:S(2)}, u32[]{:S(2)}) collective-permute-start(bf16[800,384]{1,0:T(8,128)(2,1)S(1)} %join.1.pack.own), channel_id=1, source_target_pairs={{0,16},{16,0},{4,20},{20,4},{8,24},{24,8},{12,28},{28,12},{32,48},... | collective-permute-start | bytes 1843208 | tf_op jit(solution)/shard_map/ppermute | solution.py:20
  27.6 24.0 %collective-permute-start.7 = (bf16[800,384]{1,0:T(8,128)(2,1)S(1)}, bf16[800,384]{1,0:T(8,128)(2,1)S(1)}, u32[]{:S(2)}, u32[]{:S(2)}) collective-permute-start(bf16[800,384]{1,0:T(8,128)(2,1)S(1)} %odd_join.1), channel_id=1, source_target_pairs={{16,32},{32,16},{20,36},{36,20},{24,40},{40,24},{28,44},{44,28},{4... | collective-permute-start | bytes 1843208 | tf_op jit(solution)/shard_map/ppermute | solution.py:20
  33.9 6.2 %collective-permute-start.6 = (bf16[768,384]{1,0:T(8,128)(2,1)S(1)}, bf16[768,384]{1,0:T(8,128)(2,1)S(1)}, u32[]{:S(2)}, u32[]{:S(2)}) collective-permute-start(bf16[768,384]{1,0:T(8,128)(2,1)S(1)} %collective-permute-done.5.kv_c), channel_id=1, source_target_pairs={{0,4},{4,0},{8,12},{12,8},{16,20},{20,16},{24,28},{28,24},{32,36},... | collective-permute-start | bytes 1769480 | tf_op jit(solution)/shard_map/ppermute | solution.py:20
  49.6 10.2 %collective-permute-start.8 = (bf16[384,384]{1,0:T(8,128)(2,1)S(1)}, bf16[384,384]{1,0:T(8,128)(2,1)S(1)}, u32[]{:S(2)}, u32[]{:S(2)}) collective-permute-start(bf16[384,384]{1,0:T(8,128)(2,1)S(1)} %get-tuple-element.49), channel_id=1, source_target_pairs={{0,16},{16,0},{4,20},{20,4},{8,24},{24,8},{12,28},{28,12},{32,48},... | collective-permute-start | bytes 884744 | tf_op jit(solution)/shard_map/ppermute | solution.py:20
  59.9 4.7 %collective-permute-start.13 = (bf16[2,768,384]{2,1,0:T(8,128)(2,1)S(1)}, bf16[2,768,384]{2,1,0:T(8,128)(2,1)S(1)}, u32[]{:S(2)}, u32[]{:S(2)}) collective-permute-start(bf16[2,768,384]{2,1,0:T(8,128)(2,1)S(1)} %get-tuple-element.57), channel_id=1, source_target_pairs={{0,4},{4,0},{8,12},{12,8},{16,20},{20,16},{24,28},{28,24},{32,36},... | collective-permute-start | bytes 3538952 | tf_op jit(solution)/shard_map/ppermute | solution.py:20
  64.8 27.6 %collective-permute-start.14 = (bf16[768,384]{1,0:T(8,128)(2,1)S(1)}, bf16[768,384]{1,0:T(8,128)(2,1)S(1)}, u32[]{:S(2)}, u32[]{:S(2)}) collective-permute-start(bf16[768,384]{1,0:T(8,128)(2,1)S(1)} %lend.1), channel_id=1, source_target_pairs={{0,8},{4,12},{8,0},{12,4},{16,24},{20,28},{24,16},{28,20},{32,40},... | collective-permute-start | bytes 1769480 | tf_op jit(solution)/shard_map/ppermute | solution.py:20
  67.7 19.6 %collective-permute-start.12 = (bf16[384,384]{1,0:T(8,128)(2,1)S(1)}, bf16[384,384]{1,0:T(8,128)(2,1)S(1)}, u32[]{:S(2)}, u32[]{:S(2)}) collective-permute-start(bf16[384,384]{1,0:T(8,128)(2,1)S(1)} %get-tuple-element.55), channel_id=1, source_target_pairs={{120,128},{128,120},{124,132},{132,124},{248,256},{256,248},{252,2... | collective-permute-start | bytes 884744 | tf_op jit(solution)/shard_map/ppermute | solution.py:20
  68.4 16.9 %collective-permute-start.10 = (bf16[192,384]{1,0:T(8,128)(2,1)S(1)}, bf16[192,384]{1,0:T(8,128)(2,1)S(1)}, u32[]{:S(2)}, u32[]{:S(2)}) collective-permute-start(bf16[192,384]{1,0:T(8,128)(2,1)S(1)} %get-tuple-element.53), channel_id=1, source_target_pairs={{16,32},{32,16},{20,36},{36,20},{24,40},{40,24},{28,44},{44,28},{4... | collective-permute-start | bytes 442376 | tf_op jit(solution)/shard_map/ppermute | solution.py:20
  69.7 17.6 %collective-permute-start.11 = (bf16[192,384]{1,0:T(8,128)(2,1)S(1)}, bf16[192,384]{1,0:T(8,128)(2,1)S(1)}, u32[]{:S(2)}, u32[]{:S(2)}) collective-permute-start(bf16[192,384]{1,0:T(8,128)(2,1)S(1)} %get-tuple-element.54), channel_id=1, source_target_pairs={{16,40},{32,24},{20,44},{36,28},{24,32},{40,16},{28,36},{44,20},{4... | collective-permute-start | bytes 442376 | tf_op jit(solution)/shard_map/ppermute | solution.py:20
  71.1 20.4 %collective-permute-start.9 = (bf16[192,384]{1,0:T(8,128)(2,1)S(1)}, bf16[192,384]{1,0:T(8,128)(2,1)S(1)}, u32[]{:S(2)}, u32[]{:S(2)}) collective-permute-start(bf16[192,384]{1,0:T(8,128)(2,1)S(1)} %get-tuple-element.52), channel_id=1, source_target_pairs={{0,8},{4,12},{8,0},{12,4},{16,24},{20,28},{24,16},{28,20},{32,40},... | collective-permute-start | bytes 442376 | tf_op jit(solution)/shard_map/ppermute | solution.py:20

commit v7 on v6

--- a/solution.py
+++ b/solution.py
@@ -195,59 +195,71 @@
 
 
 def frame_kernel(factor, time_all, extents, even, cross, own, kv_a, kv_b, kv_c, kv_d, acc_in, dq_in,
-                 acc, dq_own, dq_even, dq_cross, kv, packs, terms, hide, dq):
+                 acc, dq_own, dq_even, dq_cross, kv, packs, terms, dq, order):
     rows, channels = dq_own.shape
-    heads = channels // HEAD
+    heads, half = channels // HEAD, rows // 2
     for i, ref in enumerate((kv_a, kv_b, kv_c, kv_d)):
         kv[i] = ref[...]
     for i, ref in enumerate((even, cross, own)):
-        packs[i] = ref[0 : 2 * rows]
-        terms[i, 0 : 2 * heads] = row_terms(ref, rows, heads)
+        each = row_terms(ref, rows, heads)
+        for part in range(2):
+            packs[2 * i + part, 0:half] = ref[part * half : (part + 1) * half]
+            packs[2 * i + part, half:rows] = ref[rows + part * half : rows + (part + 1) * half]
+            terms[2 * i + part, 0 : 2 * heads] = each[:, part * half : (part + 1) * half]
     acc[0:2] = acc_in[...]
     acc[2:4] = jnp.zeros_like(acc[2:4])
-    dq[0:2] = jnp.zeros_like(dq[0:2])
-    dq[2] = dq_in[...]
+    dq[0:4] = jnp.zeros_like(dq[0:4])
+    dq[4] = dq_in[0:half]
+    dq[5] = dq_in[half:]
     see = [seen(extents, time_all, kind) for kind in ("even", "cross", "own")]
 
-    def add(j, members):
-        each = lambda pick, axis: jnp.concatenate([pick(m) for m in members], axis=axis) if len(members) > 1 else pick(members[0])
+    def add(j, start, size, count):
+        members = [order[start + i] for i in range(size)]
+        hide = [jnp.where(start + i < count, 0.0, NEVER) for i in range(size)]
+        each = lambda pick, axis: jnp.concatenate([pick(i, m) for i, m in enumerate(members)], axis=axis)
         for h in range(heads):
             cols = slice(h * HEAD, (h + 1) * HEAD)
             query_term, key_term, value_term = pair_terms(
-                each(lambda m: packs[m, 0:rows, cols], 0), each(lambda m: packs[m, rows:, cols], 0),
+                each(lambda i, m: packs[m, 0:half, cols], 0), each(lambda i, m: packs[m, half:rows, cols], 0),
                 kv[j, 0:rows, cols], kv[j, rows:, cols],
-                each(lambda m: terms[m, h : h + 1] + hide[m, 0:1], 1),
-                each(lambda m: terms[m, heads + h : heads + h + 1], 1), factor,
+                each(lambda i, m: terms[m, h : h + 1] + hide[i], 1),
+                each(lambda i, m: terms[m, heads + h : heads + h + 1], 1), factor,
             )
             for i, m in enumerate(members):
-                dq[m, :, cols] += query_term[i * rows : (i + 1) * rows]
+                dq[m, :, cols] += query_term[i * half : (i + 1) * half]
             acc[j, 0:rows, cols] += key_term
             acc[j, rows:, cols] += value_term
 
     def step(j, carry):
-        on = []
+        for i in range(6):
+            order[i] = 0
+        count = jnp.int32(0)
         for i, flag in enumerate(see):
-            parts = flag(j, 0), flag(j, 1)
-            hide[i, 0:1] = hidden(*parts, rows)
-            on.append(parts[0] | parts[1] if i < 2 else (parts[0] | parts[1]) & (j >= 2))
-        count = sum(x.astype(jnp.int32) for x in on)
-        one = jnp.where(on[0], 0, jnp.where(on[1], 1, 2))
-        two = jnp.where(on[0] & on[1], 1, 2)
-
-        @pl.when(count >= 2)
+            for part in range(2):
+                on = flag(j, part) if i < 2 else flag(j, part) & (j >= 2)
+
+                @pl.when(on)
+                def _(unit=2 * i + part, count=count):
+                    order[count] = unit
+
+                count = count + on.astype(jnp.int32)
+
+        @pl.when(count >= 3)
         def _():
-            add(j, [one, two])
-
-        @pl.when(count % 2 == 1)
+            add(j, 0, 4, count)
+
+        @pl.when((count > 4) | ((count > 0) & (count < 3)))
         def _():
-            add(j, [jnp.where(count == 3, 2, one)])
+            add(j, jnp.where(count > 4, 4, 0), 2, count)
 
         return carry
 
     lax.fori_loop(0, 4, step, 0)
-    dq_own[...] = dq[2] * factor
-    dq_even[...] = (dq[0] * factor).astype(BF)
-    dq_cross[...] = (dq[1] * factor).astype(BF)
+    for part in range(2):
+        at = slice(part * half, (part + 1) * half)
+        dq_even[at] = (dq[part] * factor).astype(BF)
+        dq_cross[at] = (dq[2 + part] * factor).astype(BF)
+        dq_own[at] = dq[4 + part] * factor
 
 
 def odd_kernel(factor, time_all, extents, pack, kv, acc_in, dq_straight, dq_diagonal, own, lent, sib, acc, dq):
@@ -377,7 +389,7 @@
             functools.partial(frame_kernel, factor, time_all),
             [out((4,) + two, F32), out(tile, F32), out(tile, BF), out(tile, BF), out((4,) + two, BF)],
             (extents, even_pack, whole, pack, kv_a, kv_b, kv_c, kv_d, acc, dq), 0, "frame",
-            [pltpu.VMEM((3,) + two, BF), pltpu.VMEM((3, 8, rows), F32), pltpu.VMEM((3, 8, rows), F32), pltpu.VMEM((3,) + tile, F32)],
+            [pltpu.VMEM((6,) + tile, BF), pltpu.VMEM((6, 8, half), F32), pltpu.VMEM((6, half, channels), F32), pltpu.SMEM((8,), jnp.int32)],
             scalars=1,
         )
     with jax.named_scope("odd"):

time: 95.1 us -> 94.2 us (level)
  the two profiles are of different devices: /device:TPU:62 before, /device:TPU:188 now
where the time goes in v7:
time: 94.2 us; the launch traced here: 93.7 us
  starting transfers between devices  36.2 us (38%)
  waiting for transfers between devices  36 us (38%)
  Pallas kernels  18.6 us (20%)
  local copies, waits for them, and re-layouts  2.04 us (2%)
    ppermute x15, starting transfers between devices, send(): return lax.ppermute(block, ('tm', 'space'), pairs)  36.2 us
    ppermute x15, waiting for transfers between devices, send(): return lax.ppermute(block, ('tm', 'space'), pairs)  36 us
    pallas_call x10, Pallas kernels, call(): pl.pallas_call(kernel, out_shape=shapes, in_specs=[pl.BlockSpec(memory_sp...  16.1 us
    pallas_call x1, Pallas kernels, body(): pl.pallas_call(functools.partial(pack_kernel, half), out_shape=[out(packe...  2.51 us
    unnamed x9, local copies, waits for them, and re-layouts  2.04 us
  transfers between devices with their start and end apart: 15, of which 8 were waited for; matrix products, arithmetic and copies ran while one was open for 0% of the time, Pallas kernels for 16%

profile of v7, /device:TPU:188, one launch (start us, length us, event | category | flops | bytes accessed | tf_op | source)
XLA Modules:
  0.0 93.7 jit_solution(11042916613735684154)
XLA Ops:
  0.6 2.5 %pack.1 = (bf16[800,384]{1,0:T(8,128)(2,1)}, bf16[416,384]{1,0:T(8,128)(2,1)}, bf16[416,384]{1,0:T(8,128)(2,1)}, bf16[800,384]{1,0:T(8,128)(2,1)}) custom-call(bf16[384,384]{1,0:T(8,128)(2,1)} %bitcast.11, bf16[384,384]{1,0:T(8,128)(2,1)} %bitcast.12, f32[3,1,384]{2,1,0:T(1,128)} %bitcast.14, f32[3,1,384]{2,1,0:T(1,128)} %bitcast.15), custom_call_target="tpu_custom_call" | custom-call | flops 1000 | bytes 1000 | tf_op jit(solution)/shard_map/pack/pallas_call | solution.py:356
  3.2 4.3 %collective-permute-start = (bf16[416,384]{1,0:T(8,128)(2,1)}, bf16[416,384]{1,0:T(8,128)(2,1)S(1)}, u32[]{:S(2)}, u32[]{:S(2)}) collective-permute-start(bf16[416,384]{1,0:T(8,128)(2,1)} %get-tuple-element.32), channel_id=1, source_target_pairs={{0,8},{4,12},{8,0},{12,4},{16,24},{20,28},{24,16},{28,20},{32,40},... | collective-permute-start | bytes 958472 | tf_op jit(solution)/shard_map/ppermute | solution.py:20
  7.4 1.9 %collective-permute-start.2 = (bf16[416,384]{1,0:T(8,128)(2,1)}, bf16[416,384]{1,0:T(8,128)(2,1)S(1)}, u32[]{:S(2)}, u32[]{:S(2)}) collective-permute-start(bf16[416,384]{1,0:T(8,128)(2,1)} %get-tuple-element.35), channel_id=1, source_target_pairs={{112,120},{136,128},{116,124},{140,132},{240,248},{264,256},{244,2... | collective-permute-start | bytes 958472 | tf_op jit(solution)/shard_map/ppermute | solution.py:20
  9.4 0.7 collective-permute-start.3
  10.1 1.0 %copy-done = bf16[1,1,384,384]{3,2,1,0:T(8,128)(2,1)S(1)} copy-done((bf16[1,1,384,384]{3,2,1,0:T(8,128)(2,1)S(1)}, bf16[1,1,384,384]{3,2,1,0:T(8,128)(2,1)}, u32[]{:S(2)}) %copy-start) | copy-done | bytes 294936
  11.1 1.0 %copy-done.1 = bf16[1,1,384,384]{3,2,1,0:T(8,128)(2,1)S(1)} copy-done((bf16[1,1,384,384]{3,2,1,0:T(8,128)(2,1)S(1)}, bf16[1,1,384,384]{3,2,1,0:T(8,128)(2,1)}, u32[]{:S(2)}) %copy-start.1) | copy-done | bytes 294936
  12.2 3.5 %collective-permute-done.msg = bf16[416,384]{1,0:T(8,128)(2,1)S(1)} collective-permute-done((bf16[416,384]{1,0:T(8,128)(2,1)}, bf16[416,384]{1,0:T(8,128)(2,1)S(1)}, u32[]{:S(2)}, u32[]{:S(2)}) %collective-permute-start) | collective-permute-done | bytes 319520 | tf_op jit(solution)/shard_map/ppermute | solution.py:20
  15.7 4.3 %collective-permute-start.5 = (bf16[768,384]{1,0:T(8,128)(2,1)S(1)}, bf16[768,384]{1,0:T(8,128)(2,1)S(1)}, u32[]{:S(2)}, u32[]{:S(2)}) collective-permute-start(bf16[768,384]{1,0:T(8,128)(2,1)S(1)} %stack.1.kv_a), channel_id=1, source_target_pairs={{0,8},{4,12},{8,0},{12,4},{16,24},{20,28},{24,16},{28,20},{32,40},... | collective-permute-start | bytes 1769480 | tf_op jit(solution)/shard_map/ppermute | solution.py:20
  20.0 1.9 %collective-permute-start.4 = (bf16[768,384]{1,0:T(8,128)(2,1)S(1)}, bf16[768,384]{1,0:T(8,128)(2,1)S(1)}, u32[]{:S(2)}, u32[]{:S(2)}) collective-permute-start(bf16[768,384]{1,0:T(8,128)(2,1)S(1)} %stack.1.kv_a), channel_id=1, source_target_pairs={{0,4},{4,0},{8,12},{12,8},{16,20},{20,16},{24,28},{28,24},{32,36},... | collective-permute-start | bytes 1769480 | tf_op jit(solution)/shard_map/ppermute | solution.py:20
  22.0 2.1 %collective-permute-start.1 = (bf16[800,384]{1,0:T(8,128)(2,1)S(1)}, bf16[800,384]{1,0:T(8,128)(2,1)S(1)}, u32[]{:S(2)}, u32[]{:S(2)}) collective-permute-start(bf16[800,384]{1,0:T(8,128)(2,1)S(1)} %join.1.pack.own), channel_id=1, source_target_pairs={{0,16},{16,0},{4,20},{20,4},{8,24},{24,8},{12,28},{28,12},{32,48},... | collective-permute-start | bytes 1843208 | tf_op jit(solution)/shard_map/ppermute | solution.py:20
  24.1 3.3 %own.1 = (f32[2,768,384]{2,1,0:T(8,128)S(1)}, f32[384,384]{1,0:T(8,128)S(1)}) custom-call(s32[32,4,3]{2,1,0:T(4,128)S(1)} %copy.11.extents, bf16[800,384]{1,0:T(8,128)(2,1)S(1)} %join.1.pack.own, bf16[768,384]{1,0:T(8,128)(2,1)S(1)} %stack.1.kv_a, bf16[768,384]{1,0:T(8,128)(2,1)S(1)} %collective-permute-done.4.kv_b), custom_call_target="tpu_custom_call" | custom-call | flops 1000 | bytes 1000 | tf_op jit(solution)/shard_map/own/own/pallas_call | solution.py:334
  27.6 0.7 collective-permute-start.7
  28.3 5.6 %collective-permute-done.5.kv_c = bf16[768,384]{1,0:T(8,128)(2,1)S(1)} collective-permute-done((bf16[768,384]{1,0:T(8,128)(2,1)S(1)}, bf16[768,384]{1,0:T(8,128)(2,1)S(1)}, u32[]{:S(2)}, u32[]{:S(2)}) %collective-permute-start.5) | collective-permute-done | bytes 589856 | tf_op jit(solution)/shard_map/ppermute | solution.py:20
  33.9 1.9 %collective-permute-start.6 = (bf16[768,384]{1,0:T(8,128)(2,1)S(1)}, bf16[768,384]{1,0:T(8,128)(2,1)S(1)}, u32[]{:S(2)}, u32[]{:S(2)}) collective-permute-start(bf16[768,384]{1,0:T(8,128)(2,1)S(1)} %collective-permute-done.5.kv_c), channel_id=1, source_target_pairs={{0,4},{4,0},{8,12},{12,8},{16,20},{20,16},{24,28},{28,24},{32,36},... | collective-permute-start | bytes 1769480 | tf_op jit(solution)/shard_map/ppermute | solution.py:20
  35.8 4.3 %collective-permute-done.1.even = bf16[800,384]{1,0:T(8,128)(2,1)S(1)} collective-permute-done((bf16[800,384]{1,0:T(8,128)(2,1)S(1)}, bf16[800,384]{1,0:T(8,128)(2,1)S(1)}, u32[]{:S(2)}, u32[]{:S(2)}) %collective-permute-start.1) | collective-permute-done | bytes 614432 | tf_op jit(solution)/shard_map/ppermute | solution.py:20
  40.1 8.1 %frame.1 = (f32[4,768,384]{2,1,0:T(8,128)S(1)}, f32[384,384]{1,0:T(8,128)S(1)}, bf16[384,384]{1,0:T(8,128)(2,1)S(1)}, bf16[384,384]{1,0:T(8,128)(2,1)S(1)}, bf16[4,768,384]{2,1,0:T(8,128)(2,1)S(1)}) custom-call(s32[32,4,3]{2,1,0:T(4,128)S(1)} %copy.11.extents, bf16[800,384]{1,0:T(8,128)(2,1)S(1)} %collective-permute-done.1.even, ...), custom_call_target="tpu_custom_call" | custom-call | flops 1000 | bytes 1000 | tf_op jit(solution)/shard_map/frame/frame/pallas_call | solution.py:334
  48.2 2.2 %collective-permute-start.8 = (bf16[384,384]{1,0:T(8,128)(2,1)S(1)}, bf16[384,384]{1,0:T(8,128)(2,1)S(1)}, u32[]{:S(2)}, u32[]{:S(2)}) collective-permute-start(bf16[384,384]{1,0:T(8,128)(2,1)S(1)} %get-tuple-element.49), channel_id=1, source_target_pairs={{0,16},{16,0},{4,20},{20,4},{8,24},{24,8},{12,28},{28,12},{32,48},... | collective-permute-start | bytes 884744 | tf_op jit(solution)/shard_map/ppermute | solution.py:20
  50.5 2.5 %odd.1 = (bf16[192,384]{1,0:T(8,128)(2,1)S(1)}, bf16[192,384]{1,0:T(8,128)(2,1)S(1)}, f32[768,384]{1,0:T(8,128)S(1)}, f32[768,384]{1,0:T(8,128)S(1)}, bf16[2,768,384]{2,1,0:T(8,128)(2,1)S(1)}) custom-call(s32[32,4,3]{2,1,0:T(4,128)S(1)} %copy.11.extents, bf16[800,384]{1,0:T(8,128)(2,1)S(1)} %collective-permute-done.7.pack, ...), custom_call_target="tpu_custom_call" | custom-call | flops 20000000000 | bytes 1000 | tf_op jit(solution)/shard_map/odd/odd/pallas_call | solution.py:334
  52.9 5.8 %collective-permute-done.8.even = bf16[384,384]{1,0:T(8,128)(2,1)S(1)} collective-permute-done((bf16[384,384]{1,0:T(8,128)(2,1)S(1)}, bf16[384,384]{1,0:T(8,128)(2,1)S(1)}, u32[]{:S(2)}, u32[]{:S(2)}) %collective-permute-start.8) | collective-permute-done | bytes 294944 | tf_op jit(solution)/shard_map/ppermute | solution.py:20
  58.8 1.9 %collective-permute-start.13 = (bf16[2,768,384]{2,1,0:T(8,128)(2,1)S(1)}, bf16[2,768,384]{2,1,0:T(8,128)(2,1)S(1)}, u32[]{:S(2)}, u32[]{:S(2)}) collective-permute-start(bf16[2,768,384]{2,1,0:T(8,128)(2,1)S(1)} %get-tuple-element.57), channel_id=1, source_target_pairs={{0,4},{4,0},{8,12},{12,8},{16,20},{20,16},{24,28},{28,24},{32,36},... | collective-permute-start | bytes 3538952 | tf_op jit(solution)/shard_map/ppermute | solution.py:20
  60.7 2.8 %collective-permute-done.13.sib = bf16[2,768,384]{2,1,0:T(8,128)(2,1)S(1)} collective-permute-done((bf16[2,768,384]{2,1,0:T(8,128)(2,1)S(1)}, bf16[2,768,384]{2,1,0:T(8,128)(2,1)S(1)}, u32[]{:S(2)}, u32[]{:S(2)}) %collective-permute-start.13) | collective-permute-done | bytes 1179680 | tf_op jit(solution)/shard_map/ppermute | solution.py:20
  63.5 0.2 lend.1
  63.6 5.0 %collective-permute-start.14 = (bf16[768,384]{1,0:T(8,128)(2,1)S(1)}, bf16[768,384]{1,0:T(8,128)(2,1)S(1)}, u32[]{:S(2)}, u32[]{:S(2)}) collective-permute-start(bf16[768,384]{1,0:T(8,128)(2,1)S(1)} %lend.1), channel_id=1, source_target_pairs={{0,8},{4,12},{8,0},{12,4},{16,24},{20,28},{24,16},{28,20},{32,40},... | collective-permute-start | bytes 1769480 | tf_op jit(solution)/shard_map/ppermute | solution.py:20
  68.6 0.7 collective-permute-start.12
  69.3 1.3 %collective-permute-start.10 = (bf16[192,384]{1,0:T(8,128)(2,1)S(1)}, bf16[192,384]{1,0:T(8,128)(2,1)S(1)}, u32[]{:S(2)}, u32[]{:S(2)}) collective-permute-start(bf16[192,384]{1,0:T(8,128)(2,1)S(1)} %get-tuple-element.53), channel_id=1, source_target_pairs={{16,32},{32,16},{20,36},{36,20},{24,40},{40,24},{28,44},{44,28},{4... | collective-permute-start | bytes 442376 | tf_op jit(solution)/shard_map/ppermute | solution.py:20
  70.6 1.3 %collective-permute-start.11 = (bf16[192,384]{1,0:T(8,128)(2,1)S(1)}, bf16[192,384]{1,0:T(8,128)(2,1)S(1)}, u32[]{:S(2)}, u32[]{:S(2)}) collective-permute-start(bf16[192,384]{1,0:T(8,128)(2,1)S(1)} %get-tuple-element.54), channel_id=1, source_target_pairs={{16,40},{32,24},{20,44},{36,28},{24,32},{40,16},{28,36},{44,20},{4... | collective-permute-start | bytes 442376 | tf_op jit(solution)/shard_map/ppermute | solution.py:20
  72.0 6.0 %collective-permute-start.9 = (bf16[192,384]{1,0:T(8,128)(2,1)S(1)}, bf16[192,384]{1,0:T(8,128)(2,1)S(1)}, u32[]{:S(2)}, u32[]{:S(2)}) collective-permute-start(bf16[192,384]{1,0:T(8,128)(2,1)S(1)} %get-tuple-element.52), channel_id=1, source_target_pairs={{0,8},{4,12},{8,0},{12,4},{16,24},{20,28},{24,16},{28,20},{32,40},... | collective-permute-start | bytes 442376 | tf_op jit(solution)/shard_map/ppermute | solution.py:20
  78.0 8.3 %collective-permute-done.10.straight = bf16[192,384]{1,0:T(8,128)(2,1)S(1)} collective-permute-done((bf16[192,384]{1,0:T(8,128)(2,1)S(1)}, bf16[192,384]{1,0:T(8,128)(2,1)S(1)}, u32[]{:S(2)}, u32[]{:S(2)}) %collective-permute-start.10) | collective-permute-done | bytes 147488 | tf_op jit(solution)/shard_map/ppermute | solution.py:20
  86.4 2.6 %collective-permute-done.11.diagonal = bf16[192,384]{1,0:T(8,128)(2,1)S(1)} collective-permute-done((bf16[192,384]{1,0:T(8,128)(2,1)S(1)}, bf16[192,384]{1,0:T(8,128)(2,1)S(1)}, u32[]{:S(2)}, u32[]{:S(2)}) %collective-permute-start.11) | collective-permute-done | bytes 147488 | tf_op jit(solution)/shard_map/ppermute | solution.py:20
  89.0 3.0 %collective-permute-done.9.got = bf16[192,384]{1,0:T(8,128)(2,1)S(1)} collective-permute-done((bf16[192,384]{1,0:T(8,128)(2,1)S(1)}, bf16[192,384]{1,0:T(8,128)(2,1)S(1)}, u32[]{:S(2)}, u32[]{:S(2)}) %collective-permute-start.9) | collective-permute-done | bytes 147488 | tf_op jit(solution)/shard_map/ppermute | solution.py:20
  92.0 0.8 place.1
  92.8 1.0 %close.1 = (bf16[384,384]{1,0:T(8,128)(2,1)}, bf16[384,384]{1,0:T(8,128)(2,1)}) custom-call(f32[768,384]{1,0:T(8,128)S(1)} %get-tuple-element.56.own, bf16[2,768,384]{2,1,0:T(8,128)(2,1)S(1)} %collective-permute-done.13.sib, bf16[768,384]{1,0:T(8,128)(2,1)S(1)} %collective-permute-done.14.given), custom_call_target="tpu_custom_call" | custom-call | flops 1000 | bytes 1000 | tf_op jit(solution)/shard_map/close/pallas_call | solution.py:334
  (18 shorter events, 0.4 us)
Async XLA Ops:
  0.6 11.4 %copy-start.3 = (s32[32,4,3]{0,1,2:T(4,128)S(1)}, s32[32,4,3]{0,1,2:T(4,128)}, u32[]{:S(2)}) copy-start(s32[32,4,3]{0,1,2:T(4,128)} %param.13) | copy-start | bytes 4612
  3.2 12.5 %collective-permute-start = (bf16[416,384]{1,0:T(8,128)(2,1)}, bf16[416,384]{1,0:T(8,128)(2,1)S(1)}, u32[]{:S(2)}, u32[]{:S(2)}) collective-permute-start(bf16[416,384]{1,0:T(8,128)(2,1)} %get-tuple-element.32), channel_id=1, source_target_pairs={{0,8},{4,12},{8,0},{12,4},{16,24},{20,28},{24,16},{28,20},{32,40},... | collective-permute-start | bytes 958472 | tf_op jit(solution)/shard_map/ppermute | solution.py:20
  7.4 20.0 %collective-permute-start.2 = (bf16[416,384]{1,0:T(8,128)(2,1)}, bf16[416,384]{1,0:T(8,128)(2,1)S(1)}, u32[]{:S(2)}, u32[]{:S(2)}) collective-permute-start(bf16[416,384]{1,0:T(8,128)(2,1)} %get-tuple-element.35), channel_id=1, source_target_pairs={{112,120},{136,128},{116,124},{140,132},{240,248},{264,256},{244,2... | collective-permute-start | bytes 958472 | tf_op jit(solution)/shard_map/ppermute | solution.py:20
  9.4 18.1 %collective-permute-start.3 = (bf16[800,384]{1,0:T(8,128)(2,1)}, bf16[800,384]{1,0:T(8,128)(2,1)S(1)}, u32[]{:S(2)}, u32[]{:S(2)}) collective-permute-start(bf16[800,384]{1,0:T(8,128)(2,1)} %get-tuple-element.36), channel_id=1, source_target_pairs={{120,128},{128,120},{124,132},{132,124},{248,256},{256,248},{252,2... | collective-permute-start | bytes 1843208 | tf_op jit(solution)/shard_map/ppermute | solution.py:20
  10.1 1.0 %copy-start = (bf16[1,1,384,384]{3,2,1,0:T(8,128)(2,1)S(1)}, bf16[1,1,384,384]{3,2,1,0:T(8,128)(2,1)}, u32[]{:S(2)}) copy-start(bf16[1,1,384,384]{3,2,1,0:T(8,128)(2,1)} %param.8) | copy-start | bytes 884740
  11.1 1.0 %copy-start.1 = (bf16[1,1,384,384]{3,2,1,0:T(8,128)(2,1)S(1)}, bf16[1,1,384,384]{3,2,1,0:T(8,128)(2,1)}, u32[]{:S(2)}) copy-start(bf16[1,1,384,384]{3,2,1,0:T(8,128)(2,1)} %param.9) | copy-start | bytes 884740
  12.0 9.9 %copy-start.2 = (bf16[800,384]{1,0:T(8,128)(2,1)S(1)}, bf16[800,384]{1,0:T(8,128)(2,1)}, u32[]{:S(2)}) copy-start(bf16[800,384]{1,0:T(8,128)(2,1)} %get-tuple-element.34.pack_in) | copy-start | bytes 1843204
  15.7 18.2 %collective-permute-start.5 = (bf16[768,384]{1,0:T(8,128)(2,1)S(1)}, bf16[768,384]{1,0:T(8,128)(2,1)S(1)}, u32[]{:S(2)}, u32[]{:S(2)}) collective-permute-start(bf16[768,384]{1,0:T(8,128)(2,1)S(1)} %stack.1.kv_a), channel_id=1, source_target_pairs={{0,8},{4,12},{8,0},{12,4},{16,24},{20,28},{24,16},{28,20},{32,40},... | collective-permute-start | bytes 1769480 | tf_op jit(solution)/shard_map/ppermute | solution.py:20
  20.0 4.1 %collective-permute-start.4 = (bf16[768,384]{1,0:T(8,128)(2,1)S(1)}, bf16[768,384]{1,0:T(8,128)(2,1)S(1)}, u32[]{:S(2)}, u32[]{:S(2)}) collective-permute-start(bf16[768,384]{1,0:T(8,128)(2,1)S(1)} %stack.1.kv_a), channel_id=1, source_target_pairs={{0,4},{4,0},{8,12},{12,8},{16,20},{20,16},{24,28},{28,24},{32,36},... | collective-permute-start | bytes 1769480 | tf_op jit(solution)/shard_map/ppermute | solution.py:20
  22.0 18.2 %collective-permute-start.1 = (bf16[800,384]{1,0:T(8,128)(2,1)S(1)}, bf16[800,384]{1,0:T(8,128)(2,1)S(1)}, u32[]{:S(2)}, u32[]{:S(2)}) collective-permute-start(bf16[800,384]{1,0:T(8,128)(2,1)S(1)} %join.1.pack.own), channel_id=1, source_target_pairs={{0,16},{16,0},{4,20},{20,4},{8,24},{24,8},{12,28},{28,12},{32,48},... | collective-permute-start | bytes 1843208 | tf_op jit(solution)/shard_map/ppermute | solution.py:20
  27.6 22.9 %collective-permute-start.7 = (bf16[800,384]{1,0:T(8,128)(2,1)S(1)}, bf16[800,384]{1,0:T(8,128)(2,1)S(1)}, u32[]{:S(2)}, u32[]{:S(2)}) collective-permute-start(bf16[800,384]{1,0:T(8,128)(2,1)S(1)} %odd_join.1), channel_id=1, source_target_pairs={{16,32},{32,16},{20,36},{36,20},{24,40},{40,24},{28,44},{44,28},{4... | collective-permute-start | bytes 1843208 | tf_op jit(solution)/shard_map/ppermute | solution.py:20
  33.9 6.2 %collective-permute-start.6 = (bf16[768,384]{1,0:T(8,128)(2,1)S(1)}, bf16[768,384]{1,0:T(8,128)(2,1)S(1)}, u32[]{:S(2)}, u32[]{:S(2)}) collective-permute-start(bf16[768,384]{1,0:T(8,128)(2,1)S(1)} %collective-permute-done.5.kv_c), channel_id=1, source_target_pairs={{0,4},{4,0},{8,12},{12,8},{16,20},{20,16},{24,28},{28,24},{32,36},... | collective-permute-start | bytes 1769480 | tf_op jit(solution)/shard_map/ppermute | solution.py:20
  48.2 10.5 %collective-permute-start.8 = (bf16[384,384]{1,0:T(8,128)(2,1)S(1)}, bf16[384,384]{1,0:T(8,128)(2,1)S(1)}, u32[]{:S(2)}, u32[]{:S(2)}) collective-permute-start(bf16[384,384]{1,0:T(8,128)(2,1)S(1)} %get-tuple-element.49), channel_id=1, source_target_pairs={{0,16},{16,0},{4,20},{20,4},{8,24},{24,8},{12,28},{28,12},{32,48},... | collective-permute-start | bytes 884744 | tf_op jit(solution)/shard_map/ppermute | solution.py:20
  58.8 4.7 %collective-permute-start.13 = (bf16[2,768,384]{2,1,0:T(8,128)(2,1)S(1)}, bf16[2,768,384]{2,1,0:T(8,128)(2,1)S(1)}, u32[]{:S(2)}, u32[]{:S(2)}) collective-permute-start(bf16[2,768,384]{2,1,0:T(8,128)(2,1)S(1)} %get-tuple-element.57), channel_id=1, source_target_pairs={{0,4},{4,0},{8,12},{12,8},{16,20},{20,16},{24,28},{28,24},{32,36},... | collective-permute-start | bytes 3538952 | tf_op jit(solution)/shard_map/ppermute | solution.py:20
  63.6 29.1 %collective-permute-start.14 = (bf16[768,384]{1,0:T(8,128)(2,1)S(1)}, bf16[768,384]{1,0:T(8,128)(2,1)S(1)}, u32[]{:S(2)}, u32[]{:S(2)}) collective-permute-start(bf16[768,384]{1,0:T(8,128)(2,1)S(1)} %lend.1), channel_id=1, source_target_pairs={{0,8},{4,12},{8,0},{12,4},{16,24},{20,28},{24,16},{28,20},{32,40},... | collective-permute-start | bytes 1769480 | tf_op jit(solution)/shard_map/ppermute | solution.py:20
  68.6 20.4 %collective-permute-start.12 = (bf16[384,384]{1,0:T(8,128)(2,1)S(1)}, bf16[384,384]{1,0:T(8,128)(2,1)S(1)}, u32[]{:S(2)}, u32[]{:S(2)}) collective-permute-start(bf16[384,384]{1,0:T(8,128)(2,1)S(1)} %get-tuple-element.55), channel_id=1, source_target_pairs={{120,128},{128,120},{124,132},{132,124},{248,256},{256,248},{252,2... | collective-permute-start | bytes 884744 | tf_op jit(solution)/shard_map/ppermute | solution.py:20
  69.3 17.1 %collective-permute-start.10 = (bf16[192,384]{1,0:T(8,128)(2,1)S(1)}, bf16[192,384]{1,0:T(8,128)(2,1)S(1)}, u32[]{:S(2)}, u32[]{:S(2)}) collective-permute-start(bf16[192,384]{1,0:T(8,128)(2,1)S(1)} %get-tuple-element.53), channel_id=1, source_target_pairs={{16,32},{32,16},{20,36},{36,20},{24,40},{40,24},{28,44},{44,28},{4... | collective-permute-start | bytes 442376 | tf_op jit(solution)/shard_map/ppermute | solution.py:20
  70.6 18.4 %collective-permute-start.11 = (bf16[192,384]{1,0:T(8,128)(2,1)S(1)}, bf16[192,384]{1,0:T(8,128)(2,1)S(1)}, u32[]{:S(2)}, u32[]{:S(2)}) collective-permute-start(bf16[192,384]{1,0:T(8,128)(2,1)S(1)} %get-tuple-element.54), channel_id=1, source_target_pairs={{16,40},{32,24},{20,44},{36,28},{24,32},{40,16},{28,36},{44,20},{4... | collective-permute-start | bytes 442376 | tf_op jit(solution)/shard_map/ppermute | solution.py:20
  72.0 20.0 %collective-permute-start.9 = (bf16[192,384]{1,0:T(8,128)(2,1)S(1)}, bf16[192,384]{1,0:T(8,128)(2,1)S(1)}, u32[]{:S(2)}, u32[]{:S(2)}) collective-permute-start(bf16[192,384]{1,0:T(8,128)(2,1)S(1)} %get-tuple-element.52), channel_id=1, source_target_pairs={{0,8},{4,12},{8,0},{12,4},{16,24},{20,28},{24,16},{28,20},{32,40},... | collective-permute-start | bytes 442376 | tf_op jit(solution)/shard_map/ppermute | solution.py:20
